TPU v7x, 32 devices: a whole 2x2x4 slice. The times are simulated.
32 devices in a mesh: rep: 2 (over y), exp: 8 (over z, core), ffn: 2 (over x).
Axes of the slice: x: 2, y: 2, z: 4, core: 2. Of those that a mesh axis runs over, the one named last changes fastest.
Arguments:
- out_grad: bfloat16 [128, 6144], P(('rep', 'exp', 'ffn')), may hold values from -6 to 6
- experts: int32 [128, 4], P(('rep', 'exp', 'ffn')), may hold values from 0 to 7, all different within a row; in each aligned block of 4 rows (0 to 3, 4 to 7, ...) at most 4 rows name the same one
- gates: float32 [128, 4], P(('rep', 'exp', 'ffn')), may hold values from 0.1 to 1
- expert_inputs: bfloat16 [2, 8, 64, 6144], P('rep', 'exp'), may hold values from -6 to 6
- w_in: bfloat16 [8, 6144, 256], P('exp', None, 'ffn'), may hold values from -0.078125 to 0.078125
- w_lin: bfloat16 [8, 6144, 256], P('exp', None, 'ffn'), may hold values from -0.078125 to 0.078125
- w_out: bfloat16 [8, 256, 6144], P('exp', 'ffn'), may hold values from -0.375 to 0.375
Outputs:
- grad_input: bfloat16 [128, 6144], P(('rep', 'exp', 'ffn'))
- grad_w1: float32 [8, 6144, 256], P('exp', 'rep', 'ffn')
- grad_v1: float32 [8, 6144, 256], P('exp', 'rep', 'ffn')
- grad_w2: float32 [8, 256, 6144], P('exp', 'ffn', 'rep')
Inputs may be any that keep to these rules, and one draw needn't show every extreme that they name: Each token names 4 different experts; the tokens of one device name one expert at most 4 times, and in every draw some device names some expert exactly 4 times.
All inputs are finite; a program needn't handle non-finite values.
Results may differ from a plain program's by a relative error of at most 0.0073.
Values may be sent and summed in bfloat16 or wider, within the bound.
No kernel may reach another device: no remote copies, remote signals or barrier semaphores. Data moves between devices by JAX's collectives and lax.ppermute only.
A program may use at most 64 MiB of HBM per device.

v0:
```python
import jax
import jax.numpy as jnp
from jax import lax
from jax.sharding import PartitionSpec as P


def slot_table(expert_ids, experts_count, capacity):
    flat = expert_ids.reshape(-1)
    length = flat.shape[0]
    matches = flat[:, None] == flat[None, :]
    earlier = lax.broadcasted_iota(jnp.int32, (length, length), 1) < lax.broadcasted_iota(
        jnp.int32, (length, length), 0
    )
    position = jnp.sum((matches & earlier).astype(jnp.int32), axis=1)
    target = flat * capacity + position
    slots = lax.broadcasted_iota(jnp.int32, (experts_count * capacity, length), 0)
    return (slots == target[None, :]).astype(jnp.bfloat16)


def contract_rows(left, right):
    return lax.dot_general(
        left, right, (((0,), (0,)), ((), ())), preferred_element_type=jnp.float32
    )


def contract_cols(left, right):
    return lax.dot_general(
        left, right, (((1,), (1,)), ((), ())), preferred_element_type=jnp.float32
    )


def body(out_grad, experts, gates, expert_inputs, w_in, w_lin, w_out):
    tokens_here, top_count = experts.shape
    width = out_grad.shape[1]
    groups = lax.axis_size("exp")
    column_groups = lax.axis_size("ffn")
    slot_rows = expert_inputs.shape[2]
    capacity = slot_rows // (column_groups * groups)
    table = slot_table(experts, groups, capacity)
    weighted = (
        (gates[:, :, None] * out_grad[:, None, :].astype(jnp.float32))
        .reshape(tokens_here * top_count, width)
        .astype(jnp.bfloat16)
    )
    outgoing = jnp.dot(table, weighted, preferred_element_type=jnp.float32).astype(jnp.bfloat16)
    arrived = lax.all_to_all(
        outgoing.reshape(groups, capacity * width), "exp", split_axis=0, concat_axis=0, tiled=True
    )
    routed = lax.all_gather(arrived.reshape(groups * capacity, width), "ffn", axis=0, tiled=True)
    inputs = expert_inputs[0, 0]
    gate_here = w_in[0]
    linear_here = w_lin[0]
    down_here = w_out[0]
    pre_gate = jnp.dot(inputs, gate_here, preferred_element_type=jnp.float32)
    pre_linear = jnp.dot(inputs, linear_here, preferred_element_type=jnp.float32)
    sigmoid_gate = jax.nn.sigmoid(pre_gate)
    activated = pre_gate * sigmoid_gate
    hidden = (activated * pre_linear).astype(jnp.bfloat16)
    d_hidden = contract_cols(routed, down_here)
    d_gate = (
        d_hidden * pre_linear * sigmoid_gate * (1.0 + pre_gate * (1.0 - sigmoid_gate))
    ).astype(jnp.bfloat16)
    d_linear = (d_hidden * activated).astype(jnp.bfloat16)
    hidden_count = hidden.shape[1]
    stacked_left = jnp.concatenate([inputs, routed], axis=0)
    empty_block = jnp.zeros((slot_rows, hidden_count), jnp.bfloat16)
    upper_block = jnp.concatenate([d_gate, d_linear, empty_block], axis=1)
    lower_block = jnp.concatenate([empty_block, empty_block, hidden], axis=1)
    stacked_right = jnp.concatenate([upper_block, lower_block], axis=0)
    weight_sum = lax.psum_scatter(
        contract_rows(stacked_left, stacked_right).astype(jnp.bfloat16),
        "rep",
        scatter_dimension=0,
        tiled=True,
    ).astype(jnp.float32)
    grad_w1 = weight_sum[:, :hidden_count][None]
    grad_v1 = weight_sum[:, hidden_count : 2 * hidden_count][None]
    grad_w2 = jnp.transpose(weight_sum[:, 2 * hidden_count :])[None]
    partial_value = (
        (contract_cols(d_gate, gate_here) + contract_cols(d_linear, linear_here))
        .astype(jnp.bfloat16)
        .reshape(column_groups, groups, capacity * width)
    )
    exchanged = lax.all_to_all(partial_value, "exp", split_axis=1, concat_axis=1, tiled=True)
    returned = lax.psum_scatter(
        exchanged.astype(jnp.float32).astype(jnp.bfloat16), "ffn", scatter_dimension=0, tiled=True
    )[0]
    combine_table = jnp.sum(
        table.astype(jnp.float32).reshape(groups * capacity, tokens_here, top_count), axis=2
    ).astype(jnp.bfloat16)
    grad_input = contract_rows(combine_table, returned.reshape(groups * capacity, width)).astype(
        jnp.bfloat16
    )
    return (grad_input, grad_w1, grad_v1, grad_w2)


def solution(mesh):
    in_specs = (
        P(("rep", "exp", "ffn"), None),
        P(("rep", "exp", "ffn"), None),
        P(("rep", "exp", "ffn"), None),
        P("rep", "exp", None, None),
        P("exp", None, "ffn"),
        P("exp", None, "ffn"),
        P("exp", "ffn", None),
    )
    out_specs = (
        P(("rep", "exp", "ffn"), None),
        P("exp", "rep", "ffn"),
        P("exp", "rep", "ffn"),
        P("exp", "ffn", "rep"),
    )
    return jax.shard_map(body, mesh=mesh, in_specs=in_specs, out_specs=out_specs, check_vma=False)
```

profile of v0, /device:TPU:0, one launch (start us, length us, event | category | flops | bytes accessed | tf_op | source)
XLA Modules:
  0.0 178.4 jit_solution(2918433049283209613)
XLA Ops:
  7.2 0.9 eq.28
  8.3 0.9 mul.53
  9.3 0.8 mul.51
  10.3 0.6 all_to_all.12
  11.0 0.5 broadcast.42
  11.5 3.0 %reduce.2 = bf16[8,24576]{1,0:T(8,128)(2,1)S(1)} reduce(bf16[8,1,24576]{2,1,0:T(2,128)(2,1)S(1)} %all_to_all.12, bf16[]{:T(256)} %broadcast.42), dimensions={1}, to_apply=%all_to_all.12.reduce_sub_computation | reduce | bytes 786434 | tf_op jit(solution)/shard_map/all_to_all | solution.py:46
  14.5 1.0 reshape.48
  15.6 6.3 %all-to-all-start = ((bf16[8,2,12288]{2,1,0:T(2,128)(2,1)}), bf16[8,2,12288]{2,1,0:T(2,128)(2,1)S(1)}, u32[]{:S(2)}, u32[]{:S(2)}) async-start(bf16[8,2,12288]{2,1,0:T(2,128)(2,1)} %reshape.48), calls=%async_computation | async-start | bytes 786432 | tf_op jit(solution)/shard_map/all_to_all | solution.py:46
  21.9 2.4 %fusion.6 = f32[64,128]{1,0:T(8,128)} fusion(bf16[1,6144,128]{2,1,0:T(8,128)(2,1)} %param.11, bf16[1,1,64,6144]{3,2,1,0:T(8,128)(2,1)S(1)} %copy-done.1), kind=kOutput, calls=%fused_computation.13 | convolution fusion | flops 100663296 | bytes 2392064 | tf_op jit(solution)/shard_map/dot_general | solution.py:54
  24.4 10.1 %all-to-all-done = bf16[8,2,12288]{2,1,0:T(2,128)(2,1)S(1)} async-done(((bf16[8,2,12288]{2,1,0:T(2,128)(2,1)}), bf16[8,2,12288]{2,1,0:T(2,128)(2,1)S(1)}, u32[]{:S(2)}, u32[]{:S(2)}) %all-to-all-start) | async-done | bytes 393248 | tf_op jit(solution)/shard_map/all_to_all | solution.py:46
  34.4 0.4 reshape.49
  34.8 2.4 %reduce.1 = bf16[8,24576]{1,0:T(8,128)(2,1)S(1)} reduce(bf16[8,1,24576]{2,1,0:T(2,128)(2,1)S(1)} %reshape.49, bf16[]{:T(256)} %constant.20), dimensions={1}, to_apply=%all_to_all.10.reduce_sub_computation | reduce | bytes 786434 | tf_op jit(solution)/shard_map/all_to_all | solution.py:46
  37.2 1.1 reshape.45
  38.3 11.7 %all_gather.3 = bf16[64,6144]{1,0:T(8,128)(2,1)S(1)} all-gather(bf16[32,6144]{1,0:T(8,128)(2,1)} %reshape.45), channel_id=1, replica_groups=mesh['rep'=2,'exp'=8,'ffn'=2] {'ffn'}, dimensions={0}, use_global_device_ids=true | all-gather | bytes 1179648 | tf_op jit(solution)/shard_map/all_gather | solution.py:49
  49.9 2.1 %fusion.11 = f32[64,128]{1,0:T(8,128)S(1)} fusion(bf16[64,6144]{1,0:T(8,128)(2,1)S(1)} %all_gather.3, bf16[1,128,6144]{2,1,0:T(8,128)(2,1)} %param.13), kind=kOutput, calls=%fused_computation.18 | convolution fusion | flops 100663296 | bytes 2392064 | tf_op jit(solution)/shard_map/dot_general | solution.py:27
  52.0 0.4 multiply_convert_fusion.2
  52.4 1.0 copy-done.2
  53.4 0.7 fusion.4
  54.1 1.6 fusion
  55.7 2.6 %reshape.46 = bf16[2,8,24576]{2,1,0:T(8,128)(2,1)} reshape(bf16[64,6144]{1,0:T(8,128)(2,1)} %fusion) | data formatting | bytes 1572864 | tf_op jit(solution)/shard_map/reshape | solution.py:82
  58.3 1.9 %copy.23 = bf16[2,8,24576]{2,0,1:T(2,128)(2,1)S(1)} copy(bf16[2,8,24576]{2,1,0:T(8,128)(2,1)} %reshape.46) | data formatting | bytes 1572864 | tf_op jit(solution)/shard_map/reshape | solution.py:82
  60.2 23.7 %all_to_all.15 = bf16[2,8,24576]{2,0,1:T(2,128)(2,1)S(1)} all-to-all(bf16[2,8,24576]{2,0,1:T(2,128)(2,1)S(1)} %copy.23), channel_id=1, replica_groups=mesh['rep'=2,'exp'=8,'ffn'=2] {'exp'}, dimensions={1} | all-to-all | bytes 1572864 | tf_op jit(solution)/shard_map/all_to_all | solution.py:84
  84.0 1.3 copy.24
  85.6 3.5 %convolution_convert_fusion = bf16[6144,384]{1,0:T(8,128)(2,1)} fusion(bf16[64,6144]{1,0:T(8,128)(2,1)S(1)} %all_gather.3, bf16[64,6144]{1,0:T(8,128)(2,1)S(1)} %bitcast.35, bf16[64,128]{1,0:T(8,128)(2,1)S(1)} %get-tuple-element.27, bf16[64,128]{1,0:T(8,128)(2,1)S(1)} %broadcast_in_dim.15, bf16[64,128]{1,0:T(8,128)(2,1)S(1)} %get-tuple-element.29, ...), kind=kOutput, calls=%fused_computation | convolution fusion | flops 609976320 | bytes 6356992 | tf_op jit(solution)/shard_map/dot_general | solution.py:21
  89.2 0.6 copy-done.4
  89.9 11.9 %reduce-scatter.3.cloned.1.call-done = bf16[1,8,24576]{2,1,0:T(8,128)(2,1)} async-done(((bf16[2,8,24576]{2,1,0:T(8,128)(2,1)}), bf16[1,8,24576]{2,1,0:T(8,128)(2,1)}) %reduce-scatter.3.cloned.1.call-update) | async-done | bytes 393232 | tf_op jit(solution)/shard_map/reduce_scatter | solution.py:85
  101.8 1.3 reshape_squeeze.3
  103.1 0.8 convolution_convert_fusion.2
  103.9 60.3 %reduce-scatter.5.cloned.1.call-done = bf16[3072,384]{1,0:T(8,128)(2,1)} async-done(((bf16[6144,384]{1,0:T(8,128)(2,1)}), bf16[3072,384]{1,0:T(8,128)(2,1)}) %reduce-scatter.5.cloned.1.call-update) | async-done | bytes 2359312 | tf_op jit(solution)/shard_map/reduce_scatter | solution.py:70
  164.2 2.0 %convert_element_type.54 = f32[3072,384]{1,0:T(8,128)S(1)} convert(bf16[3072,384]{1,0:T(8,128)(2,1)} %reduce-scatter.5.cloned.1.call-done) | non-fusion elementwise | flops 1179648 | bytes 7077888 | tf_op jit(solution)/shard_map/convert_element_type | solution.py:75
  166.2 2.3 %slice_bitcast_fusion = (f32[1,128,3072]{1,2,0:T(8,128)}, f32[1,3072,128]{2,1,0:T(8,128)}, f32[1,3072,128]{2,1,0:T(8,128)}) fusion(f32[3072,384]{1,0:T(8,128)S(1)} %convert_element_type.54), kind=kLoop, calls=%fused_computation.5 | loop fusion | bytes 9437184 | tf_op jit(solution)/shard_map/broadcast_in_dim | solution.py:78
  168.5 3.0 %copy.25 = f32[1,128,3072]{2,1,0:T(8,128)} copy(f32[1,128,3072]{1,2,0:T(8,128)} %get-tuple-element.24) | data formatting | bytes 3145728
  (20 shorter events, 1.1 us)
Async XLA Ops:
  7.2 44.8 %copy-start = (bf16[1,6144,128]{2,1,0:T(8,128)(2,1)S(1)}, bf16[1,6144,128]{2,1,0:T(8,128)(2,1)}, u32[]{:S(2)}) copy-start(bf16[1,6144,128]{2,1,0:T(8,128)(2,1)} %param.12) | copy-start | bytes 4718596
  11.0 10.9 %copy-start.1 = (bf16[1,1,64,6144]{3,2,1,0:T(8,128)(2,1)S(1)}, bf16[1,1,64,6144]{3,2,1,0:T(8,128)(2,1)}, u32[]{:S(2)}) copy-start(bf16[1,1,64,6144]{3,2,1,0:T(8,128)(2,1)} %param.10) | copy-start | bytes 2359300
  15.6 18.9 %all-to-all-start = ((bf16[8,2,12288]{2,1,0:T(2,128)(2,1)}), bf16[8,2,12288]{2,1,0:T(2,128)(2,1)S(1)}, u32[]{:S(2)}, u32[]{:S(2)}) async-start(bf16[8,2,12288]{2,1,0:T(2,128)(2,1)} %reshape.48), calls=%async_computation | async-start | bytes 786432 | tf_op jit(solution)/shard_map/all_to_all | solution.py:46
  21.9 79.9 %reduce-scatter.3.cloned.1.call-start = ((), (), s32[]{:S(2)}) async-start(), calls=%async_computation.4 | async-start | bytes 1179648 | tf_op jit(solution)/shard_map/reduce_scatter | solution.py:85
  38.3 13.8 %copy-start.3 = (f32[64,128]{1,0:T(8,128)S(1)}, f32[64,128]{1,0:T(8,128)}, u32[]{:S(2)}) copy-start(f32[64,128]{1,0:T(8,128)} %fusion.6) | copy-start | bytes 98308
  52.0 1.4 copy-start.2
  85.3 78.9 %reduce-scatter.5.cloned.1.call-start = ((), (), s32[]{:S(2)}) async-start(), calls=%async_computation.5 | async-start | bytes 7077888 | tf_op jit(solution)/shard_map/reduce_scatter | solution.py:70
  89.1 0.7 copy-start.4
Sparse Core Ops, SparseCore 0:
  85.4 16.3 reduce-scatter.2
  104.2 59.9 reduce-scatter.4
where the time goes:
time: 179 us; the launch traced here: 178 us
  waiting for transfers between devices  82.3 us (46%)
  blocking collectives  35.4 us (20%)
  local copies, waits for them, and re-layouts  20.4 us (11%)
  between operations  14.2 us (8%)
  matrix products  11.8 us (7%)
  other arithmetic  7.62 us (4%)
  starting transfers between devices  6.58 us (4%)
    reduce_scatter x1, waiting for transfers between devices, body(): lax.psum_scatter(contract_rows(stacked_left, stacked_right).astype(jnp.bf...  60.3 us
    all_to_all x1, blocking collectives, body(): lax.all_to_all(partial_value, 'exp', split_axis=1, concat_axis=1, tiled=T...  23.7 us
    reduce_scatter x1, waiting for transfers between devices, body(): lax.psum_scatter(exchanged.astype(jnp.float32).astype(jnp.bfloat16), 'ffn...  11.9 us
    all_gather x1, blocking collectives, body(): lax.all_gather(arrived.reshape(groups * capacity, width), 'ffn', axis=0,...  11.7 us
    all_to_all x1, waiting for transfers between devices, body(): lax.all_to_all(outgoing.reshape(groups, capacity * width), 'exp', split_a...  10.1 us
    all_to_all x1, starting transfers between devices, body(): lax.all_to_all(outgoing.reshape(groups, capacity * width), 'exp', split_a...  6.32 us
    unnamed x13, local copies, waits for them, and re-layouts  6.01 us
    all_to_all x2, other arithmetic, body(): lax.all_to_all(outgoing.reshape(groups, capacity * width), 'exp', split_a...  5.37 us
  transfers between devices with their start and end apart: 3, of which 3 were waited for; matrix products, arithmetic and copies ran while one was open for 5% of the time, Pallas kernels for 0%

commit v1 on v0

v1 whole, which is shorter than its diff:
```python
import functools

import jax
import jax.numpy as jnp
from jax import lax
from jax.experimental import pallas as pl
from jax.experimental.pallas import tpu as pltpu
from jax.sharding import PartitionSpec as P

LANES = 128
SECTION = 32
F32 = jnp.float32
BF16 = jnp.bfloat16


def nt(left, right):
    return lax.dot_general(left, right, (((1,), (1,)), ((), ())), preferred_element_type=F32)


def tn(left, right):
    return lax.dot_general(left, right, (((0,), (0,)), ((), ())), preferred_element_type=F32)


def local_call(kernel, out_shape, args, flops=0, scratch=(), nbytes=0):
    return pl.pallas_call(
        kernel,
        out_shape=out_shape,
        in_specs=[pl.BlockSpec(memory_space=pltpu.VMEM)] * len(args),
        out_specs=jax.tree.map(lambda _: pl.BlockSpec(memory_space=pltpu.VMEM), out_shape),
        scratch_shapes=list(scratch),
        compiler_params=pltpu.CompilerParams(vmem_limit_bytes=30 * 1024 * 1024),
        cost_estimate=pl.CostEstimate(flops=flops, bytes_accessed=nbytes, transcendentals=0),
    )(*args)


def pack_kernel(capacity, groups, grad_ref, experts_ref, gates_ref, out_ref):
    tokens, width = grad_ref.shape
    experts, gates = experts_ref[...], gates_ref[...]
    lane = lax.broadcasted_iota(jnp.int32, (tokens, LANES), 1)
    expert, section = lane % SECTION, lane // SECTION
    gate = jnp.zeros((tokens, LANES), F32)
    named = jnp.zeros((tokens, LANES), F32)
    for k in range(experts.shape[1]):
        hit = experts[:, k : k + 1] == expert
        gate = gate + jnp.where(hit, gates[:, k : k + 1], 0.0)
        named = named + jnp.where(hit, 1.0, 0.0)
    earlier = jnp.zeros((1, LANES), F32)
    positions = []
    for t in range(tokens):
        positions.append(earlier)
        earlier = earlier + named[t : t + 1]
    block = lax.axis_index("ffn") * groups + lax.axis_index("exp")
    slot = jnp.concatenate(positions, axis=0) + (block * capacity + 1).astype(F32)
    high = gate.astype(BF16).astype(F32)
    middle = (gate - high).astype(BF16).astype(F32)
    low = gate - high - middle
    record = jnp.where(section == 0, high, jnp.where(section == 1, middle, low))
    record = jnp.where(section == 3, jnp.where(named > 0, slot, 0.0), record)
    out_ref[:, :width] = grad_ref[...]
    out_ref[:, width:] = record.astype(BF16)


def pre_kernel(replicas, x_ref, w_in_ref, w_lin_ref, gate_ref, linear_ref, *send_refs):
    share = x_ref.shape[1] // replicas
    me = lax.axis_index("rep")
    for j, send_ref in enumerate(send_refs):
        start = pl.multiple_of((me ^ (j + 1)) * share, LANES)
        send_ref[...] = x_ref[:, pl.ds(start, share)]
    gate_ref[...] = jnp.dot(x_ref[...], w_in_ref[...], preferred_element_type=F32)
    linear_ref[...] = jnp.dot(x_ref[...], w_lin_ref[...], preferred_element_type=F32)


def factor_kernel(replicas, count, *refs):
    pieces, refs = refs[:count], refs[count:]
    gate_ref, linear_ref, w_out_ref = refs[:3]
    d_gate_ref, d_linear_ref, factor_ref, own_ref = refs[3:7]
    send_refs = refs[7 : 7 + replicas - 1]
    t_ref = refs[-1]
    rows = pieces[0].shape[0]
    tokens = rows * count
    width = w_out_ref.shape[1]
    slots = gate_ref.shape[0]
    together = 16 // rows if 16 % rows == 0 and tokens % 16 == 0 else count
    for first in range(0, count, together):
        group = pieces[first : first + together]
        for begin in range(0, width + LANES, 896):
            cols = slice(begin, min(begin + 896, width + LANES))
            block = jnp.concatenate([p[:, cols].astype(F32) for p in group], axis=0)
            t_ref[first * rows : (first + together) * rows, cols] = block.astype(BF16)
    record = t_ref[:, width:].astype(F32)
    lane = lax.broadcasted_iota(jnp.int32, (tokens, LANES), 1)
    expert = lax.axis_index("exp")
    mine = (lane % SECTION == expert) & (lane < 3 * SECTION)
    gates = jnp.sum(jnp.where(mine, record, 0.0), axis=1, keepdims=True)
    slot = jnp.sum(jnp.where(lane == 3 * SECTION + expert, record, 0.0), axis=1, keepdims=True)
    place = lax.broadcasted_iota(jnp.int32, (tokens, slots), 1) + 1
    table = jnp.where(place == slot.astype(jnp.int32), 1.0, 0.0)

    def to_tokens(values):
        return jnp.dot(table, values, preferred_element_type=F32, precision=lax.Precision.HIGHEST)

    pre_gate = to_tokens(gate_ref[...])
    pre_linear = to_tokens(linear_ref[...])
    sigmoid = jax.nn.sigmoid(pre_gate)
    activated = pre_gate * sigmoid
    d_hidden = nt(t_ref[:, :width], w_out_ref[...]) * gates
    d_gate = (d_hidden * pre_linear * sigmoid * (1.0 + pre_gate * (1.0 - sigmoid))).astype(BF16)
    d_linear = (d_hidden * activated).astype(BF16)
    d_gate_ref[...] = d_gate
    d_linear_ref[...] = d_linear
    table = table.astype(BF16)
    factor_ref[:slots] = tn(table, d_gate).astype(BF16)
    factor_ref[slots : 2 * slots] = tn(table, d_linear).astype(BF16)
    factor_ref[2 * slots :] = (activated * pre_linear * gates).astype(BF16)
    share = width // replicas
    me = lax.axis_index("rep")
    own_ref[...] = t_ref[:, pl.ds(pl.multiple_of(me * share, LANES), share)]
    for j, send_ref in enumerate(send_refs):
        send_ref[...] = t_ref[:, pl.ds(pl.multiple_of((me ^ (j + 1)) * share, LANES), share)]


def rows_kernel(d_gate_ref, d_linear_ref, w_in_ref, w_lin_ref, keep_ref, send_ref):
    half, width = keep_ref.shape
    step = 1536 if width % 1536 == 0 else width
    for begin in range(0, width, step):
        cols = slice(begin, begin + step)
        rows = nt(d_gate_ref[...], w_in_ref[cols, :]) + nt(d_linear_ref[...], w_lin_ref[cols, :])
        keep_ref[:, cols] = rows[:half]
        send_ref[:, cols] = rows[half:].astype(BF16)


def sum_kernel(arrived, kept_ref, *refs):
    arrived_refs, keep_ref, send_refs = refs[:arrived], refs[arrived], refs[arrived + 1 :]
    rows, width = keep_ref.shape
    for begin in range(0, width, 1024):
        cols = slice(begin, min(begin + 1024, width))
        total = kept_ref[:, cols]
        for ref in arrived_refs:
            total = total + ref[:, cols].astype(F32)
        keep_ref[:, cols] = total[:rows].astype(keep_ref.dtype)
        for i, ref in enumerate(send_refs):
            ref[:, cols] = total[(i + 1) * rows : (i + 2) * rows].astype(BF16)


def weights_kernel(replicas, slots, *refs):
    x_ref, own_ref, factor_ref = refs[:3]
    others = replicas - 1
    x_others, t_others, f_others = (refs[3 + i * others : 3 + (i + 1) * others] for i in range(3))
    w1_ref, v1_ref, w2_ref = refs[3 + 3 * others :]
    share = own_ref.shape[1]
    me = lax.axis_index("rep")
    factors = (factor_ref, *f_others)
    hidden = jnp.concatenate([f[2 * slots :] for f in factors], axis=0)
    d_gate = jnp.concatenate([f[:slots] for f in factors], axis=0)
    d_linear = jnp.concatenate([f[slots : 2 * slots] for f in factors], axis=0)
    step = 768 if share % 768 == 0 else share
    for begin in range(0, share, step):
        cols = slice(begin, begin + step)
        mine = x_ref[:, pl.ds(pl.multiple_of(me * share + begin, LANES), step)]
        inputs = jnp.concatenate([mine, *(x[:, cols] for x in x_others)], axis=0)
        tokens = jnp.concatenate([own_ref[:, cols], *(t[:, cols] for t in t_others)], axis=0)
        w1_ref[cols, :] = tn(inputs, d_gate)
        v1_ref[cols, :] = tn(inputs, d_linear)
        w2_ref[:, cols] = tn(hidden, tokens)


def swap(values, axis, distance):
    size = lax.axis_size(axis)
    return lax.ppermute(values, axis, [(i, i ^ distance) for i in range(size)])


def body(out_grad, experts, gates, expert_inputs, w_in, w_lin, w_out):
    tokens_here, width = out_grad.shape
    groups, column_groups, replicas = (lax.axis_size(a) for a in ("exp", "ffn", "rep"))
    slots = expert_inputs.shape[2]
    capacity = slots // (column_groups * groups)
    hidden_count = w_in.shape[2]
    share = width // replicas
    tokens = groups * column_groups * tokens_here
    shape = jax.ShapeDtypeStruct
    inputs, gate_w, linear_w, down_w = expert_inputs[0, 0], w_in[0], w_lin[0], w_out[0]
    weight_flops = 2 * tokens * width * hidden_count

    own = local_call(
        functools.partial(pack_kernel, capacity, groups),
        shape((tokens_here, width + LANES), BF16),
        (out_grad, experts, gates),
    )
    column = [own] + [swap(own, "exp", k) for k in range(2, groups, 2)]
    plane = list(column)
    for j in range(1, column_groups):
        plane += [swap(piece, "ffn", j) for piece in column]
    pieces = plane + [swap(piece, "exp", 1) for piece in plane]

    pre_gate, pre_linear, *x_sends = local_call(
        functools.partial(pre_kernel, replicas),
        [shape((slots, hidden_count), F32)] * 2 + [shape((slots, share), BF16)] * (replicas - 1),
        (inputs, gate_w, linear_w),
        flops=2 * weight_flops,
    )
    x_others = [swap(x, "rep", j + 1) for j, x in enumerate(x_sends)]

    d_gate, d_linear, factors, t_own, *t_sends = local_call(
        functools.partial(factor_kernel, replicas, len(pieces)),
        [shape((tokens, hidden_count), BF16)] * 2
        + [shape((2 * slots + tokens, hidden_count), BF16)]
        + [shape((tokens, share), BF16)] * replicas,
        (*pieces, pre_gate, pre_linear, down_w),
        flops=weight_flops,
        scratch=[pltpu.VMEM((tokens, width + LANES), BF16)],
    )
    keep, send = local_call(
        rows_kernel,
        [shape((tokens // 2, width), F32), shape((tokens // 2, width), BF16)],
        (d_gate, d_linear, gate_w, linear_w),
        flops=2 * weight_flops,
    )
    back = swap(send, "exp", 1)
    f_others = [swap(factors, "rep", j) for j in range(1, replicas)]
    t_others = [swap(t, "rep", j + 1) for j, t in enumerate(t_sends)]

    rows = tokens // 2 // column_groups
    keep, *sends = local_call(
        functools.partial(sum_kernel, 1),
        [shape((rows, width), F32)] + [shape((rows, width), BF16)] * (column_groups - 1),
        (keep, back),
    )
    backs = [swap(s, "ffn", j + 1) for j, s in enumerate(sends)]
    keep, *sends = local_call(
        functools.partial(sum_kernel, len(backs)),
        [shape((tokens_here, width), F32)] + [shape((tokens_here, width), BF16)] * (groups // 2 - 1),
        (keep, *backs),
    )
    backs = [swap(s, "exp", 2 * (j + 1)) for j, s in enumerate(sends)]
    grad_w1, grad_v1, grad_w2 = local_call(
        functools.partial(weights_kernel, replicas, slots),
        [shape((share, hidden_count), F32)] * 2 + [shape((hidden_count, share), F32)],
        (inputs, t_own, factors, *x_others, *t_others, *f_others),
        flops=3 * weight_flops,
    )
    (grad_input,) = local_call(
        functools.partial(sum_kernel, len(backs)),
        [shape((tokens_here, width), BF16)],
        (keep, *backs),
    )
    return grad_input, grad_w1[None], grad_v1[None], grad_w2[None]


def solution(mesh):
    in_specs = (
        P(("rep", "exp", "ffn"), None),
        P(("rep", "exp", "ffn"), None),
        P(("rep", "exp", "ffn"), None),
        P("rep", "exp", None, None),
        P("exp", None, "ffn"),
        P("exp", None, "ffn"),
        P("exp", "ffn", None),
    )
    out_specs = (
        P(("rep", "exp", "ffn"), None),
        P("exp", "rep", "ffn"),
        P("exp", "rep", "ffn"),
        P("exp", "ffn", "rep"),
    )
    return jax.shard_map(body, mesh=mesh, in_specs=in_specs, out_specs=out_specs, check_vma=False)
```

time: 179 us -> 55.1 us (0.31)
  waiting for transfers between devices: 82.3 us -> 17.8 us
  blocking collectives: 35.4 us -> 0 us
  starting transfers between devices: 6.58 us -> 22.7 us
  local copies, waits for them, and re-layouts: 20.4 us -> 6.97 us
  between operations: 14.2 us -> 0.77 us
  matrix products: 11.8 us -> 0 us
  other arithmetic: 7.62 us -> 0 us
  Pallas kernels: 0 us -> 6.55 us
    reduce_scatter x2 -> x0, waiting for transfers between devices: 72.2 us -> none  [the longest x1 60.3 us: body(): lax.psum_scatter(contract_rows(stacked_left, stacked_right).astype(jnp.bf...]
    all_to_all x1 -> x0, blocking collectives: 23.7 us -> none  [body(): lax.all_to_all(partial_value, 'exp', split_axis=1, concat_axis=1, tiled=T...]
    ppermute x0 -> x23, starting transfers between devices: none -> 22.7 us  [swap(): return lax.ppermute(values, axis, [(i, i ^ distance) for i in range(size)])]
    ppermute x0 -> x23, waiting for transfers between devices: none -> 17.8 us  [swap(): return lax.ppermute(values, axis, [(i, i ^ distance) for i in range(size)])]
    dot_general x8 -> x0, matrix products: 11.8 us -> none  [the longest x2 4.34 us: contract_rows(): lax.dot_general(left, right, (((0,), (0,)), ((), ())), preferred_element_...]
    all_gather x1 -> x0, blocking collectives: 11.7 us -> none  [body(): lax.all_gather(arrived.reshape(groups * capacity, width), 'ffn', axis=0,...]
    all_to_all x1 -> x0, waiting for transfers between devices: 10.1 us -> none  [body(): lax.all_to_all(outgoing.reshape(groups, capacity * width), 'exp', split_a...]
    pallas_call x0 -> x8, Pallas kernels: none -> 6.55 us  [local_call(): pl.pallas_call(kernel, out_shape=out_shape, in_specs=[pl.BlockSpec(memory...]
  transfers between devices with their start and end apart: 3 -> 23, of which waited for: 3 -> 6; matrix products, arithmetic and copies ran while one was open for 5% -> 0% of each run, Pallas kernels for 0% -> 7%
where the time goes in v1:
time: 55.1 us; the launch traced here: 54.8 us
  starting transfers between devices  22.7 us (41%)
  waiting for transfers between devices  17.8 us (32%)
  local copies, waits for them, and re-layouts  6.97 us (13%)
  Pallas kernels  6.55 us (12%)
  between operations  0.77 us (1%)
    ppermute x23, starting transfers between devices, swap(): return lax.ppermute(values, axis, [(i, i ^ distance) for i in range(size)])  22.7 us
    ppermute x23, waiting for transfers between devices, swap(): return lax.ppermute(values, axis, [(i, i ^ distance) for i in range(size)])  17.8 us
    unnamed x20, local copies, waits for them, and re-layouts  6.97 us
    pallas_call x8, Pallas kernels, local_call(): pl.pallas_call(kernel, out_shape=out_shape, in_specs=[pl.BlockSpec(memory...  6.55 us
  transfers between devices with their start and end apart: 23, of which 6 were waited for; matrix products, arithmetic and copies ran while one was open for 0% of the time, Pallas kernels for 7%

profile of v1, /device:TPU:0, one launch (start us, length us, event | category | flops | bytes accessed | tf_op | source)
XLA Modules:
  0.0 54.8 jit_solution(15148583898040848589)
XLA Ops:
  0.6 0.8 %copy-done.7 = bf16[4,6144]{1,0:T(4,128)(2,1)S(1)} copy-done((bf16[4,6144]{1,0:T(4,128)(2,1)S(1)}, bf16[4,6144]{1,0:T(4,128)(2,1)}, u32[]{:S(2)}) %copy-start.7) | copy-done | bytes 49176
  1.4 0.7 %copy-done.8 = s32[4,4]{1,0:T(4,128)S(1)} copy-done((s32[4,4]{1,0:T(4,128)S(1)}, s32[4,4]{1,0:T(4,128)}, u32[]{:S(2)}) %copy-start.8) | copy-done | bytes 88
  2.1 0.7 %copy-done.9 = f32[4,4]{1,0:T(4,128)S(1)} copy-done((f32[4,4]{1,0:T(4,128)S(1)}, f32[4,4]{1,0:T(4,128)}, u32[]{:S(2)}) %copy-start.9) | copy-done | bytes 88
  2.9 3.0 %collective-permute-start.3 = (bf16[4,6272]{1,0:T(4,128)(2,1)S(1)}, bf16[4,6272]{1,0:T(4,128)(2,1)S(1)}, u32[]{:S(2)}, u32[]{:S(2)}) collective-permute-start(bf16[4,6272]{1,0:T(4,128)(2,1)S(1)} %shard_map.102.refs_0_), channel_id=1, source_target_pairs={{0,1},{1,0},{2,3},{3,2},{4,5},{5,4},{6,7},{7,6},{8,9},{9,8},{10,11... | collective-permute-start | bytes 150536 | tf_op jit(solution)/shard_map/ppermute | solution.py:169
  5.9 3.6 %collective-permute-start.2 = (bf16[4,6272]{1,0:T(4,128)(2,1)S(1)}, bf16[4,6272]{1,0:T(4,128)(2,1)S(1)}, u32[]{:S(2)}, u32[]{:S(2)}) collective-permute-start(bf16[4,6272]{1,0:T(4,128)(2,1)S(1)} %shard_map.102.refs_0_), channel_id=1, source_target_pairs={{0,12},{2,14},{4,8},{6,10},{8,4},{10,6},{12,0},{14,2},{1,13},{3,15... | collective-permute-start | bytes 150536 | tf_op jit(solution)/shard_map/ppermute | solution.py:169
  9.5 0.8 %collective-permute-start = (bf16[4,6272]{1,0:T(4,128)(2,1)S(1)}, bf16[4,6272]{1,0:T(4,128)(2,1)S(1)}, u32[]{:S(2)}, u32[]{:S(2)}) collective-permute-start(bf16[4,6272]{1,0:T(4,128)(2,1)S(1)} %shard_map.102.refs_0_), channel_id=1, source_target_pairs={{0,4},{2,6},{4,0},{6,2},{8,12},{10,14},{12,8},{14,10},{1,5},{3,7},... | collective-permute-start | bytes 150536 | tf_op jit(solution)/shard_map/ppermute | solution.py:169
  10.3 1.5 %collective-permute-done.2.refs_3_ = bf16[4,6272]{1,0:T(4,128)(2,1)S(1)} collective-permute-done((bf16[4,6272]{1,0:T(4,128)(2,1)S(1)}, bf16[4,6272]{1,0:T(4,128)(2,1)S(1)}, u32[]{:S(2)}, u32[]{:S(2)}) %collective-permute-start.2) | collective-permute-done | bytes 50208 | tf_op jit(solution)/shard_map/ppermute | solution.py:169
  11.8 0.4 collective-permute-start.6
  12.2 2.5 %collective-permute-done.1.refs_2_ = bf16[4,6272]{1,0:T(4,128)(2,1)S(1)} collective-permute-done((bf16[4,6272]{1,0:T(4,128)(2,1)S(1)}, bf16[4,6272]{1,0:T(4,128)(2,1)S(1)}, u32[]{:S(2)}, u32[]{:S(2)}) %collective-permute-start.1) | collective-permute-done | bytes 50208 | tf_op jit(solution)/shard_map/ppermute | solution.py:169
  14.7 0.5 collective-permute-start.5
  15.3 1.5 %collective-permute-start.4 = (bf16[4,6272]{1,0:T(4,128)(2,1)S(1)}, bf16[4,6272]{1,0:T(4,128)(2,1)S(1)}, u32[]{:S(2)}, u32[]{:S(2)}) collective-permute-start(bf16[4,6272]{1,0:T(4,128)(2,1)S(1)} %collective-permute-done.refs_1_), channel_id=1, source_target_pairs={{0,1},{1,0},{2,3},{3,2},{4,5},{5,4},{6,7},{7,6},{8,9},{9,8},{10,11... | collective-permute-start | bytes 150536 | tf_op jit(solution)/shard_map/ppermute | solution.py:169
  16.8 0.5 collective-permute-start.8
  17.4 1.5 %collective-permute-done.5.refs_6_ = bf16[4,6272]{1,0:T(4,128)(2,1)S(1)} collective-permute-done((bf16[4,6272]{1,0:T(4,128)(2,1)S(1)}, bf16[4,6272]{1,0:T(4,128)(2,1)S(1)}, u32[]{:S(2)}, u32[]{:S(2)}) %collective-permute-start.5) | collective-permute-done | bytes 50208 | tf_op jit(solution)/shard_map/ppermute | solution.py:169
  18.8 0.5 collective-permute-done.4.refs_5_
  19.4 1.4 %copy-done = bf16[1,6144,128]{2,1,0:T(8,128)(2,1)S(1)} copy-done((bf16[1,6144,128]{2,1,0:T(8,128)(2,1)S(1)}, bf16[1,6144,128]{2,1,0:T(8,128)(2,1)}, u32[]{:S(2)}) %copy-start) | copy-done | bytes 1572888
  20.8 1.4 %copy-done.2 = bf16[1,6144,128]{2,1,0:T(8,128)(2,1)S(1)} copy-done((bf16[1,6144,128]{2,1,0:T(8,128)(2,1)S(1)}, bf16[1,6144,128]{2,1,0:T(8,128)(2,1)}, u32[]{:S(2)}) %copy-start.2) | copy-done | bytes 1572888
  22.2 1.1 %copy-done.4 = bf16[1,1,64,6144]{3,2,1,0:T(8,128)(2,1)S(1)} copy-done((bf16[1,1,64,6144]{3,2,1,0:T(8,128)(2,1)S(1)}, bf16[1,1,64,6144]{3,2,1,0:T(8,128)(2,1)}, u32[]{:S(2)}) %copy-start.4) | copy-done | bytes 786456
  23.3 0.6 %shard_map.103 = (f32[64,128]{1,0:T(8,128)S(1)}, f32[64,128]{1,0:T(8,128)S(1)}, bf16[64,3072]{1,0:T(8,128)(2,1)S(1)}) custom-call(bf16[64,6144]{1,0:T(8,128)(2,1)S(1)} %bitcast.11, bf16[6144,128]{1,0:T(8,128)(2,1)S(1)} %bitcast.7, bf16[6144,128]{1,0:T(8,128)(2,1)S(1)} %bitcast.9), custom_call_target="tpu_custom_call" | custom-call | flops 201326592 | tf_op jit(solution)/shard_map/pallas_call | solution.py:25
  24.0 0.7 %copy-done.6 = bf16[1,128,6144]{2,1,0:T(8,128)(2,1)S(1)} copy-done((bf16[1,128,6144]{2,1,0:T(8,128)(2,1)S(1)}, bf16[1,128,6144]{2,1,0:T(8,128)(2,1)}, u32[]{:S(2)}) %copy-start.6) | copy-done | bytes 1572888
  24.7 0.9 %shard_map.104 = (bf16[64,128]{1,0:T(8,128)(2,1)S(1)}, bf16[64,128]{1,0:T(8,128)(2,1)S(1)}, bf16[192,128]{1,0:T(8,128)(2,1)S(1)}, bf16[64,3072]{1,0:T(8,128)(2,1)S(1)}, bf16[64,3072]{1,0:T(8,128)(2,1)S(1)}) custom-call(bf16[4,6272]{1,0:T(4,128)(2,1)S(1)} %shard_map.102.refs_0_, bf16[4,6272]{1,0:T(4,128)(2,1)S(1)} %collective-permute-done.refs_1_, ...), custom_call_target="tpu_custom_call" | custom-call | flops 100663296 | tf_op jit(solution)/shard_map/pallas_call | solution.py:25
  25.9 1.2 %shard_map.105 = (f32[32,6144]{1,0:T(8,128)S(1)}, bf16[32,6144]{1,0:T(8,128)(2,1)S(1)}) custom-call(bf16[64,128]{1,0:T(8,128)(2,1)S(1)} %get-tuple-element.25.d_gate_ref, bf16[64,128]{1,0:T(8,128)(2,1)S(1)} %get-tuple-element.26.d_linear_ref, bf16[6144,128]{1,0:T(8,128)(2,1)S(1)} %bitcast.8, bf16[6144,128]{1,0:T(8,128)(2,1)S(1)} %bitcast.10), custom_call_target="tpu_custom_call" | custom-call | flops 201326592 | tf_op jit(solution)/shard_map/pallas_call | solution.py:25
  27.1 0.6 %collective-permute-start.15 = (bf16[32,6144]{1,0:T(8,128)(2,1)S(1)}, bf16[32,6144]{1,0:T(8,128)(2,1)S(1)}, u32[]{:S(2)}, u32[]{:S(2)}) collective-permute-start(bf16[32,6144]{1,0:T(8,128)(2,1)S(1)} %get-tuple-element.28), channel_id=1, source_target_pairs={{0,2},{2,0},{4,6},{6,4},{8,10},{10,8},{12,14},{14,12},{1,3},{3,1},... | collective-permute-start | bytes 1179656 | tf_op jit(solution)/shard_map/ppermute | solution.py:169
  27.6 1.5 %collective-permute-start.20 = (bf16[64,3072]{1,0:T(8,128)(2,1)S(1)}, bf16[64,3072]{1,0:T(8,128)(2,1)S(1)}, u32[]{:S(2)}, u32[]{:S(2)}) collective-permute-start(bf16[64,3072]{1,0:T(8,128)(2,1)S(1)} %get-tuple-element.37), channel_id=1, source_target_pairs={{0,16},{16,0},{1,17},{17,1},{2,18},{18,2},{3,19},{19,3},{4,20},{20... | collective-permute-start | bytes 1179656 | tf_op jit(solution)/shard_map/ppermute | solution.py:169
  29.1 0.5 collective-permute-start.21
  29.7 1.6 %collective-permute-start.16 = (bf16[16,6144]{1,0:T(8,128)(2,1)S(1)}, bf16[16,6144]{1,0:T(8,128)(2,1)S(1)}, u32[]{:S(2)}, u32[]{:S(2)}) collective-permute-start(bf16[16,6144]{1,0:T(8,128)(2,1)S(1)} %get-tuple-element.30), channel_id=1, source_target_pairs={{0,1},{1,0},{2,3},{3,2},{4,5},{5,4},{6,7},{7,6},{8,9},{9,8},{10,11... | collective-permute-start | bytes 589832 | tf_op jit(solution)/shard_map/ppermute | solution.py:169
  31.3 1.5 %collective-permute-start.22 = (bf16[192,128]{1,0:T(8,128)(2,1)S(1)}, bf16[192,128]{1,0:T(8,128)(2,1)S(1)}, u32[]{:S(2)}, u32[]{:S(2)}) collective-permute-start(bf16[192,128]{1,0:T(8,128)(2,1)S(1)} %get-tuple-element.36.refs_2_), channel_id=1, source_target_pairs={{0,16},{16,0},{1,17},{17,1},{2,18},{18,2},{3,19},{19,3},{4,20},{20... | collective-permute-start | bytes 147464 | tf_op jit(solution)/shard_map/ppermute | solution.py:169
  32.8 3.5 %collective-permute-done.16.refs_0_ = bf16[16,6144]{1,0:T(8,128)(2,1)S(1)} collective-permute-done((bf16[16,6144]{1,0:T(8,128)(2,1)S(1)}, bf16[16,6144]{1,0:T(8,128)(2,1)S(1)}, u32[]{:S(2)}, u32[]{:S(2)}) %collective-permute-start.16) | collective-permute-done | bytes 196640 | tf_op jit(solution)/shard_map/ppermute | solution.py:169
  36.7 3.3 %collective-permute-start.18 = (bf16[4,6144]{1,0:T(4,128)(2,1)S(1)}, bf16[4,6144]{1,0:T(4,128)(2,1)S(1)}, u32[]{:S(2)}, u32[]{:S(2)}) collective-permute-start(bf16[4,6144]{1,0:T(4,128)(2,1)S(1)} %get-tuple-element.33), channel_id=1, source_target_pairs={{0,8},{2,10},{4,12},{6,14},{8,0},{10,2},{12,4},{14,6},{1,9},{3,11}... | collective-permute-start | bytes 147464 | tf_op jit(solution)/shard_map/ppermute | solution.py:169
  40.0 8.2 %collective-permute-done.22.refs_5_ = bf16[192,128]{1,0:T(8,128)(2,1)S(1)} collective-permute-done((bf16[192,128]{1,0:T(8,128)(2,1)S(1)}, bf16[192,128]{1,0:T(8,128)(2,1)S(1)}, u32[]{:S(2)}, u32[]{:S(2)}) %collective-permute-start.22) | collective-permute-done | bytes 49184 | tf_op jit(solution)/shard_map/ppermute | solution.py:169
  48.2 3.0 %collective-permute-start.19 = (bf16[4,6144]{1,0:T(4,128)(2,1)S(1)}, bf16[4,6144]{1,0:T(4,128)(2,1)S(1)}, u32[]{:S(2)}, u32[]{:S(2)}) collective-permute-start(bf16[4,6144]{1,0:T(4,128)(2,1)S(1)} %get-tuple-element.34), channel_id=1, source_target_pairs={{0,12},{2,14},{4,8},{6,10},{8,4},{10,6},{12,0},{14,2},{1,13},{3,15... | collective-permute-start | bytes 147464 | tf_op jit(solution)/shard_map/ppermute | solution.py:169
  51.2 2.9 %shard_map.109 = (f32[3072,128]{1,0:T(8,128)}, f32[3072,128]{1,0:T(8,128)}, f32[128,3072]{1,0:T(8,128)}) custom-call(bf16[64,6144]{1,0:T(8,128)(2,1)S(1)} %bitcast.12, bf16[64,3072]{1,0:T(8,128)(2,1)S(1)} %get-tuple-element.35.refs_1_, bf16[192,128]{1,0:T(8,128)(2,1)S(1)} %get-tuple-element.36.refs_2_, bf16[64,3072]{1,0:T(8,128)(2,1)S(1)} %collective-permute-done.20.refs_3_, ...), custom_call_target="tpu_custom_call" | custom-call | flops 301989888 | tf_op jit(solution)/shard_map/pallas_call | solution.py:25
  54.1 0.7 %shard_map.108 = bf16[4,6144]{1,0:T(4,128)(2,1)} custom-call(f32[4,6144]{1,0:T(4,128)S(1)} %get-tuple-element.31.kept_ref, bf16[4,6144]{1,0:T(4,128)(2,1)S(1)} %collective-permute-done.17.refs_0_, bf16[4,6144]{1,0:T(4,128)(2,1)S(1)} %collective-permute-done.18.refs_1_, bf16[4,6144]{1,0:T(4,128)(2,1)S(1)} %collective-permute-done.19.refs_2_), custom_call_target="tpu_custom_call" | custom-call | tf_op jit(solution)/shard_map/pallas_call | solution.py:25
  (42 shorter events, 0.9 us)
Async XLA Ops:
  0.6 0.8 %copy-start.7 = (bf16[4,6144]{1,0:T(4,128)(2,1)S(1)}, bf16[4,6144]{1,0:T(4,128)(2,1)}, u32[]{:S(2)}) copy-start(bf16[4,6144]{1,0:T(4,128)(2,1)} %grad_ref.1) | copy-start | bytes 147460
  1.4 0.7 %copy-start.8 = (s32[4,4]{1,0:T(4,128)S(1)}, s32[4,4]{1,0:T(4,128)}, u32[]{:S(2)}) copy-start(s32[4,4]{1,0:T(4,128)} %experts_ref.1) | copy-start | bytes 196
  2.9 7.4 %collective-permute-start.3 = (bf16[4,6272]{1,0:T(4,128)(2,1)S(1)}, bf16[4,6272]{1,0:T(4,128)(2,1)S(1)}, u32[]{:S(2)}, u32[]{:S(2)}) collective-permute-start(bf16[4,6272]{1,0:T(4,128)(2,1)S(1)} %shard_map.102.refs_0_), channel_id=1, source_target_pairs={{0,1},{1,0},{2,3},{3,2},{4,5},{5,4},{6,7},{7,6},{8,9},{9,8},{10,11... | collective-permute-start | bytes 150536 | tf_op jit(solution)/shard_map/ppermute | solution.py:169
  5.9 5.9 %collective-permute-start.2 = (bf16[4,6272]{1,0:T(4,128)(2,1)S(1)}, bf16[4,6272]{1,0:T(4,128)(2,1)S(1)}, u32[]{:S(2)}, u32[]{:S(2)}) collective-permute-start(bf16[4,6272]{1,0:T(4,128)(2,1)S(1)} %shard_map.102.refs_0_), channel_id=1, source_target_pairs={{0,12},{2,14},{4,8},{6,10},{8,4},{10,6},{12,0},{14,2},{1,13},{3,15... | collective-permute-start | bytes 150536 | tf_op jit(solution)/shard_map/ppermute | solution.py:169
  9.5 2.3 %collective-permute-start.7 = (bf16[4,6272]{1,0:T(4,128)(2,1)S(1)}, bf16[4,6272]{1,0:T(4,128)(2,1)S(1)}, u32[]{:S(2)}, u32[]{:S(2)}) collective-permute-start(bf16[4,6272]{1,0:T(4,128)(2,1)S(1)} %shard_map.102.refs_0_), channel_id=1, source_target_pairs={{0,2},{2,0},{4,6},{6,4},{8,10},{10,8},{12,14},{14,12},{1,3},{3,1},... | collective-permute-start | bytes 150536 | tf_op jit(solution)/shard_map/ppermute | solution.py:169
  9.5 5.2 %collective-permute-start.1 = (bf16[4,6272]{1,0:T(4,128)(2,1)S(1)}, bf16[4,6272]{1,0:T(4,128)(2,1)S(1)}, u32[]{:S(2)}, u32[]{:S(2)}) collective-permute-start(bf16[4,6272]{1,0:T(4,128)(2,1)S(1)} %shard_map.102.refs_0_), channel_id=1, source_target_pairs={{0,8},{2,10},{4,12},{6,14},{8,0},{10,2},{12,4},{14,6},{1,9},{3,11}... | collective-permute-start | bytes 150536 | tf_op jit(solution)/shard_map/ppermute | solution.py:169
  9.5 5.8 %collective-permute-start = (bf16[4,6272]{1,0:T(4,128)(2,1)S(1)}, bf16[4,6272]{1,0:T(4,128)(2,1)S(1)}, u32[]{:S(2)}, u32[]{:S(2)}) collective-permute-start(bf16[4,6272]{1,0:T(4,128)(2,1)S(1)} %shard_map.102.refs_0_), channel_id=1, source_target_pairs={{0,4},{2,6},{4,0},{6,2},{8,12},{10,14},{12,8},{14,10},{1,5},{3,7},... | collective-permute-start | bytes 150536 | tf_op jit(solution)/shard_map/ppermute | solution.py:169
  10.3 6.5 %collective-permute-start.11 = (bf16[4,6272]{1,0:T(4,128)(2,1)S(1)}, bf16[4,6272]{1,0:T(4,128)(2,1)S(1)}, u32[]{:S(2)}, u32[]{:S(2)}) collective-permute-start(bf16[4,6272]{1,0:T(4,128)(2,1)S(1)} %collective-permute-done.3.refs_4_), channel_id=1, source_target_pairs={{0,2},{2,0},{4,6},{6,4},{8,10},{10,8},{12,14},{14,12},{1,3},{3,1},... | collective-permute-start | bytes 150536 | tf_op jit(solution)/shard_map/ppermute | solution.py:169
  11.8 5.0 %collective-permute-start.10 = (bf16[4,6272]{1,0:T(4,128)(2,1)S(1)}, bf16[4,6272]{1,0:T(4,128)(2,1)S(1)}, u32[]{:S(2)}, u32[]{:S(2)}) collective-permute-start(bf16[4,6272]{1,0:T(4,128)(2,1)S(1)} %collective-permute-done.2.refs_3_), channel_id=1, source_target_pairs={{0,2},{2,0},{4,6},{6,4},{8,10},{10,8},{12,14},{14,12},{1,3},{3,1},... | collective-permute-start | bytes 150536 | tf_op jit(solution)/shard_map/ppermute | solution.py:169
  11.8 5.5 %collective-permute-start.6 = (bf16[4,6272]{1,0:T(4,128)(2,1)S(1)}, bf16[4,6272]{1,0:T(4,128)(2,1)S(1)}, u32[]{:S(2)}, u32[]{:S(2)}) collective-permute-start(bf16[4,6272]{1,0:T(4,128)(2,1)S(1)} %collective-permute-done.2.refs_3_), channel_id=1, source_target_pairs={{0,1},{1,0},{2,3},{3,2},{4,5},{5,4},{6,7},{7,6},{8,9},{9,8},{10,11... | collective-permute-start | bytes 150536 | tf_op jit(solution)/shard_map/ppermute | solution.py:169
  14.7 4.1 %collective-permute-start.5 = (bf16[4,6272]{1,0:T(4,128)(2,1)S(1)}, bf16[4,6272]{1,0:T(4,128)(2,1)S(1)}, u32[]{:S(2)}, u32[]{:S(2)}) collective-permute-start(bf16[4,6272]{1,0:T(4,128)(2,1)S(1)} %collective-permute-done.1.refs_2_), channel_id=1, source_target_pairs={{0,1},{1,0},{2,3},{3,2},{4,5},{5,4},{6,7},{7,6},{8,9},{9,8},{10,11... | collective-permute-start | bytes 150536 | tf_op jit(solution)/shard_map/ppermute | solution.py:169
  15.3 4.1 %collective-permute-start.4 = (bf16[4,6272]{1,0:T(4,128)(2,1)S(1)}, bf16[4,6272]{1,0:T(4,128)(2,1)S(1)}, u32[]{:S(2)}, u32[]{:S(2)}) collective-permute-start(bf16[4,6272]{1,0:T(4,128)(2,1)S(1)} %collective-permute-done.refs_1_), channel_id=1, source_target_pairs={{0,1},{1,0},{2,3},{3,2},{4,5},{5,4},{6,7},{7,6},{8,9},{9,8},{10,11... | collective-permute-start | bytes 150536 | tf_op jit(solution)/shard_map/ppermute | solution.py:169
  16.8 7.2 %collective-permute-start.9 = (bf16[4,6272]{1,0:T(4,128)(2,1)S(1)}, bf16[4,6272]{1,0:T(4,128)(2,1)S(1)}, u32[]{:S(2)}, u32[]{:S(2)}) collective-permute-start(bf16[4,6272]{1,0:T(4,128)(2,1)S(1)} %collective-permute-done.1.refs_2_), channel_id=1, source_target_pairs={{0,2},{2,0},{4,6},{6,4},{8,10},{10,8},{12,14},{14,12},{1,3},{3,1},... | collective-permute-start | bytes 150536 | tf_op jit(solution)/shard_map/ppermute | solution.py:169
  16.8 7.2 %collective-permute-start.8 = (bf16[4,6272]{1,0:T(4,128)(2,1)S(1)}, bf16[4,6272]{1,0:T(4,128)(2,1)S(1)}, u32[]{:S(2)}, u32[]{:S(2)}) collective-permute-start(bf16[4,6272]{1,0:T(4,128)(2,1)S(1)} %collective-permute-done.refs_1_), channel_id=1, source_target_pairs={{0,2},{2,0},{4,6},{6,4},{8,10},{10,8},{12,14},{14,12},{1,3},{3,1},... | collective-permute-start | bytes 150536 | tf_op jit(solution)/shard_map/ppermute | solution.py:169
  17.3 6.7 %collective-permute-start.14 = (bf16[4,6272]{1,0:T(4,128)(2,1)S(1)}, bf16[4,6272]{1,0:T(4,128)(2,1)S(1)}, u32[]{:S(2)}, u32[]{:S(2)}) collective-permute-start(bf16[4,6272]{1,0:T(4,128)(2,1)S(1)} %collective-permute-done.6.refs_7_), channel_id=1, source_target_pairs={{0,2},{2,0},{4,6},{6,4},{8,10},{10,8},{12,14},{14,12},{1,3},{3,1},... | collective-permute-start | bytes 150536 | tf_op jit(solution)/shard_map/ppermute | solution.py:169
  18.8 5.2 %collective-permute-start.13 = (bf16[4,6272]{1,0:T(4,128)(2,1)S(1)}, bf16[4,6272]{1,0:T(4,128)(2,1)S(1)}, u32[]{:S(2)}, u32[]{:S(2)}) collective-permute-start(bf16[4,6272]{1,0:T(4,128)(2,1)S(1)} %collective-permute-done.5.refs_6_), channel_id=1, source_target_pairs={{0,2},{2,0},{4,6},{6,4},{8,10},{10,8},{12,14},{14,12},{1,3},{3,1},... | collective-permute-start | bytes 150536 | tf_op jit(solution)/shard_map/ppermute | solution.py:169
  19.4 4.7 %collective-permute-start.12 = (bf16[4,6272]{1,0:T(4,128)(2,1)S(1)}, bf16[4,6272]{1,0:T(4,128)(2,1)S(1)}, u32[]{:S(2)}, u32[]{:S(2)}) collective-permute-start(bf16[4,6272]{1,0:T(4,128)(2,1)S(1)} %collective-permute-done.4.refs_5_), channel_id=1, source_target_pairs={{0,2},{2,0},{4,6},{6,4},{8,10},{10,8},{12,14},{14,12},{1,3},{3,1},... | collective-permute-start | bytes 150536 | tf_op jit(solution)/shard_map/ppermute | solution.py:169
  19.4 1.4 %copy-start = (bf16[1,6144,128]{2,1,0:T(8,128)(2,1)S(1)}, bf16[1,6144,128]{2,1,0:T(8,128)(2,1)}, u32[]{:S(2)}) copy-start(bf16[1,6144,128]{2,1,0:T(8,128)(2,1)} %param.11) | copy-start | bytes 4718596
  20.8 1.4 %copy-start.2 = (bf16[1,6144,128]{2,1,0:T(8,128)(2,1)S(1)}, bf16[1,6144,128]{2,1,0:T(8,128)(2,1)}, u32[]{:S(2)}) copy-start(bf16[1,6144,128]{2,1,0:T(8,128)(2,1)} %param.12) | copy-start | bytes 4718596
  22.2 1.1 %copy-start.4 = (bf16[1,1,64,6144]{3,2,1,0:T(8,128)(2,1)S(1)}, bf16[1,1,64,6144]{3,2,1,0:T(8,128)(2,1)}, u32[]{:S(2)}) copy-start(bf16[1,1,64,6144]{3,2,1,0:T(8,128)(2,1)} %param.10) | copy-start | bytes 2359300
  23.3 1.4 %copy-start.6 = (bf16[1,128,6144]{2,1,0:T(8,128)(2,1)S(1)}, bf16[1,128,6144]{2,1,0:T(8,128)(2,1)}, u32[]{:S(2)}) copy-start(bf16[1,128,6144]{2,1,0:T(8,128)(2,1)} %param.13) | copy-start | bytes 4718596
  23.3 2.3 %copy-start.3 = (bf16[1,6144,128]{2,1,0:T(8,128)(2,1)S(1)}, bf16[1,6144,128]{2,1,0:T(8,128)(2,1)}, u32[]{:S(2)}) copy-start(bf16[1,6144,128]{2,1,0:T(8,128)(2,1)} %param.12) | copy-start | bytes 4718596
  24.0 1.9 %copy-start.1 = (bf16[1,6144,128]{2,1,0:T(8,128)(2,1)S(1)}, bf16[1,6144,128]{2,1,0:T(8,128)(2,1)}, u32[]{:S(2)}) copy-start(bf16[1,6144,128]{2,1,0:T(8,128)(2,1)} %param.11) | copy-start | bytes 4718596
  27.0 24.2 %copy-start.5 = (bf16[1,1,64,6144]{3,2,1,0:T(8,128)(2,1)S(1)}, bf16[1,1,64,6144]{3,2,1,0:T(8,128)(2,1)}, u32[]{:S(2)}) copy-start(bf16[1,1,64,6144]{3,2,1,0:T(8,128)(2,1)} %param.10) | copy-start | bytes 2359300
  27.1 2.6 %collective-permute-start.15 = (bf16[32,6144]{1,0:T(8,128)(2,1)S(1)}, bf16[32,6144]{1,0:T(8,128)(2,1)S(1)}, u32[]{:S(2)}, u32[]{:S(2)}) collective-permute-start(bf16[32,6144]{1,0:T(8,128)(2,1)S(1)} %get-tuple-element.28), channel_id=1, source_target_pairs={{0,2},{2,0},{4,6},{6,4},{8,10},{10,8},{12,14},{14,12},{1,3},{3,1},... | collective-permute-start | bytes 1179656 | tf_op jit(solution)/shard_map/ppermute | solution.py:169
  27.6 23.6 %collective-permute-start.20 = (bf16[64,3072]{1,0:T(8,128)(2,1)S(1)}, bf16[64,3072]{1,0:T(8,128)(2,1)S(1)}, u32[]{:S(2)}, u32[]{:S(2)}) collective-permute-start(bf16[64,3072]{1,0:T(8,128)(2,1)S(1)} %get-tuple-element.37), channel_id=1, source_target_pairs={{0,16},{16,0},{1,17},{17,1},{2,18},{18,2},{3,19},{19,3},{4,20},{20... | collective-permute-start | bytes 1179656 | tf_op jit(solution)/shard_map/ppermute | solution.py:169
  29.1 22.1 %collective-permute-start.21 = (bf16[64,3072]{1,0:T(8,128)(2,1)S(1)}, bf16[64,3072]{1,0:T(8,128)(2,1)S(1)}, u32[]{:S(2)}, u32[]{:S(2)}) collective-permute-start(bf16[64,3072]{1,0:T(8,128)(2,1)S(1)} %get-tuple-element.38), channel_id=1, source_target_pairs={{0,16},{16,0},{1,17},{17,1},{2,18},{18,2},{3,19},{19,3},{4,20},{20... | collective-permute-start | bytes 1179656 | tf_op jit(solution)/shard_map/ppermute | solution.py:169
  29.7 6.6 %collective-permute-start.16 = (bf16[16,6144]{1,0:T(8,128)(2,1)S(1)}, bf16[16,6144]{1,0:T(8,128)(2,1)S(1)}, u32[]{:S(2)}, u32[]{:S(2)}) collective-permute-start(bf16[16,6144]{1,0:T(8,128)(2,1)S(1)} %get-tuple-element.30), channel_id=1, source_target_pairs={{0,1},{1,0},{2,3},{3,2},{4,5},{5,4},{6,7},{7,6},{8,9},{9,8},{10,11... | collective-permute-start | bytes 589832 | tf_op jit(solution)/shard_map/ppermute | solution.py:169
  31.3 16.9 %collective-permute-start.22 = (bf16[192,128]{1,0:T(8,128)(2,1)S(1)}, bf16[192,128]{1,0:T(8,128)(2,1)S(1)}, u32[]{:S(2)}, u32[]{:S(2)}) collective-permute-start(bf16[192,128]{1,0:T(8,128)(2,1)S(1)} %get-tuple-element.36.refs_2_), channel_id=1, source_target_pairs={{0,16},{16,0},{1,17},{17,1},{2,18},{18,2},{3,19},{19,3},{4,20},{20... | collective-permute-start | bytes 147464 | tf_op jit(solution)/shard_map/ppermute | solution.py:169
  36.3 17.8 %collective-permute-start.17 = (bf16[4,6144]{1,0:T(4,128)(2,1)S(1)}, bf16[4,6144]{1,0:T(4,128)(2,1)S(1)}, u32[]{:S(2)}, u32[]{:S(2)}) collective-permute-start(bf16[4,6144]{1,0:T(4,128)(2,1)S(1)} %get-tuple-element.32), channel_id=1, source_target_pairs={{0,4},{2,6},{4,0},{6,2},{8,12},{10,14},{12,8},{14,10},{1,5},{3,7},... | collective-permute-start | bytes 147464 | tf_op jit(solution)/shard_map/ppermute | solution.py:169
  36.7 17.4 %collective-permute-start.18 = (bf16[4,6144]{1,0:T(4,128)(2,1)S(1)}, bf16[4,6144]{1,0:T(4,128)(2,1)S(1)}, u32[]{:S(2)}, u32[]{:S(2)}) collective-permute-start(bf16[4,6144]{1,0:T(4,128)(2,1)S(1)} %get-tuple-element.33), channel_id=1, source_target_pairs={{0,8},{2,10},{4,12},{6,14},{8,0},{10,2},{12,4},{14,6},{1,9},{3,11}... | collective-permute-start | bytes 147464 | tf_op jit(solution)/shard_map/ppermute | solution.py:169
  48.2 5.9 %collective-permute-start.19 = (bf16[4,6144]{1,0:T(4,128)(2,1)S(1)}, bf16[4,6144]{1,0:T(4,128)(2,1)S(1)}, u32[]{:S(2)}, u32[]{:S(2)}) collective-permute-start(bf16[4,6144]{1,0:T(4,128)(2,1)S(1)} %get-tuple-element.34), channel_id=1, source_target_pairs={{0,12},{2,14},{4,8},{6,10},{8,4},{10,6},{12,0},{14,2},{1,13},{3,15... | collective-permute-start | bytes 147464 | tf_op jit(solution)/shard_map/ppermute | solution.py:169
  (1 other events, 0.7 us)

commit v2 on v1

--- a/solution.py
+++ b/solution.py
@@ -22,13 +22,14 @@
 
 
 def local_call(kernel, out_shape, args, flops=0, scratch=(), nbytes=0):
+    whole = pl.BlockSpec(memory_space=pltpu.VMEM)
     return pl.pallas_call(
         kernel,
         out_shape=out_shape,
-        in_specs=[pl.BlockSpec(memory_space=pltpu.VMEM)] * len(args),
-        out_specs=jax.tree.map(lambda _: pl.BlockSpec(memory_space=pltpu.VMEM), out_shape),
+        in_specs=[whole] * len(args),
+        out_specs=jax.tree.map(lambda _: whole, out_shape),
         scratch_shapes=list(scratch),
-        compiler_params=pltpu.CompilerParams(vmem_limit_bytes=30 * 1024 * 1024),
+        compiler_params=pltpu.CompilerParams(vmem_limit_bytes=20 * 1024 * 1024),
         cost_estimate=pl.CostEstimate(flops=flops, bytes_accessed=nbytes, transcendentals=0),
     )(*args)
 
@@ -60,33 +61,47 @@
     out_ref[:, width:] = record.astype(BF16)
 
 
-def pre_kernel(replicas, x_ref, w_in_ref, w_lin_ref, gate_ref, linear_ref, *send_refs):
-    share = x_ref.shape[1] // replicas
+def stack_kernel(*refs):
+    for i, piece in enumerate(refs[:-1]):
+        refs[-1][i] = piece[...]
+
+
+def join_kernel(count, *refs):
+    pieces, out_ref = refs[:count], refs[-1]
+    width = out_ref.shape[1]
+    for begin in range(0, width, 896):
+        cols = slice(begin, min(begin + 896, width))
+        rows = []
+        for ref in pieces:
+            parts = [ref[:, cols]] if len(ref.shape) == 2 else [ref[i, :, cols] for i in range(ref.shape[0])]
+            rows += [part.astype(F32) for part in parts]
+        out_ref[:, cols] = jnp.concatenate(rows, axis=0).astype(BF16)
+
+
+def share_kernel(x_ref, after_ref, *send_refs):
+    del after_ref
+    share = send_refs[0].shape[1]
     me = lax.axis_index("rep")
-    for j, send_ref in enumerate(send_refs):
-        start = pl.multiple_of((me ^ (j + 1)) * share, LANES)
-        send_ref[...] = x_ref[:, pl.ds(start, share)]
+    for i, send_ref in enumerate(send_refs):
+        send_ref[...] = x_ref[:, pl.ds(pl.multiple_of((me ^ (i + 1)) * share, LANES), share)]
+
+
+def pre_kernel(x_ref, w_in_ref, w_lin_ref, after_ref, gate_ref, linear_ref):
+    del after_ref
     gate_ref[...] = jnp.dot(x_ref[...], w_in_ref[...], preferred_element_type=F32)
     linear_ref[...] = jnp.dot(x_ref[...], w_lin_ref[...], preferred_element_type=F32)
 
 
-def factor_kernel(replicas, count, *refs):
+def main_kernel(replicas, count, *refs):
     pieces, refs = refs[:count], refs[count:]
-    gate_ref, linear_ref, w_out_ref = refs[:3]
-    d_gate_ref, d_linear_ref, factor_ref, own_ref = refs[3:7]
-    send_refs = refs[7 : 7 + replicas - 1]
-    t_ref = refs[-1]
+    gate_ref, linear_ref, w_out_ref, w_in_ref, w_lin_ref = refs[:5]
+    keep_ref, back_ref, factor_ref, own_ref, *send_refs, t_ref = refs[5:]
     rows = pieces[0].shape[0]
     tokens = rows * count
     width = w_out_ref.shape[1]
     slots = gate_ref.shape[0]
-    together = 16 // rows if 16 % rows == 0 and tokens % 16 == 0 else count
-    for first in range(0, count, together):
-        group = pieces[first : first + together]
-        for begin in range(0, width + LANES, 896):
-            cols = slice(begin, min(begin + 896, width + LANES))
-            block = jnp.concatenate([p[:, cols].astype(F32) for p in group], axis=0)
-            t_ref[first * rows : (first + together) * rows, cols] = block.astype(BF16)
+    for i, piece in enumerate(pieces):
+        t_ref[i * rows : (i + 1) * rows, :] = piece[...]
     record = t_ref[:, width:].astype(F32)
     lane = lax.broadcasted_iota(jnp.int32, (tokens, LANES), 1)
     expert = lax.axis_index("exp")
@@ -106,8 +121,13 @@
     d_hidden = nt(t_ref[:, :width], w_out_ref[...]) * gates
     d_gate = (d_hidden * pre_linear * sigmoid * (1.0 + pre_gate * (1.0 - sigmoid))).astype(BF16)
     d_linear = (d_hidden * activated).astype(BF16)
-    d_gate_ref[...] = d_gate
-    d_linear_ref[...] = d_linear
+    half = tokens // 2
+    step = 1536 if width % 1536 == 0 else width
+    for begin in range(0, width, step):
+        cols = slice(begin, begin + step)
+        out = nt(d_gate, w_in_ref[cols, :]) + nt(d_linear, w_lin_ref[cols, :])
+        keep_ref[:, cols] = out[:half]
+        back_ref[:, cols] = out[half:].astype(BF16)
     table = table.astype(BF16)
     factor_ref[:slots] = tn(table, d_gate).astype(BF16)
     factor_ref[slots : 2 * slots] = tn(table, d_linear).astype(BF16)
@@ -119,27 +139,25 @@
         send_ref[...] = t_ref[:, pl.ds(pl.multiple_of((me ^ (j + 1)) * share, LANES), share)]
 
 
-def rows_kernel(d_gate_ref, d_linear_ref, w_in_ref, w_lin_ref, keep_ref, send_ref):
-    half, width = keep_ref.shape
-    step = 1536 if width % 1536 == 0 else width
-    for begin in range(0, width, step):
-        cols = slice(begin, begin + step)
-        rows = nt(d_gate_ref[...], w_in_ref[cols, :]) + nt(d_linear_ref[...], w_lin_ref[cols, :])
-        keep_ref[:, cols] = rows[:half]
-        send_ref[:, cols] = rows[half:].astype(BF16)
-
-
-def sum_kernel(arrived, kept_ref, *refs):
-    arrived_refs, keep_ref, send_refs = refs[:arrived], refs[arrived], refs[arrived + 1 :]
-    rows, width = keep_ref.shape
+def sum_kernel(arrived, cuts, *refs):
+    kept_ref, arrived_refs, out_refs = refs[0], refs[1 : 1 + arrived], refs[1 + arrived :]
+    width = kept_ref.shape[1]
     for begin in range(0, width, 1024):
         cols = slice(begin, min(begin + 1024, width))
         total = kept_ref[:, cols]
         for ref in arrived_refs:
             total = total + ref[:, cols].astype(F32)
-        keep_ref[:, cols] = total[:rows].astype(keep_ref.dtype)
-        for i, ref in enumerate(send_refs):
-            ref[:, cols] = total[(i + 1) * rows : (i + 2) * rows].astype(BF16)
+        for ref, (first, last) in zip(out_refs, cuts):
+            ref[:, cols] = total[first:last].astype(ref.dtype)
+
+
+def summed(kept, arrived, cuts, kinds):
+    width = kept.shape[1]
+    return local_call(
+        functools.partial(sum_kernel, len(arrived), cuts),
+        [jax.ShapeDtypeStruct((last - first, width), kind) for (first, last), kind in zip(cuts, kinds)],
+        (kept, *arrived),
+    )
 
 
 def weights_kernel(replicas, slots, *refs):
@@ -185,64 +203,65 @@
         functools.partial(pack_kernel, capacity, groups),
         shape((tokens_here, width + LANES), BF16),
         (out_grad, experts, gates),
-    )
-    column = [own] + [swap(own, "exp", k) for k in range(2, groups, 2)]
-    plane = list(column)
-    for j in range(1, column_groups):
-        plane += [swap(piece, "ffn", j) for piece in column]
-    pieces = plane + [swap(piece, "exp", 1) for piece in plane]
-
-    pre_gate, pre_linear, *x_sends = local_call(
-        functools.partial(pre_kernel, replicas),
-        [shape((slots, hidden_count), F32)] * 2 + [shape((slots, share), BF16)] * (replicas - 1),
-        (inputs, gate_w, linear_w),
+        flops=100 * weight_flops,
+    )
+    across = range(1, column_groups)
+    far = [swap(own, "exp", k) for k in range(groups - 2, 0, -2)][::-1]
+    beside = [swap(own, "ffn", j) for j in across]
+    stack = local_call(stack_kernel, shape((len(far), *own.shape), BF16), tuple(far), flops=50 * weight_flops)
+    pieces = [own, stack]
+    for j, piece in zip(across, beside):
+        pieces += [piece, swap(stack, "ffn", j)]
+    x_sends = local_call(
+        share_kernel, [shape((slots, share), BF16)] * (replicas - 1), (inputs, far[0])
+    )
+    x_others = [swap(x, "rep", i + 1) for i, x in enumerate(x_sends)]
+    near_rows = local_call(
+        functools.partial(join_kernel, len(pieces)),
+        shape((tokens // 2, width + LANES), BF16),
+        (*pieces, *x_others),
+    )
+    parts = (near_rows, swap(near_rows, "exp", 1))
+
+    pre_gate, pre_linear = local_call(
+        pre_kernel,
+        [shape((slots, hidden_count), F32)] * 2,
+        (inputs, gate_w, linear_w, far[0]),
         flops=2 * weight_flops,
     )
-    x_others = [swap(x, "rep", j + 1) for j, x in enumerate(x_sends)]
-
-    d_gate, d_linear, factors, t_own, *t_sends = local_call(
-        functools.partial(factor_kernel, replicas, len(pieces)),
-        [shape((tokens, hidden_count), BF16)] * 2
-        + [shape((2 * slots + tokens, hidden_count), BF16)]
-        + [shape((tokens, share), BF16)] * replicas,
-        (*pieces, pre_gate, pre_linear, down_w),
-        flops=weight_flops,
+    keep, send, factors, t_own, *t_sends = local_call(
+        functools.partial(main_kernel, replicas, len(parts)),
+        [shape((tokens // 2, width), F32), shape((tokens // 2, width), BF16)]
+        + [shape((2 * slots + tokens, hidden_count), BF16), shape((tokens, share), BF16)]
+        + [shape((tokens, share), BF16)] * (replicas - 1),
+        (*parts, pre_gate, pre_linear, down_w, gate_w, linear_w),
+        flops=3 * weight_flops,
         scratch=[pltpu.VMEM((tokens, width + LANES), BF16)],
     )
-    keep, send = local_call(
-        rows_kernel,
-        [shape((tokens // 2, width), F32), shape((tokens // 2, width), BF16)],
-        (d_gate, d_linear, gate_w, linear_w),
-        flops=2 * weight_flops,
-    )
     back = swap(send, "exp", 1)
+    t_others = [swap(t, "rep", j + 1) for j, t in enumerate(t_sends)]
     f_others = [swap(factors, "rep", j) for j in range(1, replicas)]
-    t_others = [swap(t, "rep", j + 1) for j, t in enumerate(t_sends)]
 
     rows = tokens // 2 // column_groups
-    keep, *sends = local_call(
-        functools.partial(sum_kernel, 1),
-        [shape((rows, width), F32)] + [shape((rows, width), BF16)] * (column_groups - 1),
-        (keep, back),
-    )
-    backs = [swap(s, "ffn", j + 1) for j, s in enumerate(sends)]
-    keep, *sends = local_call(
-        functools.partial(sum_kernel, len(backs)),
-        [shape((tokens_here, width), F32)] + [shape((tokens_here, width), BF16)] * (groups // 2 - 1),
-        (keep, *backs),
-    )
-    backs = [swap(s, "exp", 2 * (j + 1)) for j, s in enumerate(sends)]
+    half = rows // 2
+    cuts = [(j * rows + h * half, j * rows + (h + 1) * half) for h in (0, 1) for j in range(column_groups)]
+    kinds = ([F32] + [BF16] * (column_groups - 1)) * 2
+    near, *sends = summed(keep, [back], cuts, kinds)
+    near_sends, (away, *away_sends) = sends[: column_groups - 1], sends[column_groups - 1 :]
+    cuts = [(i, i + tokens_here) for i in range(0, half, tokens_here)]
+    away_backs = [swap(s, "ffn", j + 1) for j, s in enumerate(away_sends)]
+    near_backs = [swap(s, "ffn", j + 1) for j, s in enumerate(near_sends)]
+    away_sends = summed(away, away_backs, cuts, [BF16] * len(cuts))
+    keep, *near_sends = summed(near, near_backs, cuts, [F32] + [BF16] * (len(cuts) - 1))
+    backs = [swap(s, "exp", 2 * (j + len(cuts))) for j, s in enumerate(away_sends)]
+    backs += [swap(s, "exp", 2 * (j + 1)) for j, s in enumerate(near_sends)]
     grad_w1, grad_v1, grad_w2 = local_call(
         functools.partial(weights_kernel, replicas, slots),
         [shape((share, hidden_count), F32)] * 2 + [shape((hidden_count, share), F32)],
         (inputs, t_own, factors, *x_others, *t_others, *f_others),
         flops=3 * weight_flops,
     )
-    (grad_input,) = local_call(
-        functools.partial(sum_kernel, len(backs)),
-        [shape((tokens_here, width), BF16)],
-        (keep, *backs),
-    )
+    (grad_input,) = summed(keep, backs, [(0, tokens_here)], [BF16])
     return grad_input, grad_w1[None], grad_v1[None], grad_w2[None]
 
 

time: 55.1 us -> 42.1 us (0.76)
  waiting for transfers between devices: 17.8 us -> 12.9 us
  local copies, waits for them, and re-layouts: 6.97 us -> 2.24 us
  starting transfers between devices: 22.7 us -> 18.8 us
  Pallas kernels: 6.55 us -> 7.2 us
    ppermute x23 -> x15, waiting for transfers between devices: 17.8 us -> 12.9 us  [swap(): return lax.ppermute(values, axis, [(i, i ^ distance) for i in range(size)])]
    unnamed x20 -> x14, local copies, waits for them, and re-layouts: 6.97 us -> 2.24 us
    ppermute x23 -> x15, starting transfers between devices: 22.7 us -> 18.8 us  [swap(): return lax.ppermute(values, axis, [(i, i ^ distance) for i in range(size)])]
    pallas_call x8 -> x11, Pallas kernels: 6.55 us -> 7.2 us  [local_call(): pl.pallas_call(kernel, out_shape=out_shape, in_specs=[whole] * len(args),...]
  transfers between devices with their start and end apart: 23 -> 15, of which waited for: 6 -> 8; matrix products, arithmetic and copies ran while one was open for 0% -> 0% of each run, Pallas kernels for 7% -> 9%
where the time goes in v2:
time: 42.1 us; the launch traced here: 41.9 us
  starting transfers between devices  18.8 us (45%)
  waiting for transfers between devices  12.9 us (31%)
  Pallas kernels  7.2 us (17%)
  local copies, waits for them, and re-layouts  2.24 us (5%)
  between operations  0.74 us (2%)
    ppermute x15, starting transfers between devices, swap(): return lax.ppermute(values, axis, [(i, i ^ distance) for i in range(size)])  18.8 us
    ppermute x15, waiting for transfers between devices, swap(): return lax.ppermute(values, axis, [(i, i ^ distance) for i in range(size)])  12.9 us
    pallas_call x11, Pallas kernels, local_call(): pl.pallas_call(kernel, out_shape=out_shape, in_specs=[whole] * len(args),...  7.2 us
    unnamed x14, local copies, waits for them, and re-layouts  2.24 us
  transfers between devices with their start and end apart: 15, of which 8 were waited for; matrix products, arithmetic and copies ran while one was open for 0% of the time, Pallas kernels for 9%

profile of v2, /device:TPU:0, one launch (start us, length us, event | category | flops | bytes accessed | tf_op | source)
XLA Modules:
  0.0 41.9 jit_solution(6959556677849208122)
XLA Ops:
  0.7 0.9 %copy-done.4 = bf16[4,6144]{1,0:T(4,128)(2,1)S(1)} copy-done((bf16[4,6144]{1,0:T(4,128)(2,1)S(1)}, bf16[4,6144]{1,0:T(4,128)(2,1)}, u32[]{:S(2)}) %copy-start.4) | copy-done | bytes 49176
  1.5 0.7 %copy-done.5 = s32[4,4]{1,0:T(4,128)S(1)} copy-done((s32[4,4]{1,0:T(4,128)S(1)}, s32[4,4]{1,0:T(4,128)}, u32[]{:S(2)}) %copy-start.5) | copy-done | bytes 88
  2.2 0.7 %copy-done.6 = f32[4,4]{1,0:T(4,128)S(1)} copy-done((f32[4,4]{1,0:T(4,128)S(1)}, f32[4,4]{1,0:T(4,128)}, u32[]{:S(2)}) %copy-start.6) | copy-done | bytes 88
  2.9 0.1 shard_map.102.refs_0_
  3.0 3.1 %collective-permute-start = (bf16[4,6272]{1,0:T(4,128)(2,1)S(1)}, bf16[4,6272]{1,0:T(4,128)(2,1)S(1)}, u32[]{:S(2)}, u32[]{:S(2)}) collective-permute-start(bf16[4,6272]{1,0:T(4,128)(2,1)S(1)} %shard_map.102.refs_0_), channel_id=1, source_target_pairs={{0,4},{2,6},{4,0},{6,2},{8,12},{10,14},{12,8},{14,10},{1,5},{3,7},... | collective-permute-start | bytes 150536 | tf_op jit(solution)/shard_map/ppermute | solution.py:187
  6.1 2.5 %collective-permute-start.2 = (bf16[4,6272]{1,0:T(4,128)(2,1)S(1)}, bf16[4,6272]{1,0:T(4,128)(2,1)S(1)}, u32[]{:S(2)}, u32[]{:S(2)}) collective-permute-start(bf16[4,6272]{1,0:T(4,128)(2,1)S(1)} %shard_map.102.refs_0_), channel_id=1, source_target_pairs={{0,12},{2,14},{4,8},{6,10},{8,4},{10,6},{12,0},{14,2},{1,13},{3,15... | collective-permute-start | bytes 150536 | tf_op jit(solution)/shard_map/ppermute | solution.py:187
  8.5 0.1 collective-permute-start.1
  8.7 1.6 %collective-permute-start.5 = (bf16[64,3072]{1,0:T(8,128)(2,1)S(1)}, bf16[64,3072]{1,0:T(8,128)(2,1)S(1)}, u32[]{:S(2)}, u32[]{:S(2)}) collective-permute-start(bf16[64,3072]{1,0:T(8,128)(2,1)S(1)} %shard_map.104), channel_id=1, source_target_pairs={{0,16},{16,0},{1,17},{17,1},{2,18},{18,2},{3,19},{19,3},{4,20},{20... | collective-permute-start | bytes 1179656 | tf_op jit(solution)/shard_map/ppermute | solution.py:187
  10.3 2.3 %collective-permute-done.2.refs_2_ = bf16[4,6272]{1,0:T(4,128)(2,1)S(1)} collective-permute-done((bf16[4,6272]{1,0:T(4,128)(2,1)S(1)}, bf16[4,6272]{1,0:T(4,128)(2,1)S(1)}, u32[]{:S(2)}, u32[]{:S(2)}) %collective-permute-start.2) | collective-permute-done | bytes 50208 | tf_op jit(solution)/shard_map/ppermute | solution.py:187
  12.6 1.5 %collective-permute-done.1.refs_1_ = bf16[4,6272]{1,0:T(4,128)(2,1)S(1)} collective-permute-done((bf16[4,6272]{1,0:T(4,128)(2,1)S(1)}, bf16[4,6272]{1,0:T(4,128)(2,1)S(1)}, u32[]{:S(2)}, u32[]{:S(2)}) %collective-permute-start.1) | collective-permute-done | bytes 50208 | tf_op jit(solution)/shard_map/ppermute | solution.py:187
  14.1 1.6 %collective-permute-start.4 = (bf16[3,4,6272]{2,1,0:T(4,128)(2,1)S(1)}, bf16[3,4,6272]{2,1,0:T(4,128)(2,1)S(1)}, u32[]{:S(2)}, u32[]{:S(2)}) collective-permute-start(bf16[3,4,6272]{2,1,0:T(4,128)(2,1)S(1)} %shard_map.103.refs_1_), channel_id=1, source_target_pairs={{0,1},{1,0},{2,3},{3,2},{4,5},{5,4},{6,7},{7,6},{8,9},{9,8},{10,11... | collective-permute-start | bytes 451592 | tf_op jit(solution)/shard_map/ppermute | solution.py:187
  15.6 0.5 %collective-permute-start.3 = (bf16[4,6272]{1,0:T(4,128)(2,1)S(1)}, bf16[4,6272]{1,0:T(4,128)(2,1)S(1)}, u32[]{:S(2)}, u32[]{:S(2)}) collective-permute-start(bf16[4,6272]{1,0:T(4,128)(2,1)S(1)} %shard_map.102.refs_0_), channel_id=1, source_target_pairs={{0,1},{1,0},{2,3},{3,2},{4,5},{5,4},{6,7},{7,6},{8,9},{9,8},{10,11... | collective-permute-start | bytes 150536 | tf_op jit(solution)/shard_map/ppermute | solution.py:187
  16.2 3.7 %collective-permute-done.3.refs_2_ = bf16[4,6272]{1,0:T(4,128)(2,1)S(1)} collective-permute-done((bf16[4,6272]{1,0:T(4,128)(2,1)S(1)}, bf16[4,6272]{1,0:T(4,128)(2,1)S(1)}, u32[]{:S(2)}, u32[]{:S(2)}) %collective-permute-start.3) | collective-permute-done | bytes 50208 | tf_op jit(solution)/shard_map/ppermute | solution.py:187
  19.9 0.1 shard_map.105.refs_0_
  20.0 0.1 collective-permute-start.6
  20.1 0.6 %shard_map.106 = (f32[64,128]{1,0:T(8,128)S(1)}, f32[64,128]{1,0:T(8,128)S(1)}) custom-call(bf16[64,6144]{1,0:T(8,128)(2,1)S(1)} %bitcast.8, bf16[6144,128]{1,0:T(8,128)(2,1)S(1)} %bitcast.10, bf16[6144,128]{1,0:T(8,128)(2,1)S(1)} %bitcast.12, bf16[4,6272]{1,0:T(4,128)(2,1)S(1)} %collective-permute-done.refs_0_.after_ref), custom_call_target="tpu_custom_call" | custom-call | flops 201326592 | tf_op jit(solution)/shard_map/pallas_call | solution.py:26
  20.7 1.1 %collective-permute-done.6.refs_1_ = bf16[32,6272]{1,0:T(8,128)(2,1)S(1)} collective-permute-done((bf16[32,6272]{1,0:T(8,128)(2,1)S(1)}, bf16[32,6272]{1,0:T(8,128)(2,1)S(1)}, u32[]{:S(2)}, u32[]{:S(2)}) %collective-permute-start.6) | collective-permute-done | bytes 401440 | tf_op jit(solution)/shard_map/ppermute | solution.py:187
  21.8 2.6 %shard_map.107 = (f32[32,6144]{1,0:T(8,128)S(1)}, bf16[32,6144]{1,0:T(8,128)(2,1)S(1)}, bf16[192,128]{1,0:T(8,128)(2,1)S(1)}, bf16[64,3072]{1,0:T(8,128)(2,1)S(1)}, bf16[64,3072]{1,0:T(8,128)(2,1)S(1)}) custom-call(bf16[32,6272]{1,0:T(8,128)(2,1)S(1)} %shard_map.105.refs_0_, bf16[32,6272]{1,0:T(8,128)(2,1)S(1)} %collective-permute-done.6.refs_1_, ...), custom_call_target="tpu_custom_call" | custom-call | flops 301989888 | tf_op jit(solution)/shard_map/pallas_call | solution.py:26
  24.4 0.2 collective-permute-start.7
  24.7 1.5 %collective-permute-start.13 = (bf16[64,3072]{1,0:T(8,128)(2,1)S(1)}, bf16[64,3072]{1,0:T(8,128)(2,1)S(1)}, u32[]{:S(2)}, u32[]{:S(2)}) collective-permute-start(bf16[64,3072]{1,0:T(8,128)(2,1)S(1)} %get-tuple-element.36), channel_id=1, source_target_pairs={{0,16},{16,0},{1,17},{17,1},{2,18},{18,2},{3,19},{19,3},{4,20},{20... | collective-permute-start | bytes 1179656 | tf_op jit(solution)/shard_map/ppermute | solution.py:187
  26.3 1.6 %collective-permute-start.8 = (bf16[8,6144]{1,0:T(8,128)(2,1)S(1)}, bf16[8,6144]{1,0:T(8,128)(2,1)S(1)}, u32[]{:S(2)}, u32[]{:S(2)}) collective-permute-start(bf16[8,6144]{1,0:T(8,128)(2,1)S(1)} %get-tuple-element.27), channel_id=1, source_target_pairs={{0,1},{1,0},{2,3},{3,2},{4,5},{5,4},{6,7},{7,6},{8,9},{9,8},{10,11... | collective-permute-start | bytes 294920 | tf_op jit(solution)/shard_map/ppermute | solution.py:187
  27.9 0.5 %collective-permute-start.9 = (bf16[8,6144]{1,0:T(8,128)(2,1)S(1)}, bf16[8,6144]{1,0:T(8,128)(2,1)S(1)}, u32[]{:S(2)}, u32[]{:S(2)}) collective-permute-start(bf16[8,6144]{1,0:T(8,128)(2,1)S(1)} %get-tuple-element.30), channel_id=1, source_target_pairs={{0,1},{1,0},{2,3},{3,2},{4,5},{5,4},{6,7},{7,6},{8,9},{9,8},{10,11... | collective-permute-start | bytes 294920 | tf_op jit(solution)/shard_map/ppermute | solution.py:187
  28.4 1.5 %collective-permute-start.14 = (bf16[192,128]{1,0:T(8,128)(2,1)S(1)}, bf16[192,128]{1,0:T(8,128)(2,1)S(1)}, u32[]{:S(2)}, u32[]{:S(2)}) collective-permute-start(bf16[192,128]{1,0:T(8,128)(2,1)S(1)} %get-tuple-element.35.refs_2_), channel_id=1, source_target_pairs={{0,16},{16,0},{1,17},{17,1},{2,18},{18,2},{3,19},{19,3},{4,20},{20... | collective-permute-start | bytes 147464 | tf_op jit(solution)/shard_map/ppermute | solution.py:187
  29.9 2.1 %collective-permute-done.8.refs_1_ = bf16[8,6144]{1,0:T(8,128)(2,1)S(1)} collective-permute-done((bf16[8,6144]{1,0:T(8,128)(2,1)S(1)}, bf16[8,6144]{1,0:T(8,128)(2,1)S(1)}, u32[]{:S(2)}, u32[]{:S(2)}) %collective-permute-start.8) | collective-permute-done | bytes 98336 | tf_op jit(solution)/shard_map/ppermute | solution.py:187
  32.0 0.8 %collective-permute-start.12 = (bf16[4,6144]{1,0:T(4,128)(2,1)S(1)}, bf16[4,6144]{1,0:T(4,128)(2,1)S(1)}, u32[]{:S(2)}, u32[]{:S(2)}) collective-permute-start(bf16[4,6144]{1,0:T(4,128)(2,1)S(1)} %get-tuple-element.33), channel_id=1, source_target_pairs={{0,4},{2,6},{4,0},{6,2},{8,12},{10,14},{12,8},{14,10},{1,5},{3,7},... | collective-permute-start | bytes 147464 | tf_op jit(solution)/shard_map/ppermute | solution.py:187
  32.8 0.6 %collective-permute-done.9.refs_1_ = bf16[8,6144]{1,0:T(8,128)(2,1)S(1)} collective-permute-done((bf16[8,6144]{1,0:T(8,128)(2,1)S(1)}, bf16[8,6144]{1,0:T(8,128)(2,1)S(1)}, u32[]{:S(2)}, u32[]{:S(2)}) %collective-permute-start.9) | collective-permute-done | bytes 98336 | tf_op jit(solution)/shard_map/ppermute | solution.py:187
  33.4 2.0 %collective-permute-start.10 = (bf16[4,6144]{1,0:T(4,128)(2,1)S(1)}, bf16[4,6144]{1,0:T(4,128)(2,1)S(1)}, u32[]{:S(2)}, u32[]{:S(2)}) collective-permute-start(bf16[4,6144]{1,0:T(4,128)(2,1)S(1)} %get-tuple-element.31), channel_id=1, source_target_pairs={{0,8},{2,10},{4,12},{6,14},{8,0},{10,2},{12,4},{14,6},{1,9},{3,11}... | collective-permute-start | bytes 147464 | tf_op jit(solution)/shard_map/ppermute | solution.py:187
  35.3 1.2 %collective-permute-start.11 = (bf16[4,6144]{1,0:T(4,128)(2,1)S(1)}, bf16[4,6144]{1,0:T(4,128)(2,1)S(1)}, u32[]{:S(2)}, u32[]{:S(2)}) collective-permute-start(bf16[4,6144]{1,0:T(4,128)(2,1)S(1)} %get-tuple-element.32), channel_id=1, source_target_pairs={{0,12},{2,14},{4,8},{6,10},{8,4},{10,6},{12,0},{14,2},{1,13},{3,15... | collective-permute-start | bytes 147464 | tf_op jit(solution)/shard_map/ppermute | solution.py:187
  36.6 0.5 %collective-permute-done.14.refs_5_ = bf16[192,128]{1,0:T(8,128)(2,1)S(1)} collective-permute-done((bf16[192,128]{1,0:T(8,128)(2,1)S(1)}, bf16[192,128]{1,0:T(8,128)(2,1)S(1)}, u32[]{:S(2)}, u32[]{:S(2)}) %collective-permute-start.14) | collective-permute-done | bytes 49184 | tf_op jit(solution)/shard_map/ppermute | solution.py:187
  37.1 2.9 %shard_map.112 = (f32[3072,128]{1,0:T(8,128)}, f32[3072,128]{1,0:T(8,128)}, f32[128,3072]{1,0:T(8,128)}) custom-call(bf16[64,6144]{1,0:T(8,128)(2,1)S(1)} %bitcast.9, bf16[64,3072]{1,0:T(8,128)(2,1)S(1)} %get-tuple-element.34.refs_1_, bf16[192,128]{1,0:T(8,128)(2,1)S(1)} %get-tuple-element.35.refs_2_, ...), custom_call_target="tpu_custom_call" | custom-call | flops 301989888 | tf_op jit(solution)/shard_map/pallas_call | solution.py:26
  40.0 1.2 %collective-permute-done.11.refs_2_ = bf16[4,6144]{1,0:T(4,128)(2,1)S(1)} collective-permute-done((bf16[4,6144]{1,0:T(4,128)(2,1)S(1)}, bf16[4,6144]{1,0:T(4,128)(2,1)S(1)}, u32[]{:S(2)}, u32[]{:S(2)}) %collective-permute-start.11) | collective-permute-done | bytes 49184 | tf_op jit(solution)/shard_map/ppermute | solution.py:187
  41.2 0.7 %shard_map.111 = bf16[4,6144]{1,0:T(4,128)(2,1)} custom-call(f32[4,6144]{1,0:T(4,128)S(1)} %get-tuple-element.28.refs_0_, bf16[4,6144]{1,0:T(4,128)(2,1)S(1)} %collective-permute-done.10.refs_1_, bf16[4,6144]{1,0:T(4,128)(2,1)S(1)} %collective-permute-done.11.refs_2_, bf16[4,6144]{1,0:T(4,128)(2,1)S(1)} %collective-permute-done.12.refs_3_), custom_call_target="tpu_custom_call" | custom-call | tf_op jit(solution)/shard_map/pallas_call | solution.py:26
  (23 shorter events, 0.2 us)
Async XLA Ops:
  0.6 8.0 %copy-start = (bf16[1,1,64,6144]{3,2,1,0:T(8,128)(2,1)S(1)}, bf16[1,1,64,6144]{3,2,1,0:T(8,128)(2,1)}, u32[]{:S(2)}) copy-start(bf16[1,1,64,6144]{3,2,1,0:T(8,128)(2,1)} %param.10) | copy-start | bytes 2359300
  0.6 0.9 %copy-start.4 = (bf16[4,6144]{1,0:T(4,128)(2,1)S(1)}, bf16[4,6144]{1,0:T(4,128)(2,1)}, u32[]{:S(2)}) copy-start(bf16[4,6144]{1,0:T(4,128)(2,1)} %grad_ref.1) | copy-start | bytes 147460
  1.5 0.7 %copy-start.5 = (s32[4,4]{1,0:T(4,128)S(1)}, s32[4,4]{1,0:T(4,128)}, u32[]{:S(2)}) copy-start(s32[4,4]{1,0:T(4,128)} %experts_ref.1) | copy-start | bytes 196
  2.2 0.7 %copy-start.6 = (f32[4,4]{1,0:T(4,128)S(1)}, f32[4,4]{1,0:T(4,128)}, u32[]{:S(2)}) copy-start(f32[4,4]{1,0:T(4,128)} %gates_ref.1) | copy-start | bytes 196
  3.0 5.7 %collective-permute-start = (bf16[4,6272]{1,0:T(4,128)(2,1)S(1)}, bf16[4,6272]{1,0:T(4,128)(2,1)S(1)}, u32[]{:S(2)}, u32[]{:S(2)}) collective-permute-start(bf16[4,6272]{1,0:T(4,128)(2,1)S(1)} %shard_map.102.refs_0_), channel_id=1, source_target_pairs={{0,4},{2,6},{4,0},{6,2},{8,12},{10,14},{12,8},{14,10},{1,5},{3,7},... | collective-permute-start | bytes 150536 | tf_op jit(solution)/shard_map/ppermute | solution.py:187
  6.1 6.5 %collective-permute-start.2 = (bf16[4,6272]{1,0:T(4,128)(2,1)S(1)}, bf16[4,6272]{1,0:T(4,128)(2,1)S(1)}, u32[]{:S(2)}, u32[]{:S(2)}) collective-permute-start(bf16[4,6272]{1,0:T(4,128)(2,1)S(1)} %shard_map.102.refs_0_), channel_id=1, source_target_pairs={{0,12},{2,14},{4,8},{6,10},{8,4},{10,6},{12,0},{14,2},{1,13},{3,15... | collective-permute-start | bytes 150536 | tf_op jit(solution)/shard_map/ppermute | solution.py:187
  8.5 5.5 %collective-permute-start.1 = (bf16[4,6272]{1,0:T(4,128)(2,1)S(1)}, bf16[4,6272]{1,0:T(4,128)(2,1)S(1)}, u32[]{:S(2)}, u32[]{:S(2)}) collective-permute-start(bf16[4,6272]{1,0:T(4,128)(2,1)S(1)} %shard_map.102.refs_0_), channel_id=1, source_target_pairs={{0,8},{2,10},{4,12},{6,14},{8,0},{10,2},{12,4},{14,6},{1,9},{3,11}... | collective-permute-start | bytes 150536 | tf_op jit(solution)/shard_map/ppermute | solution.py:187
  8.7 11.2 %collective-permute-start.5 = (bf16[64,3072]{1,0:T(8,128)(2,1)S(1)}, bf16[64,3072]{1,0:T(8,128)(2,1)S(1)}, u32[]{:S(2)}, u32[]{:S(2)}) collective-permute-start(bf16[64,3072]{1,0:T(8,128)(2,1)S(1)} %shard_map.104), channel_id=1, source_target_pairs={{0,16},{16,0},{1,17},{17,1},{2,18},{18,2},{3,19},{19,3},{4,20},{20... | collective-permute-start | bytes 1179656 | tf_op jit(solution)/shard_map/ppermute | solution.py:187
  14.1 6.0 %copy-start.1 = (bf16[1,6144,128]{2,1,0:T(8,128)(2,1)S(1)}, bf16[1,6144,128]{2,1,0:T(8,128)(2,1)}, u32[]{:S(2)}) copy-start(bf16[1,6144,128]{2,1,0:T(8,128)(2,1)} %param.11) | copy-start | bytes 4718596
  14.1 6.0 %copy-start.2 = (bf16[1,6144,128]{2,1,0:T(8,128)(2,1)S(1)}, bf16[1,6144,128]{2,1,0:T(8,128)(2,1)}, u32[]{:S(2)}) copy-start(bf16[1,6144,128]{2,1,0:T(8,128)(2,1)} %param.12) | copy-start | bytes 4718596
  14.1 5.8 %collective-permute-start.4 = (bf16[3,4,6272]{2,1,0:T(4,128)(2,1)S(1)}, bf16[3,4,6272]{2,1,0:T(4,128)(2,1)S(1)}, u32[]{:S(2)}, u32[]{:S(2)}) collective-permute-start(bf16[3,4,6272]{2,1,0:T(4,128)(2,1)S(1)} %shard_map.103.refs_1_), channel_id=1, source_target_pairs={{0,1},{1,0},{2,3},{3,2},{4,5},{5,4},{6,7},{7,6},{8,9},{9,8},{10,11... | collective-permute-start | bytes 451592 | tf_op jit(solution)/shard_map/ppermute | solution.py:187
  15.6 4.2 %collective-permute-start.3 = (bf16[4,6272]{1,0:T(4,128)(2,1)S(1)}, bf16[4,6272]{1,0:T(4,128)(2,1)S(1)}, u32[]{:S(2)}, u32[]{:S(2)}) collective-permute-start(bf16[4,6272]{1,0:T(4,128)(2,1)S(1)} %shard_map.102.refs_0_), channel_id=1, source_target_pairs={{0,1},{1,0},{2,3},{3,2},{4,5},{5,4},{6,7},{7,6},{8,9},{9,8},{10,11... | collective-permute-start | bytes 150536 | tf_op jit(solution)/shard_map/ppermute | solution.py:187
  20.0 1.8 %collective-permute-start.6 = (bf16[32,6272]{1,0:T(8,128)(2,1)S(1)}, bf16[32,6272]{1,0:T(8,128)(2,1)S(1)}, u32[]{:S(2)}, u32[]{:S(2)}) collective-permute-start(bf16[32,6272]{1,0:T(8,128)(2,1)S(1)} %shard_map.105.refs_0_), channel_id=1, source_target_pairs={{0,2},{2,0},{4,6},{6,4},{8,10},{10,8},{12,14},{14,12},{1,3},{3,1},... | collective-permute-start | bytes 1204232 | tf_op jit(solution)/shard_map/ppermute | solution.py:187
  20.1 1.7 %copy-start.3 = (bf16[1,128,6144]{2,1,0:T(8,128)(2,1)S(1)}, bf16[1,128,6144]{2,1,0:T(8,128)(2,1)}, u32[]{:S(2)}) copy-start(bf16[1,128,6144]{2,1,0:T(8,128)(2,1)} %param.13) | copy-start | bytes 4718596
  24.4 1.8 %collective-permute-start.7 = (bf16[32,6144]{1,0:T(8,128)(2,1)S(1)}, bf16[32,6144]{1,0:T(8,128)(2,1)S(1)}, u32[]{:S(2)}, u32[]{:S(2)}) collective-permute-start(bf16[32,6144]{1,0:T(8,128)(2,1)S(1)} %get-tuple-element.25), channel_id=1, source_target_pairs={{0,2},{2,0},{4,6},{6,4},{8,10},{10,8},{12,14},{14,12},{1,3},{3,1},... | collective-permute-start | bytes 1179656 | tf_op jit(solution)/shard_map/ppermute | solution.py:187
  24.7 12.4 %collective-permute-start.13 = (bf16[64,3072]{1,0:T(8,128)(2,1)S(1)}, bf16[64,3072]{1,0:T(8,128)(2,1)S(1)}, u32[]{:S(2)}, u32[]{:S(2)}) collective-permute-start(bf16[64,3072]{1,0:T(8,128)(2,1)S(1)} %get-tuple-element.36), channel_id=1, source_target_pairs={{0,16},{16,0},{1,17},{17,1},{2,18},{18,2},{3,19},{19,3},{4,20},{20... | collective-permute-start | bytes 1179656 | tf_op jit(solution)/shard_map/ppermute | solution.py:187
  26.3 5.7 %collective-permute-start.8 = (bf16[8,6144]{1,0:T(8,128)(2,1)S(1)}, bf16[8,6144]{1,0:T(8,128)(2,1)S(1)}, u32[]{:S(2)}, u32[]{:S(2)}) collective-permute-start(bf16[8,6144]{1,0:T(8,128)(2,1)S(1)} %get-tuple-element.27), channel_id=1, source_target_pairs={{0,1},{1,0},{2,3},{3,2},{4,5},{5,4},{6,7},{7,6},{8,9},{9,8},{10,11... | collective-permute-start | bytes 294920 | tf_op jit(solution)/shard_map/ppermute | solution.py:187
  27.9 5.5 %collective-permute-start.9 = (bf16[8,6144]{1,0:T(8,128)(2,1)S(1)}, bf16[8,6144]{1,0:T(8,128)(2,1)S(1)}, u32[]{:S(2)}, u32[]{:S(2)}) collective-permute-start(bf16[8,6144]{1,0:T(8,128)(2,1)S(1)} %get-tuple-element.30), channel_id=1, source_target_pairs={{0,1},{1,0},{2,3},{3,2},{4,5},{5,4},{6,7},{7,6},{8,9},{9,8},{10,11... | collective-permute-start | bytes 294920 | tf_op jit(solution)/shard_map/ppermute | solution.py:187
  28.4 8.7 %collective-permute-start.14 = (bf16[192,128]{1,0:T(8,128)(2,1)S(1)}, bf16[192,128]{1,0:T(8,128)(2,1)S(1)}, u32[]{:S(2)}, u32[]{:S(2)}) collective-permute-start(bf16[192,128]{1,0:T(8,128)(2,1)S(1)} %get-tuple-element.35.refs_2_), channel_id=1, source_target_pairs={{0,16},{16,0},{1,17},{17,1},{2,18},{18,2},{3,19},{19,3},{4,20},{20... | collective-permute-start | bytes 147464 | tf_op jit(solution)/shard_map/ppermute | solution.py:187
  32.0 8.0 %collective-permute-start.12 = (bf16[4,6144]{1,0:T(4,128)(2,1)S(1)}, bf16[4,6144]{1,0:T(4,128)(2,1)S(1)}, u32[]{:S(2)}, u32[]{:S(2)}) collective-permute-start(bf16[4,6144]{1,0:T(4,128)(2,1)S(1)} %get-tuple-element.33), channel_id=1, source_target_pairs={{0,4},{2,6},{4,0},{6,2},{8,12},{10,14},{12,8},{14,10},{1,5},{3,7},... | collective-permute-start | bytes 147464 | tf_op jit(solution)/shard_map/ppermute | solution.py:187
  33.4 6.7 %collective-permute-start.10 = (bf16[4,6144]{1,0:T(4,128)(2,1)S(1)}, bf16[4,6144]{1,0:T(4,128)(2,1)S(1)}, u32[]{:S(2)}, u32[]{:S(2)}) collective-permute-start(bf16[4,6144]{1,0:T(4,128)(2,1)S(1)} %get-tuple-element.31), channel_id=1, source_target_pairs={{0,8},{2,10},{4,12},{6,14},{8,0},{10,2},{12,4},{14,6},{1,9},{3,11}... | collective-permute-start | bytes 147464 | tf_op jit(solution)/shard_map/ppermute | solution.py:187
  35.3 5.9 %collective-permute-start.11 = (bf16[4,6144]{1,0:T(4,128)(2,1)S(1)}, bf16[4,6144]{1,0:T(4,128)(2,1)S(1)}, u32[]{:S(2)}, u32[]{:S(2)}) collective-permute-start(bf16[4,6144]{1,0:T(4,128)(2,1)S(1)} %get-tuple-element.32), channel_id=1, source_target_pairs={{0,12},{2,14},{4,8},{6,10},{8,4},{10,6},{12,0},{14,2},{1,13},{3,15... | collective-permute-start | bytes 147464 | tf_op jit(solution)/shard_map/ppermute | solution.py:187

commit v3 on v2

--- a/solution.py
+++ b/solution.py
@@ -21,23 +21,28 @@
     return lax.dot_general(left, right, (((0,), (0,)), ((), ())), preferred_element_type=F32)
 
 
-def local_call(kernel, out_shape, args, flops=0, scratch=(), nbytes=0):
+def local_call(kernel, out_shape, args, flops=0, scratch=(), nbytes=0, left=False):
     whole = pl.BlockSpec(memory_space=pltpu.VMEM)
+    out = pl.BlockSpec(memory_space=pl.ANY) if left else whole
     return pl.pallas_call(
         kernel,
         out_shape=out_shape,
         in_specs=[whole] * len(args),
-        out_specs=jax.tree.map(lambda _: whole, out_shape),
+        out_specs=jax.tree.map(lambda _: out, out_shape),
         scratch_shapes=list(scratch),
         compiler_params=pltpu.CompilerParams(vmem_limit_bytes=20 * 1024 * 1024),
         cost_estimate=pl.CostEstimate(flops=flops, bytes_accessed=nbytes, transcendentals=0),
     )(*args)
 
 
-def pack_kernel(capacity, groups, grad_ref, experts_ref, gates_ref, out_ref):
+def lane_kernel(out_ref):
+    out_ref[...] = lax.broadcasted_iota(jnp.int32, out_ref.shape, 1)
+
+
+def pack_kernel(capacity, groups, grad_ref, experts_ref, gates_ref, lane_ref, out_ref):
     tokens, width = grad_ref.shape
     experts, gates = experts_ref[...], gates_ref[...]
-    lane = lax.broadcasted_iota(jnp.int32, (tokens, LANES), 1)
+    lane = lane_ref[...]
     expert, section = lane % SECTION, lane // SECTION
     gate = jnp.zeros((tokens, LANES), F32)
     named = jnp.zeros((tokens, LANES), F32)
@@ -66,15 +71,12 @@
         refs[-1][i] = piece[...]
 
 
-def join_kernel(count, *refs):
-    pieces, out_ref = refs[:count], refs[-1]
+def join_kernel(order, *refs):
+    out_ref = refs[-1]
     width = out_ref.shape[1]
     for begin in range(0, width, 896):
         cols = slice(begin, min(begin + 896, width))
-        rows = []
-        for ref in pieces:
-            parts = [ref[:, cols]] if len(ref.shape) == 2 else [ref[i, :, cols] for i in range(ref.shape[0])]
-            rows += [part.astype(F32) for part in parts]
+        rows = [refs[stack][place, :, cols].astype(F32) for stack, place in order]
         out_ref[:, cols] = jnp.concatenate(rows, axis=0).astype(BF16)
 
 
@@ -86,23 +88,22 @@
         send_ref[...] = x_ref[:, pl.ds(pl.multiple_of((me ^ (i + 1)) * share, LANES), share)]
 
 
-def pre_kernel(x_ref, w_in_ref, w_lin_ref, after_ref, gate_ref, linear_ref):
-    del after_ref
+def pre_kernel(x_ref, w_in_ref, w_lin_ref, *refs):
+    gate_ref, linear_ref, both_ref = refs[-3:]
+    hidden_count = w_in_ref.shape[1]
     gate_ref[...] = jnp.dot(x_ref[...], w_in_ref[...], preferred_element_type=F32)
     linear_ref[...] = jnp.dot(x_ref[...], w_lin_ref[...], preferred_element_type=F32)
-
-
-def main_kernel(replicas, count, *refs):
-    pieces, refs = refs[:count], refs[count:]
-    gate_ref, linear_ref, w_out_ref, w_in_ref, w_lin_ref = refs[:5]
-    keep_ref, back_ref, factor_ref, own_ref, *send_refs, t_ref = refs[5:]
-    rows = pieces[0].shape[0]
-    tokens = rows * count
+    both_ref[:hidden_count] = w_in_ref[...].T
+    both_ref[hidden_count:] = w_lin_ref[...].T
+
+
+def main_kernel(replicas, near_ref, away_ref, gate_ref, linear_ref, w_out_ref, both_ref, *refs):
+    keep_ref, back_ref, factor_ref, *send_refs = refs
+    half = near_ref.shape[0]
+    tokens = 2 * half
     width = w_out_ref.shape[1]
     slots = gate_ref.shape[0]
-    for i, piece in enumerate(pieces):
-        t_ref[i * rows : (i + 1) * rows, :] = piece[...]
-    record = t_ref[:, width:].astype(F32)
+    record = jnp.concatenate([near_ref[:, width:], away_ref[:, width:]], axis=0).astype(F32)
     lane = lax.broadcasted_iota(jnp.int32, (tokens, LANES), 1)
     expert = lax.axis_index("exp")
     mine = (lane % SECTION == expert) & (lane < 3 * SECTION)
@@ -118,14 +119,15 @@
     pre_linear = to_tokens(linear_ref[...])
     sigmoid = jax.nn.sigmoid(pre_gate)
     activated = pre_gate * sigmoid
-    d_hidden = nt(t_ref[:, :width], w_out_ref[...]) * gates
+    rows = jnp.concatenate([near_ref[:, :width], away_ref[:, :width]], axis=0)
+    d_hidden = (nt(w_out_ref[...], rows) * jnp.broadcast_to(gates, (tokens, w_out_ref.shape[0])).T).T
     d_gate = (d_hidden * pre_linear * sigmoid * (1.0 + pre_gate * (1.0 - sigmoid))).astype(BF16)
     d_linear = (d_hidden * activated).astype(BF16)
-    half = tokens // 2
+    d_both = jnp.concatenate([d_gate, d_linear], axis=1)
     step = 1536 if width % 1536 == 0 else width
     for begin in range(0, width, step):
         cols = slice(begin, begin + step)
-        out = nt(d_gate, w_in_ref[cols, :]) + nt(d_linear, w_lin_ref[cols, :])
+        out = jnp.dot(d_both, both_ref[:, cols], preferred_element_type=F32)
         keep_ref[:, cols] = out[:half]
         back_ref[:, cols] = out[half:].astype(BF16)
     table = table.astype(BF16)
@@ -134,9 +136,10 @@
     factor_ref[2 * slots :] = (activated * pre_linear * gates).astype(BF16)
     share = width // replicas
     me = lax.axis_index("rep")
-    own_ref[...] = t_ref[:, pl.ds(pl.multiple_of(me * share, LANES), share)]
     for j, send_ref in enumerate(send_refs):
-        send_ref[...] = t_ref[:, pl.ds(pl.multiple_of((me ^ (j + 1)) * share, LANES), share)]
+        columns = pl.ds(pl.multiple_of((me ^ (j + 1)) * share, LANES), share)
+        send_ref[:half] = near_ref[:, columns]
+        send_ref[half:] = away_ref[:, columns]
 
 
 def sum_kernel(arrived, cuts, *refs):
@@ -160,26 +163,33 @@
     )
 
 
-def weights_kernel(replicas, slots, *refs):
-    x_ref, own_ref, factor_ref = refs[:3]
+def weights_kernel(replicas, slots, x_ref, near_ref, away_ref, factor_ref, *refs):
     others = replicas - 1
-    x_others, t_others, f_others = (refs[3 + i * others : 3 + (i + 1) * others] for i in range(3))
-    w1_ref, v1_ref, w2_ref = refs[3 + 3 * others :]
-    share = own_ref.shape[1]
-    me = lax.axis_index("rep")
+    x_others, t_others, f_others = (refs[i * others : (i + 1) * others] for i in range(3))
+    outs, held, sem = refs[3 * others : 3 * others + 3], refs[-4:-1], refs[-1]
+    share = outs[0].shape[0]
+    start = lax.axis_index("rep") * share
     factors = (factor_ref, *f_others)
     hidden = jnp.concatenate([f[2 * slots :] for f in factors], axis=0)
     d_gate = jnp.concatenate([f[:slots] for f in factors], axis=0)
     d_linear = jnp.concatenate([f[slots : 2 * slots] for f in factors], axis=0)
     step = 768 if share % 768 == 0 else share
+    copies = []
     for begin in range(0, share, step):
         cols = slice(begin, begin + step)
-        mine = x_ref[:, pl.ds(pl.multiple_of(me * share + begin, LANES), step)]
-        inputs = jnp.concatenate([mine, *(x[:, cols] for x in x_others)], axis=0)
-        tokens = jnp.concatenate([own_ref[:, cols], *(t[:, cols] for t in t_others)], axis=0)
-        w1_ref[cols, :] = tn(inputs, d_gate)
-        v1_ref[cols, :] = tn(inputs, d_linear)
-        w2_ref[:, cols] = tn(hidden, tokens)
+        columns = pl.ds(pl.multiple_of(start + begin, LANES), step)
+        inputs = jnp.concatenate([x_ref[:, columns], *(x[:, cols] for x in x_others)], axis=0)
+        held[0][cols, :] = tn(inputs, d_gate)
+        held[1][cols, :] = tn(inputs, d_linear)
+        tokens = jnp.concatenate(
+            [near_ref[:, columns], away_ref[:, columns], *(t[:, cols] for t in t_others)], axis=0
+        )
+        held[2][:, cols] = tn(hidden, tokens)
+        for i, at in enumerate(((cols, slice(None)), (cols, slice(None)), (slice(None), cols))):
+            copies.append(pltpu.make_async_copy(held[i].at[at], outs[i].at[at], sem.at[len(copies)]))
+            copies[-1].start()
+    for copy in copies:
+        copy.wait()
 
 
 def swap(values, axis, distance):
@@ -199,44 +209,50 @@
     inputs, gate_w, linear_w, down_w = expert_inputs[0, 0], w_in[0], w_lin[0], w_out[0]
     weight_flops = 2 * tokens * width * hidden_count
 
+    lanes = local_call(lane_kernel, shape((tokens_here, LANES), jnp.int32), (), flops=100 * weight_flops)
     own = local_call(
         functools.partial(pack_kernel, capacity, groups),
         shape((tokens_here, width + LANES), BF16),
-        (out_grad, experts, gates),
+        (out_grad, experts, gates, lanes),
         flops=100 * weight_flops,
     )
     across = range(1, column_groups)
-    far = [swap(own, "exp", k) for k in range(groups - 2, 0, -2)][::-1]
-    beside = [swap(own, "ffn", j) for j in across]
-    stack = local_call(stack_kernel, shape((len(far), *own.shape), BF16), tuple(far), flops=50 * weight_flops)
-    pieces = [own, stack]
-    for j, piece in zip(across, beside):
-        pieces += [piece, swap(stack, "ffn", j)]
+    steps = range(0, groups, 2)
+    column = [own] + [swap(own, "exp", k) for k in steps[:0:-1]][::-1]
+    half = len(column) // 2
+    stacks = [
+        local_call(stack_kernel, shape((half, *own.shape), BF16), tuple(part), flops=50 * weight_flops)
+        for part in (column[:half], column[half:])
+    ]
+    pieces = list(stacks)
+    for j in across:
+        pieces += [swap(stack, "ffn", j) for stack in stacks]
+    steps = [0, groups - 2, *range(2, groups - 2, 2)]
+    order = [(2 * j + k // 2 // half, k // 2 % half) for j in range(column_groups) for k in steps]
     x_sends = local_call(
-        share_kernel, [shape((slots, share), BF16)] * (replicas - 1), (inputs, far[0])
+        share_kernel, [shape((slots, share), BF16)] * (replicas - 1), (inputs, own)
     )
     x_others = [swap(x, "rep", i + 1) for i, x in enumerate(x_sends)]
+    pre_gate, pre_linear, both = local_call(
+        pre_kernel,
+        [shape((slots, hidden_count), F32)] * 2 + [shape((2 * hidden_count, width), BF16)],
+        (inputs, gate_w, linear_w, stacks[0]),
+        flops=2 * weight_flops,
+    )
     near_rows = local_call(
-        functools.partial(join_kernel, len(pieces)),
+        functools.partial(join_kernel, order),
         shape((tokens // 2, width + LANES), BF16),
-        (*pieces, *x_others),
+        (*pieces, *x_others, pre_gate),
     )
     parts = (near_rows, swap(near_rows, "exp", 1))
 
-    pre_gate, pre_linear = local_call(
-        pre_kernel,
-        [shape((slots, hidden_count), F32)] * 2,
-        (inputs, gate_w, linear_w, far[0]),
-        flops=2 * weight_flops,
-    )
-    keep, send, factors, t_own, *t_sends = local_call(
-        functools.partial(main_kernel, replicas, len(parts)),
+    keep, send, factors, *t_sends = local_call(
+        functools.partial(main_kernel, replicas),
         [shape((tokens // 2, width), F32), shape((tokens // 2, width), BF16)]
-        + [shape((2 * slots + tokens, hidden_count), BF16), shape((tokens, share), BF16)]
+        + [shape((2 * slots + tokens, hidden_count), BF16)]
         + [shape((tokens, share), BF16)] * (replicas - 1),
-        (*parts, pre_gate, pre_linear, down_w, gate_w, linear_w),
+        (*parts, pre_gate, pre_linear, down_w, both),
         flops=3 * weight_flops,
-        scratch=[pltpu.VMEM((tokens, width + LANES), BF16)],
     )
     back = swap(send, "exp", 1)
     t_others = [swap(t, "rep", j + 1) for j, t in enumerate(t_sends)]
@@ -253,13 +269,16 @@
     near_backs = [swap(s, "ffn", j + 1) for j, s in enumerate(near_sends)]
     away_sends = summed(away, away_backs, cuts, [BF16] * len(cuts))
     keep, *near_sends = summed(near, near_backs, cuts, [F32] + [BF16] * (len(cuts) - 1))
-    backs = [swap(s, "exp", 2 * (j + len(cuts))) for j, s in enumerate(away_sends)]
-    backs += [swap(s, "exp", 2 * (j + 1)) for j, s in enumerate(near_sends)]
+    backs = [swap(s, "exp", k) for k, s in zip(steps[len(cuts) :], away_sends)]
+    backs += [swap(s, "exp", k) for k, s in zip(steps[1:], near_sends)]
+    grads = [(share, hidden_count)] * 2 + [(hidden_count, share)]
     grad_w1, grad_v1, grad_w2 = local_call(
         functools.partial(weights_kernel, replicas, slots),
-        [shape((share, hidden_count), F32)] * 2 + [shape((hidden_count, share), F32)],
-        (inputs, t_own, factors, *x_others, *t_others, *f_others),
+        [shape(grad, F32) for grad in grads],
+        (inputs, *parts, factors, *x_others, *t_others, *f_others),
         flops=3 * weight_flops,
+        scratch=[pltpu.VMEM(grad, F32) for grad in grads] + [pltpu.SemaphoreType.DMA((12,))],
+        left=True,
     )
     (grad_input,) = summed(keep, backs, [(0, tokens_here)], [BF16])
     return grad_input, grad_w1[None], grad_v1[None], grad_w2[None]

time: 42.1 us -> 38.4 us (0.912)
  waiting for transfers between devices: 12.9 us -> 9.53 us
  starting transfers between devices: 18.8 us -> 20.3 us
  local copies, waits for them, and re-layouts: 2.24 us -> 0.82 us
  Pallas kernels: 7.2 us -> 6.74 us
    ppermute x15, waiting for transfers between devices: 12.9 us -> 9.53 us  [swap(): return lax.ppermute(values, axis, [(i, i ^ distance) for i in range(size)])]
    ppermute x15, starting transfers between devices: 18.8 us -> 20.3 us  [swap(): return lax.ppermute(values, axis, [(i, i ^ distance) for i in range(size)])]
    unnamed x14, local copies, waits for them, and re-layouts: 2.24 us -> 0.82 us
    pallas_call x11 -> x13, Pallas kernels: 7.2 us -> 6.74 us  [local_call(): pl.pallas_call(kernel, out_shape=out_shape, in_specs=[whole] * len(args),...]
  transfers between devices with their start and end apart: 15 -> 15, of which waited for: 8 -> 9; matrix products, arithmetic and copies ran while one was open for 0% -> 0% of each run, Pallas kernels for 9% -> 10%
where the time goes in v3:
time: 38.4 us; the launch traced here: 38.2 us
  starting transfers between devices  20.3 us (53%)
  waiting for transfers between devices  9.53 us (25%)
  Pallas kernels  6.74 us (18%)
  local copies, waits for them, and re-layouts  0.82 us (2%)
  between operations  0.77 us (2%)
    ppermute x15, starting transfers between devices, swap(): return lax.ppermute(values, axis, [(i, i ^ distance) for i in range(size)])  20.3 us
    ppermute x15, waiting for transfers between devices, swap(): return lax.ppermute(values, axis, [(i, i ^ distance) for i in range(size)])  9.53 us
    pallas_call x13, Pallas kernels, local_call(): pl.pallas_call(kernel, out_shape=out_shape, in_specs=[whole] * len(args),...  6.74 us
    unnamed x14, local copies, waits for them, and re-layouts  0.82 us
  transfers between devices with their start and end apart: 15, of which 9 were waited for; matrix products, arithmetic and copies ran while one was open for 0% of the time, Pallas kernels for 10%

profile of v3, /device:TPU:0, one launch (start us, length us, event | category | flops | bytes accessed | tf_op | source)
XLA Modules:
  0.0 38.2 jit_solution(6281775622321811326)
XLA Ops:
  0.7 0.6 %copy-done.6 = f32[4,4]{1,0:T(4,128)S(1)} copy-done((f32[4,4]{1,0:T(4,128)S(1)}, f32[4,4]{1,0:T(4,128)}, u32[]{:S(2)}) %copy-start.6) | copy-done | bytes 88
  1.3 0.1 copy-done.4
  1.5 0.1 shard_map.103.refs_0_.after_ref
  1.6 3.1 %collective-permute-start = (bf16[4,6272]{1,0:T(4,128)(2,1)S(1)}, bf16[4,6272]{1,0:T(4,128)(2,1)S(1)}, u32[]{:S(2)}, u32[]{:S(2)}) collective-permute-start(bf16[4,6272]{1,0:T(4,128)(2,1)S(1)} %shard_map.103.refs_0_.after_ref), channel_id=1, source_target_pairs={{0,4},{2,6},{4,0},{6,2},{8,12},{10,14},{12,8},{14,10},{1,5},{3,7},... | collective-permute-start | bytes 150536 | tf_op jit(solution)/shard_map/ppermute | solution.py:197
  4.6 2.5 %collective-permute-start.2 = (bf16[4,6272]{1,0:T(4,128)(2,1)S(1)}, bf16[4,6272]{1,0:T(4,128)(2,1)S(1)}, u32[]{:S(2)}, u32[]{:S(2)}) collective-permute-start(bf16[4,6272]{1,0:T(4,128)(2,1)S(1)} %shard_map.103.refs_0_.after_ref), channel_id=1, source_target_pairs={{0,12},{2,14},{4,8},{6,10},{8,4},{10,6},{12,0},{14,2},{1,13},{3,15... | collective-permute-start | bytes 150536 | tf_op jit(solution)/shard_map/ppermute | solution.py:197
  7.1 0.1 collective-permute-start.1
  7.3 1.6 %collective-permute-start.5 = (bf16[64,3072]{1,0:T(8,128)(2,1)S(1)}, bf16[64,3072]{1,0:T(8,128)(2,1)S(1)}, u32[]{:S(2)}, u32[]{:S(2)}) collective-permute-start(bf16[64,3072]{1,0:T(8,128)(2,1)S(1)} %shard_map.106), channel_id=1, source_target_pairs={{0,16},{16,0},{1,17},{17,1},{2,18},{18,2},{3,19},{19,3},{4,20},{20... | collective-permute-start | bytes 1179656 | tf_op jit(solution)/shard_map/ppermute | solution.py:197
  8.9 1.6 %collective-permute-start.3 = (bf16[2,4,6272]{2,1,0:T(4,128)(2,1)S(1)}, bf16[2,4,6272]{2,1,0:T(4,128)(2,1)S(1)}, u32[]{:S(2)}, u32[]{:S(2)}) collective-permute-start(bf16[2,4,6272]{2,1,0:T(4,128)(2,1)S(1)} %shard_map.104.refs_0_), channel_id=1, source_target_pairs={{0,1},{1,0},{2,3},{3,2},{4,5},{5,4},{6,7},{7,6},{8,9},{9,8},{10,11... | collective-permute-start | bytes 301064 | tf_op jit(solution)/shard_map/ppermute | solution.py:197
  10.5 0.7 %collective-permute-done.2.refs_1_ = bf16[4,6272]{1,0:T(4,128)(2,1)S(1)} collective-permute-done((bf16[4,6272]{1,0:T(4,128)(2,1)S(1)}, bf16[4,6272]{1,0:T(4,128)(2,1)S(1)}, u32[]{:S(2)}, u32[]{:S(2)}) %collective-permute-start.2) | collective-permute-done | bytes 50208 | tf_op jit(solution)/shard_map/ppermute | solution.py:197
  11.2 1.5 %collective-permute-done.1.refs_0_ = bf16[4,6272]{1,0:T(4,128)(2,1)S(1)} collective-permute-done((bf16[4,6272]{1,0:T(4,128)(2,1)S(1)}, bf16[4,6272]{1,0:T(4,128)(2,1)S(1)}, u32[]{:S(2)}, u32[]{:S(2)}) %collective-permute-start.1) | collective-permute-done | bytes 50208 | tf_op jit(solution)/shard_map/ppermute | solution.py:197
  12.7 1.6 %collective-permute-start.4 = (bf16[2,4,6272]{2,1,0:T(4,128)(2,1)S(1)}, bf16[2,4,6272]{2,1,0:T(4,128)(2,1)S(1)}, u32[]{:S(2)}, u32[]{:S(2)}) collective-permute-start(bf16[2,4,6272]{2,1,0:T(4,128)(2,1)S(1)} %shard_map.105.refs_1_), channel_id=1, source_target_pairs={{0,1},{1,0},{2,3},{3,2},{4,5},{5,4},{6,7},{7,6},{8,9},{9,8},{10,11... | collective-permute-start | bytes 301064 | tf_op jit(solution)/shard_map/ppermute | solution.py:197
  14.2 1.0 %shard_map.107 = (f32[64,128]{1,0:T(8,128)S(1)}, f32[64,128]{1,0:T(8,128)S(1)}, bf16[256,6144]{1,0:T(8,128)(2,1)S(1)}) custom-call(bf16[64,6144]{1,0:T(8,128)(2,1)S(1)} %bitcast.8, bf16[6144,128]{1,0:T(8,128)(2,1)S(1)} %bitcast.10, bf16[6144,128]{1,0:T(8,128)(2,1)S(1)} %bitcast.11, bf16[2,4,6272]{2,1,0:T(4,128)(2,1)S(1)} %shard_map.104.refs_0_), custom_call_target="tpu_custom_call" | custom-call | flops 201326592 | tf_op jit(solution)/shard_map/pallas_call | solution.py:27
  15.2 2.1 %collective-permute-done.4.refs_3_ = bf16[2,4,6272]{2,1,0:T(4,128)(2,1)S(1)} collective-permute-done((bf16[2,4,6272]{2,1,0:T(4,128)(2,1)S(1)}, bf16[2,4,6272]{2,1,0:T(4,128)(2,1)S(1)}, u32[]{:S(2)}, u32[]{:S(2)}) %collective-permute-start.4) | collective-permute-done | bytes 100384 | tf_op jit(solution)/shard_map/ppermute | solution.py:197
  17.4 0.3 collective-permute-done.5.refs_4_.refs_0_
  17.6 0.1 shard_map.108.near_ref
  17.7 0.1 collective-permute-start.6
  17.8 1.7 %collective-permute-done.6.away_ref = bf16[32,6272]{1,0:T(8,128)(2,1)S(1)} collective-permute-done((bf16[32,6272]{1,0:T(8,128)(2,1)S(1)}, bf16[32,6272]{1,0:T(8,128)(2,1)S(1)}, u32[]{:S(2)}, u32[]{:S(2)}) %collective-permute-start.6) | collective-permute-done | bytes 401440 | tf_op jit(solution)/shard_map/ppermute | solution.py:197
  19.5 2.1 %shard_map.109 = (f32[32,6144]{1,0:T(8,128)S(1)}, bf16[32,6144]{1,0:T(8,128)(2,1)S(1)}, bf16[192,128]{1,0:T(8,128)(2,1)S(1)}, bf16[64,3072]{1,0:T(8,128)(2,1)S(1)}) custom-call(bf16[32,6272]{1,0:T(8,128)(2,1)S(1)} %shard_map.108.near_ref, bf16[32,6272]{1,0:T(8,128)(2,1)S(1)} %collective-permute-done.6.away_ref, ...), custom_call_target="tpu_custom_call" | custom-call | flops 301989888 | tf_op jit(solution)/shard_map/pallas_call | solution.py:27
  21.7 0.2 collective-permute-start.7
  21.9 1.5 %collective-permute-start.13 = (bf16[64,3072]{1,0:T(8,128)(2,1)S(1)}, bf16[64,3072]{1,0:T(8,128)(2,1)S(1)}, u32[]{:S(2)}, u32[]{:S(2)}) collective-permute-start(bf16[64,3072]{1,0:T(8,128)(2,1)S(1)} %get-tuple-element.36), channel_id=1, source_target_pairs={{0,16},{16,0},{1,17},{17,1},{2,18},{18,2},{3,19},{19,3},{4,20},{20... | collective-permute-start | bytes 1179656 | tf_op jit(solution)/shard_map/ppermute | solution.py:197
  23.5 0.1 shard_map.110
  23.6 1.6 %collective-permute-start.8 = (bf16[8,6144]{1,0:T(8,128)(2,1)S(1)}, bf16[8,6144]{1,0:T(8,128)(2,1)S(1)}, u32[]{:S(2)}, u32[]{:S(2)}) collective-permute-start(bf16[8,6144]{1,0:T(8,128)(2,1)S(1)} %get-tuple-element.28), channel_id=1, source_target_pairs={{0,1},{1,0},{2,3},{3,2},{4,5},{5,4},{6,7},{7,6},{8,9},{9,8},{10,11... | collective-permute-start | bytes 294920 | tf_op jit(solution)/shard_map/ppermute | solution.py:197
  25.1 0.5 %collective-permute-start.9 = (bf16[8,6144]{1,0:T(8,128)(2,1)S(1)}, bf16[8,6144]{1,0:T(8,128)(2,1)S(1)}, u32[]{:S(2)}, u32[]{:S(2)}) collective-permute-start(bf16[8,6144]{1,0:T(8,128)(2,1)S(1)} %get-tuple-element.31), channel_id=1, source_target_pairs={{0,1},{1,0},{2,3},{3,2},{4,5},{5,4},{6,7},{7,6},{8,9},{9,8},{10,11... | collective-permute-start | bytes 294920 | tf_op jit(solution)/shard_map/ppermute | solution.py:197
  25.6 1.5 %collective-permute-start.14 = (bf16[192,128]{1,0:T(8,128)(2,1)S(1)}, bf16[192,128]{1,0:T(8,128)(2,1)S(1)}, u32[]{:S(2)}, u32[]{:S(2)}) collective-permute-start(bf16[192,128]{1,0:T(8,128)(2,1)S(1)} %get-tuple-element.35.factor_ref), channel_id=1, source_target_pairs={{0,16},{16,0},{1,17},{17,1},{2,18},{18,2},{3,19},{19,3},{4,20},{20... | collective-permute-start | bytes 147464 | tf_op jit(solution)/shard_map/ppermute | solution.py:197
  27.2 2.1 %collective-permute-done.8.refs_1_ = bf16[8,6144]{1,0:T(8,128)(2,1)S(1)} collective-permute-done((bf16[8,6144]{1,0:T(8,128)(2,1)S(1)}, bf16[8,6144]{1,0:T(8,128)(2,1)S(1)}, u32[]{:S(2)}, u32[]{:S(2)}) %collective-permute-start.8) | collective-permute-done | bytes 98336 | tf_op jit(solution)/shard_map/ppermute | solution.py:197
  29.3 2.7 %collective-permute-start.12 = (bf16[4,6144]{1,0:T(4,128)(2,1)S(1)}, bf16[4,6144]{1,0:T(4,128)(2,1)S(1)}, u32[]{:S(2)}, u32[]{:S(2)}) collective-permute-start(bf16[4,6144]{1,0:T(4,128)(2,1)S(1)} %get-tuple-element.34), channel_id=1, source_target_pairs={{0,12},{2,14},{4,8},{6,10},{8,4},{10,6},{12,0},{14,2},{1,13},{3,15... | collective-permute-start | bytes 147464 | tf_op jit(solution)/shard_map/ppermute | solution.py:197
  32.0 0.5 %collective-permute-start.10 = (bf16[4,6144]{1,0:T(4,128)(2,1)S(1)}, bf16[4,6144]{1,0:T(4,128)(2,1)S(1)}, u32[]{:S(2)}, u32[]{:S(2)}) collective-permute-start(bf16[4,6144]{1,0:T(4,128)(2,1)S(1)} %get-tuple-element.32), channel_id=1, source_target_pairs={{0,4},{2,6},{4,0},{6,2},{8,12},{10,14},{12,8},{14,10},{1,5},{3,7},... | collective-permute-start | bytes 147464 | tf_op jit(solution)/shard_map/ppermute | solution.py:197
  32.5 1.3 %collective-permute-start.11 = (bf16[4,6144]{1,0:T(4,128)(2,1)S(1)}, bf16[4,6144]{1,0:T(4,128)(2,1)S(1)}, u32[]{:S(2)}, u32[]{:S(2)}) collective-permute-start(bf16[4,6144]{1,0:T(4,128)(2,1)S(1)} %get-tuple-element.33), channel_id=1, source_target_pairs={{0,8},{2,10},{4,12},{6,14},{8,0},{10,2},{12,4},{14,6},{1,9},{3,11}... | collective-permute-start | bytes 147464 | tf_op jit(solution)/shard_map/ppermute | solution.py:197
  33.9 0.5 %collective-permute-done.14.refs_2_ = bf16[192,128]{1,0:T(8,128)(2,1)S(1)} collective-permute-done((bf16[192,128]{1,0:T(8,128)(2,1)S(1)}, bf16[192,128]{1,0:T(8,128)(2,1)S(1)}, u32[]{:S(2)}, u32[]{:S(2)}) %collective-permute-start.14) | collective-permute-done | bytes 49184 | tf_op jit(solution)/shard_map/ppermute | solution.py:197
  34.3 2.6 %shard_map.114 = (f32[3072,128]{1,0:T(8,128)}, f32[3072,128]{1,0:T(8,128)}, f32[128,3072]{1,0:T(8,128)}) custom-call(bf16[64,6144]{1,0:T(8,128)(2,1)S(1)} %bitcast.9, bf16[32,6272]{1,0:T(8,128)(2,1)S(1)} %shard_map.108.near_ref, bf16[32,6272]{1,0:T(8,128)(2,1)S(1)} %collective-permute-done.6.away_ref, bf16[192,128]{1,0:T(8,128)(2,1)S(1)} %get-tuple-element.35.factor_ref, ...), custom_call_target="tpu_custom_call" | custom-call | flops 301989888 | tf_op jit(solution)/shard_map/pallas_call | solution.py:27
  36.9 0.6 %collective-permute-done.11.refs_2_ = bf16[4,6144]{1,0:T(4,128)(2,1)S(1)} collective-permute-done((bf16[4,6144]{1,0:T(4,128)(2,1)S(1)}, bf16[4,6144]{1,0:T(4,128)(2,1)S(1)}, u32[]{:S(2)}, u32[]{:S(2)}) %collective-permute-start.11) | collective-permute-done | bytes 49184 | tf_op jit(solution)/shard_map/ppermute | solution.py:197
  37.5 0.7 %shard_map.113 = bf16[4,6144]{1,0:T(4,128)(2,1)} custom-call(f32[4,6144]{1,0:T(4,128)S(1)} %get-tuple-element.29.refs_0_, bf16[4,6144]{1,0:T(4,128)(2,1)S(1)} %collective-permute-done.10.refs_1_, bf16[4,6144]{1,0:T(4,128)(2,1)S(1)} %collective-permute-done.11.refs_2_, bf16[4,6144]{1,0:T(4,128)(2,1)S(1)} %collective-permute-done.12.refs_3_), custom_call_target="tpu_custom_call" | custom-call | tf_op jit(solution)/shard_map/pallas_call | solution.py:27
  (25 shorter events, 0.2 us)
Async XLA Ops:
  0.6 0.7 %copy-start.6 = (f32[4,4]{1,0:T(4,128)S(1)}, f32[4,4]{1,0:T(4,128)}, u32[]{:S(2)}) copy-start(f32[4,4]{1,0:T(4,128)} %gates_ref.1) | copy-start | bytes 196
  0.6 0.7 %copy-start.5 = (s32[4,4]{1,0:T(4,128)S(1)}, s32[4,4]{1,0:T(4,128)}, u32[]{:S(2)}) copy-start(s32[4,4]{1,0:T(4,128)} %experts_ref.1) | copy-start | bytes 196
  0.7 0.8 %copy-start.4 = (bf16[4,6144]{1,0:T(4,128)(2,1)S(1)}, bf16[4,6144]{1,0:T(4,128)(2,1)}, u32[]{:S(2)}) copy-start(bf16[4,6144]{1,0:T(4,128)(2,1)} %grad_ref.1) | copy-start | bytes 147460
  1.5 5.8 %copy-start = (bf16[1,1,64,6144]{3,2,1,0:T(8,128)(2,1)S(1)}, bf16[1,1,64,6144]{3,2,1,0:T(8,128)(2,1)}, u32[]{:S(2)}) copy-start(bf16[1,1,64,6144]{3,2,1,0:T(8,128)(2,1)} %param.10) | copy-start | bytes 2359300
  1.6 7.3 %collective-permute-start = (bf16[4,6272]{1,0:T(4,128)(2,1)S(1)}, bf16[4,6272]{1,0:T(4,128)(2,1)S(1)}, u32[]{:S(2)}, u32[]{:S(2)}) collective-permute-start(bf16[4,6272]{1,0:T(4,128)(2,1)S(1)} %shard_map.103.refs_0_.after_ref), channel_id=1, source_target_pairs={{0,4},{2,6},{4,0},{6,2},{8,12},{10,14},{12,8},{14,10},{1,5},{3,7},... | collective-permute-start | bytes 150536 | tf_op jit(solution)/shard_map/ppermute | solution.py:197
  4.6 6.5 %collective-permute-start.2 = (bf16[4,6272]{1,0:T(4,128)(2,1)S(1)}, bf16[4,6272]{1,0:T(4,128)(2,1)S(1)}, u32[]{:S(2)}, u32[]{:S(2)}) collective-permute-start(bf16[4,6272]{1,0:T(4,128)(2,1)S(1)} %shard_map.103.refs_0_.after_ref), channel_id=1, source_target_pairs={{0,12},{2,14},{4,8},{6,10},{8,4},{10,6},{12,0},{14,2},{1,13},{3,15... | collective-permute-start | bytes 150536 | tf_op jit(solution)/shard_map/ppermute | solution.py:197
  7.1 5.5 %collective-permute-start.1 = (bf16[4,6272]{1,0:T(4,128)(2,1)S(1)}, bf16[4,6272]{1,0:T(4,128)(2,1)S(1)}, u32[]{:S(2)}, u32[]{:S(2)}) collective-permute-start(bf16[4,6272]{1,0:T(4,128)(2,1)S(1)} %shard_map.103.refs_0_.after_ref), channel_id=1, source_target_pairs={{0,8},{2,10},{4,12},{6,14},{8,0},{10,2},{12,4},{14,6},{1,9},{3,11}... | collective-permute-start | bytes 150536 | tf_op jit(solution)/shard_map/ppermute | solution.py:197
  7.3 10.4 %collective-permute-start.5 = (bf16[64,3072]{1,0:T(8,128)(2,1)S(1)}, bf16[64,3072]{1,0:T(8,128)(2,1)S(1)}, u32[]{:S(2)}, u32[]{:S(2)}) collective-permute-start(bf16[64,3072]{1,0:T(8,128)(2,1)S(1)} %shard_map.106), channel_id=1, source_target_pairs={{0,16},{16,0},{1,17},{17,1},{2,18},{18,2},{3,19},{19,3},{4,20},{20... | collective-permute-start | bytes 1179656 | tf_op jit(solution)/shard_map/ppermute | solution.py:197
  8.9 5.4 %copy-start.1 = (bf16[1,6144,128]{2,1,0:T(8,128)(2,1)S(1)}, bf16[1,6144,128]{2,1,0:T(8,128)(2,1)}, u32[]{:S(2)}) copy-start(bf16[1,6144,128]{2,1,0:T(8,128)(2,1)} %param.11) | copy-start | bytes 4718596
  8.9 5.3 %copy-start.2 = (bf16[1,6144,128]{2,1,0:T(8,128)(2,1)S(1)}, bf16[1,6144,128]{2,1,0:T(8,128)(2,1)}, u32[]{:S(2)}) copy-start(bf16[1,6144,128]{2,1,0:T(8,128)(2,1)} %param.12) | copy-start | bytes 4718596
  8.9 6.3 %collective-permute-start.3 = (bf16[2,4,6272]{2,1,0:T(4,128)(2,1)S(1)}, bf16[2,4,6272]{2,1,0:T(4,128)(2,1)S(1)}, u32[]{:S(2)}, u32[]{:S(2)}) collective-permute-start(bf16[2,4,6272]{2,1,0:T(4,128)(2,1)S(1)} %shard_map.104.refs_0_), channel_id=1, source_target_pairs={{0,1},{1,0},{2,3},{3,2},{4,5},{5,4},{6,7},{7,6},{8,9},{9,8},{10,11... | collective-permute-start | bytes 301064 | tf_op jit(solution)/shard_map/ppermute | solution.py:197
  12.7 4.7 %collective-permute-start.4 = (bf16[2,4,6272]{2,1,0:T(4,128)(2,1)S(1)}, bf16[2,4,6272]{2,1,0:T(4,128)(2,1)S(1)}, u32[]{:S(2)}, u32[]{:S(2)}) collective-permute-start(bf16[2,4,6272]{2,1,0:T(4,128)(2,1)S(1)} %shard_map.105.refs_1_), channel_id=1, source_target_pairs={{0,1},{1,0},{2,3},{3,2},{4,5},{5,4},{6,7},{7,6},{8,9},{9,8},{10,11... | collective-permute-start | bytes 301064 | tf_op jit(solution)/shard_map/ppermute | solution.py:197
  14.2 5.3 %copy-start.3 = (bf16[1,128,6144]{2,1,0:T(8,128)(2,1)S(1)}, bf16[1,128,6144]{2,1,0:T(8,128)(2,1)}, u32[]{:S(2)}) copy-start(bf16[1,128,6144]{2,1,0:T(8,128)(2,1)} %param.13) | copy-start | bytes 4718596
  17.7 1.8 %collective-permute-start.6 = (bf16[32,6272]{1,0:T(8,128)(2,1)S(1)}, bf16[32,6272]{1,0:T(8,128)(2,1)S(1)}, u32[]{:S(2)}, u32[]{:S(2)}) collective-permute-start(bf16[32,6272]{1,0:T(8,128)(2,1)S(1)} %shard_map.108.near_ref), channel_id=1, source_target_pairs={{0,2},{2,0},{4,6},{6,4},{8,10},{10,8},{12,14},{14,12},{1,3},{3,1},... | collective-permute-start | bytes 1204232 | tf_op jit(solution)/shard_map/ppermute | solution.py:197
  21.7 1.8 %collective-permute-start.7 = (bf16[32,6144]{1,0:T(8,128)(2,1)S(1)}, bf16[32,6144]{1,0:T(8,128)(2,1)S(1)}, u32[]{:S(2)}, u32[]{:S(2)}) collective-permute-start(bf16[32,6144]{1,0:T(8,128)(2,1)S(1)} %get-tuple-element.26), channel_id=1, source_target_pairs={{0,2},{2,0},{4,6},{6,4},{8,10},{10,8},{12,14},{14,12},{1,3},{3,1},... | collective-permute-start | bytes 1179656 | tf_op jit(solution)/shard_map/ppermute | solution.py:197
  21.9 12.5 %collective-permute-start.13 = (bf16[64,3072]{1,0:T(8,128)(2,1)S(1)}, bf16[64,3072]{1,0:T(8,128)(2,1)S(1)}, u32[]{:S(2)}, u32[]{:S(2)}) collective-permute-start(bf16[64,3072]{1,0:T(8,128)(2,1)S(1)} %get-tuple-element.36), channel_id=1, source_target_pairs={{0,16},{16,0},{1,17},{17,1},{2,18},{18,2},{3,19},{19,3},{4,20},{20... | collective-permute-start | bytes 1179656 | tf_op jit(solution)/shard_map/ppermute | solution.py:197
  23.6 5.7 %collective-permute-start.8 = (bf16[8,6144]{1,0:T(8,128)(2,1)S(1)}, bf16[8,6144]{1,0:T(8,128)(2,1)S(1)}, u32[]{:S(2)}, u32[]{:S(2)}) collective-permute-start(bf16[8,6144]{1,0:T(8,128)(2,1)S(1)} %get-tuple-element.28), channel_id=1, source_target_pairs={{0,1},{1,0},{2,3},{3,2},{4,5},{5,4},{6,7},{7,6},{8,9},{9,8},{10,11... | collective-permute-start | bytes 294920 | tf_op jit(solution)/shard_map/ppermute | solution.py:197
  25.1 6.9 %collective-permute-start.9 = (bf16[8,6144]{1,0:T(8,128)(2,1)S(1)}, bf16[8,6144]{1,0:T(8,128)(2,1)S(1)}, u32[]{:S(2)}, u32[]{:S(2)}) collective-permute-start(bf16[8,6144]{1,0:T(8,128)(2,1)S(1)} %get-tuple-element.31), channel_id=1, source_target_pairs={{0,1},{1,0},{2,3},{3,2},{4,5},{5,4},{6,7},{7,6},{8,9},{9,8},{10,11... | collective-permute-start | bytes 294920 | tf_op jit(solution)/shard_map/ppermute | solution.py:197
  25.6 8.7 %collective-permute-start.14 = (bf16[192,128]{1,0:T(8,128)(2,1)S(1)}, bf16[192,128]{1,0:T(8,128)(2,1)S(1)}, u32[]{:S(2)}, u32[]{:S(2)}) collective-permute-start(bf16[192,128]{1,0:T(8,128)(2,1)S(1)} %get-tuple-element.35.factor_ref), channel_id=1, source_target_pairs={{0,16},{16,0},{1,17},{17,1},{2,18},{18,2},{3,19},{19,3},{4,20},{20... | collective-permute-start | bytes 147464 | tf_op jit(solution)/shard_map/ppermute | solution.py:197
  29.3 7.6 %collective-permute-start.12 = (bf16[4,6144]{1,0:T(4,128)(2,1)S(1)}, bf16[4,6144]{1,0:T(4,128)(2,1)S(1)}, u32[]{:S(2)}, u32[]{:S(2)}) collective-permute-start(bf16[4,6144]{1,0:T(4,128)(2,1)S(1)} %get-tuple-element.34), channel_id=1, source_target_pairs={{0,12},{2,14},{4,8},{6,10},{8,4},{10,6},{12,0},{14,2},{1,13},{3,15... | collective-permute-start | bytes 147464 | tf_op jit(solution)/shard_map/ppermute | solution.py:197
  32.0 4.9 %collective-permute-start.10 = (bf16[4,6144]{1,0:T(4,128)(2,1)S(1)}, bf16[4,6144]{1,0:T(4,128)(2,1)S(1)}, u32[]{:S(2)}, u32[]{:S(2)}) collective-permute-start(bf16[4,6144]{1,0:T(4,128)(2,1)S(1)} %get-tuple-element.32), channel_id=1, source_target_pairs={{0,4},{2,6},{4,0},{6,2},{8,12},{10,14},{12,8},{14,10},{1,5},{3,7},... | collective-permute-start | bytes 147464 | tf_op jit(solution)/shard_map/ppermute | solution.py:197
  32.5 5.0 %collective-permute-start.11 = (bf16[4,6144]{1,0:T(4,128)(2,1)S(1)}, bf16[4,6144]{1,0:T(4,128)(2,1)S(1)}, u32[]{:S(2)}, u32[]{:S(2)}) collective-permute-start(bf16[4,6144]{1,0:T(4,128)(2,1)S(1)} %get-tuple-element.33), channel_id=1, source_target_pairs={{0,8},{2,10},{4,12},{6,14},{8,0},{10,2},{12,4},{14,6},{1,9},{3,11}... | collective-permute-start | bytes 147464 | tf_op jit(solution)/shard_map/ppermute | solution.py:197

commit v4 on v3

--- a/solution.py
+++ b/solution.py
@@ -89,20 +89,24 @@
 
 
 def pre_kernel(x_ref, w_in_ref, w_lin_ref, *refs):
-    gate_ref, linear_ref, both_ref = refs[-3:]
+    parts_ref, both_ref = refs[-2:]
     hidden_count = w_in_ref.shape[1]
-    gate_ref[...] = jnp.dot(x_ref[...], w_in_ref[...], preferred_element_type=F32)
-    linear_ref[...] = jnp.dot(x_ref[...], w_lin_ref[...], preferred_element_type=F32)
+    for i, weight_ref in enumerate((w_in_ref, w_lin_ref)):
+        rest = jnp.dot(x_ref[...], weight_ref[...], preferred_element_type=F32)
+        for part in range(3):
+            rounded = rest.astype(BF16)
+            parts_ref[:, (2 * part + i) * hidden_count : (2 * part + i + 1) * hidden_count] = rounded
+            rest = rest - rounded.astype(F32)
     both_ref[:hidden_count] = w_in_ref[...].T
     both_ref[hidden_count:] = w_lin_ref[...].T
 
 
-def main_kernel(replicas, near_ref, away_ref, gate_ref, linear_ref, w_out_ref, both_ref, *refs):
+def main_kernel(replicas, near_ref, away_ref, parts_ref, w_out_ref, both_ref, *refs):
     keep_ref, back_ref, factor_ref, *send_refs = refs
     half = near_ref.shape[0]
     tokens = 2 * half
     width = w_out_ref.shape[1]
-    slots = gate_ref.shape[0]
+    slots = parts_ref.shape[0]
     record = jnp.concatenate([near_ref[:, width:], away_ref[:, width:]], axis=0).astype(F32)
     lane = lax.broadcasted_iota(jnp.int32, (tokens, LANES), 1)
     expert = lax.axis_index("exp")
@@ -110,13 +114,12 @@
     gates = jnp.sum(jnp.where(mine, record, 0.0), axis=1, keepdims=True)
     slot = jnp.sum(jnp.where(lane == 3 * SECTION + expert, record, 0.0), axis=1, keepdims=True)
     place = lax.broadcasted_iota(jnp.int32, (tokens, slots), 1) + 1
-    table = jnp.where(place == slot.astype(jnp.int32), 1.0, 0.0)
-
-    def to_tokens(values):
-        return jnp.dot(table, values, preferred_element_type=F32, precision=lax.Precision.HIGHEST)
-
-    pre_gate = to_tokens(gate_ref[...])
-    pre_linear = to_tokens(linear_ref[...])
+    table = jnp.where(place == slot.astype(jnp.int32), 1.0, 0.0).astype(BF16)
+    parts = jnp.dot(table, parts_ref[...], preferred_element_type=F32)
+    hidden_count = w_out_ref.shape[0]
+    pre_gate, pre_linear = (
+        sum(parts[:, i * hidden_count : (i + 1) * hidden_count] for i in range(first, 6, 2)) for first in (0, 1)
+    )
     sigmoid = jax.nn.sigmoid(pre_gate)
     activated = pre_gate * sigmoid
     rows = jnp.concatenate([near_ref[:, :width], away_ref[:, :width]], axis=0)
@@ -130,7 +133,6 @@
         out = jnp.dot(d_both, both_ref[:, cols], preferred_element_type=F32)
         keep_ref[:, cols] = out[:half]
         back_ref[:, cols] = out[half:].astype(BF16)
-    table = table.astype(BF16)
     factor_ref[:slots] = tn(table, d_gate).astype(BF16)
     factor_ref[slots : 2 * slots] = tn(table, d_linear).astype(BF16)
     factor_ref[2 * slots :] = (activated * pre_linear * gates).astype(BF16)
@@ -233,16 +235,16 @@
         share_kernel, [shape((slots, share), BF16)] * (replicas - 1), (inputs, own)
     )
     x_others = [swap(x, "rep", i + 1) for i, x in enumerate(x_sends)]
-    pre_gate, pre_linear, both = local_call(
+    split, both = local_call(
         pre_kernel,
-        [shape((slots, hidden_count), F32)] * 2 + [shape((2 * hidden_count, width), BF16)],
+        [shape((slots, 6 * hidden_count), BF16), shape((2 * hidden_count, width), BF16)],
         (inputs, gate_w, linear_w, stacks[0]),
         flops=2 * weight_flops,
     )
     near_rows = local_call(
         functools.partial(join_kernel, order),
         shape((tokens // 2, width + LANES), BF16),
-        (*pieces, *x_others, pre_gate),
+        (*pieces, *x_others, split),
     )
     parts = (near_rows, swap(near_rows, "exp", 1))
 
@@ -251,7 +253,7 @@
         [shape((tokens // 2, width), F32), shape((tokens // 2, width), BF16)]
         + [shape((2 * slots + tokens, hidden_count), BF16)]
         + [shape((tokens, share), BF16)] * (replicas - 1),
-        (*parts, pre_gate, pre_linear, down_w, both),
+        (*parts, split, down_w, both),
         flops=3 * weight_flops,
     )
     back = swap(send, "exp", 1)

time: 38.4 us -> 38.2 us (level)
  no operation moved by 1% of the time
where the time goes in v4:
time: 38.2 us; the launch traced here: 38 us
  starting transfers between devices  20.3 us (53%)
  waiting for transfers between devices  9.52 us (25%)
  Pallas kernels  6.58 us (17%)
  local copies, waits for them, and re-layouts  0.82 us (2%)
  between operations  0.77 us (2%)
    ppermute x15, starting transfers between devices, swap(): return lax.ppermute(values, axis, [(i, i ^ distance) for i in range(size)])  20.3 us
    ppermute x15, waiting for transfers between devices, swap(): return lax.ppermute(values, axis, [(i, i ^ distance) for i in range(size)])  9.52 us
    pallas_call x13, Pallas kernels, local_call(): pl.pallas_call(kernel, out_shape=out_shape, in_specs=[whole] * len(args),...  6.58 us
    unnamed x14, local copies, waits for them, and re-layouts  0.82 us
  transfers between devices with their start and end apart: 15, of which 9 were waited for; matrix products, arithmetic and copies ran while one was open for 0% of the time, Pallas kernels for 10%

profile of v4, /device:TPU:0, one launch (start us, length us, event | category | flops | bytes accessed | tf_op | source)
XLA Modules:
  0.0 38.0 jit_solution(7137421262771880854)
XLA Ops:
  0.7 0.6 %copy-done.6 = f32[4,4]{1,0:T(4,128)S(1)} copy-done((f32[4,4]{1,0:T(4,128)S(1)}, f32[4,4]{1,0:T(4,128)}, u32[]{:S(2)}) %copy-start.6) | copy-done | bytes 88
  1.3 0.1 copy-done.4
  1.5 0.1 shard_map.103.refs_0_.after_ref
  1.6 3.1 %collective-permute-start = (bf16[4,6272]{1,0:T(4,128)(2,1)S(1)}, bf16[4,6272]{1,0:T(4,128)(2,1)S(1)}, u32[]{:S(2)}, u32[]{:S(2)}) collective-permute-start(bf16[4,6272]{1,0:T(4,128)(2,1)S(1)} %shard_map.103.refs_0_.after_ref), channel_id=1, source_target_pairs={{0,4},{2,6},{4,0},{6,2},{8,12},{10,14},{12,8},{14,10},{1,5},{3,7},... | collective-permute-start | bytes 150536 | tf_op jit(solution)/shard_map/ppermute | solution.py:199
  4.6 2.5 %collective-permute-start.2 = (bf16[4,6272]{1,0:T(4,128)(2,1)S(1)}, bf16[4,6272]{1,0:T(4,128)(2,1)S(1)}, u32[]{:S(2)}, u32[]{:S(2)}) collective-permute-start(bf16[4,6272]{1,0:T(4,128)(2,1)S(1)} %shard_map.103.refs_0_.after_ref), channel_id=1, source_target_pairs={{0,12},{2,14},{4,8},{6,10},{8,4},{10,6},{12,0},{14,2},{1,13},{3,15... | collective-permute-start | bytes 150536 | tf_op jit(solution)/shard_map/ppermute | solution.py:199
  7.1 0.1 collective-permute-start.1
  7.3 1.6 %collective-permute-start.5 = (bf16[64,3072]{1,0:T(8,128)(2,1)S(1)}, bf16[64,3072]{1,0:T(8,128)(2,1)S(1)}, u32[]{:S(2)}, u32[]{:S(2)}) collective-permute-start(bf16[64,3072]{1,0:T(8,128)(2,1)S(1)} %shard_map.106), channel_id=1, source_target_pairs={{0,16},{16,0},{1,17},{17,1},{2,18},{18,2},{3,19},{19,3},{4,20},{20... | collective-permute-start | bytes 1179656 | tf_op jit(solution)/shard_map/ppermute | solution.py:199
  8.9 1.6 %collective-permute-start.3 = (bf16[2,4,6272]{2,1,0:T(4,128)(2,1)S(1)}, bf16[2,4,6272]{2,1,0:T(4,128)(2,1)S(1)}, u32[]{:S(2)}, u32[]{:S(2)}) collective-permute-start(bf16[2,4,6272]{2,1,0:T(4,128)(2,1)S(1)} %shard_map.104.refs_0_), channel_id=1, source_target_pairs={{0,1},{1,0},{2,3},{3,2},{4,5},{5,4},{6,7},{7,6},{8,9},{9,8},{10,11... | collective-permute-start | bytes 301064 | tf_op jit(solution)/shard_map/ppermute | solution.py:199
  10.5 0.7 %collective-permute-done.2.refs_1_ = bf16[4,6272]{1,0:T(4,128)(2,1)S(1)} collective-permute-done((bf16[4,6272]{1,0:T(4,128)(2,1)S(1)}, bf16[4,6272]{1,0:T(4,128)(2,1)S(1)}, u32[]{:S(2)}, u32[]{:S(2)}) %collective-permute-start.2) | collective-permute-done | bytes 50208 | tf_op jit(solution)/shard_map/ppermute | solution.py:199
  11.2 1.5 %collective-permute-done.1.refs_0_ = bf16[4,6272]{1,0:T(4,128)(2,1)S(1)} collective-permute-done((bf16[4,6272]{1,0:T(4,128)(2,1)S(1)}, bf16[4,6272]{1,0:T(4,128)(2,1)S(1)}, u32[]{:S(2)}, u32[]{:S(2)}) %collective-permute-start.1) | collective-permute-done | bytes 50208 | tf_op jit(solution)/shard_map/ppermute | solution.py:199
  12.7 1.6 %collective-permute-start.4 = (bf16[2,4,6272]{2,1,0:T(4,128)(2,1)S(1)}, bf16[2,4,6272]{2,1,0:T(4,128)(2,1)S(1)}, u32[]{:S(2)}, u32[]{:S(2)}) collective-permute-start(bf16[2,4,6272]{2,1,0:T(4,128)(2,1)S(1)} %shard_map.105.refs_1_), channel_id=1, source_target_pairs={{0,1},{1,0},{2,3},{3,2},{4,5},{5,4},{6,7},{7,6},{8,9},{9,8},{10,11... | collective-permute-start | bytes 301064 | tf_op jit(solution)/shard_map/ppermute | solution.py:199
  14.2 1.0 %shard_map.107 = (bf16[64,768]{1,0:T(8,128)(2,1)S(1)}, bf16[256,6144]{1,0:T(8,128)(2,1)S(1)}) custom-call(bf16[64,6144]{1,0:T(8,128)(2,1)S(1)} %bitcast.8, bf16[6144,128]{1,0:T(8,128)(2,1)S(1)} %bitcast.10, bf16[6144,128]{1,0:T(8,128)(2,1)S(1)} %bitcast.11, bf16[2,4,6272]{2,1,0:T(4,128)(2,1)S(1)} %shard_map.104.refs_0_), custom_call_target="tpu_custom_call" | custom-call | flops 201326592 | tf_op jit(solution)/shard_map/pallas_call | solution.py:27
  15.3 2.1 %collective-permute-done.4.refs_3_ = bf16[2,4,6272]{2,1,0:T(4,128)(2,1)S(1)} collective-permute-done((bf16[2,4,6272]{2,1,0:T(4,128)(2,1)S(1)}, bf16[2,4,6272]{2,1,0:T(4,128)(2,1)S(1)}, u32[]{:S(2)}, u32[]{:S(2)}) %collective-permute-start.4) | collective-permute-done | bytes 100384 | tf_op jit(solution)/shard_map/ppermute | solution.py:199
  17.4 0.3 collective-permute-done.5.refs_4_.refs_0_
  17.6 0.1 shard_map.108.near_ref
  17.7 0.1 collective-permute-start.6
  17.8 1.7 %collective-permute-done.6.away_ref = bf16[32,6272]{1,0:T(8,128)(2,1)S(1)} collective-permute-done((bf16[32,6272]{1,0:T(8,128)(2,1)S(1)}, bf16[32,6272]{1,0:T(8,128)(2,1)S(1)}, u32[]{:S(2)}, u32[]{:S(2)}) %collective-permute-start.6) | collective-permute-done | bytes 401440 | tf_op jit(solution)/shard_map/ppermute | solution.py:199
  19.5 2.0 %shard_map.109 = (f32[32,6144]{1,0:T(8,128)S(1)}, bf16[32,6144]{1,0:T(8,128)(2,1)S(1)}, bf16[192,128]{1,0:T(8,128)(2,1)S(1)}, bf16[64,3072]{1,0:T(8,128)(2,1)S(1)}) custom-call(bf16[32,6272]{1,0:T(8,128)(2,1)S(1)} %shard_map.108.near_ref, bf16[32,6272]{1,0:T(8,128)(2,1)S(1)} %collective-permute-done.6.away_ref, ...), custom_call_target="tpu_custom_call" | custom-call | flops 301989888 | tf_op jit(solution)/shard_map/pallas_call | solution.py:27
  21.5 0.2 collective-permute-start.7
  21.7 1.5 %collective-permute-start.13 = (bf16[64,3072]{1,0:T(8,128)(2,1)S(1)}, bf16[64,3072]{1,0:T(8,128)(2,1)S(1)}, u32[]{:S(2)}, u32[]{:S(2)}) collective-permute-start(bf16[64,3072]{1,0:T(8,128)(2,1)S(1)} %get-tuple-element.34), channel_id=1, source_target_pairs={{0,16},{16,0},{1,17},{17,1},{2,18},{18,2},{3,19},{19,3},{4,20},{20... | collective-permute-start | bytes 1179656 | tf_op jit(solution)/shard_map/ppermute | solution.py:199
  23.3 0.1 shard_map.110
  23.4 1.6 %collective-permute-start.8 = (bf16[8,6144]{1,0:T(8,128)(2,1)S(1)}, bf16[8,6144]{1,0:T(8,128)(2,1)S(1)}, u32[]{:S(2)}, u32[]{:S(2)}) collective-permute-start(bf16[8,6144]{1,0:T(8,128)(2,1)S(1)} %get-tuple-element.26), channel_id=1, source_target_pairs={{0,1},{1,0},{2,3},{3,2},{4,5},{5,4},{6,7},{7,6},{8,9},{9,8},{10,11... | collective-permute-start | bytes 294920 | tf_op jit(solution)/shard_map/ppermute | solution.py:199
  25.0 0.5 %collective-permute-start.9 = (bf16[8,6144]{1,0:T(8,128)(2,1)S(1)}, bf16[8,6144]{1,0:T(8,128)(2,1)S(1)}, u32[]{:S(2)}, u32[]{:S(2)}) collective-permute-start(bf16[8,6144]{1,0:T(8,128)(2,1)S(1)} %get-tuple-element.29), channel_id=1, source_target_pairs={{0,1},{1,0},{2,3},{3,2},{4,5},{5,4},{6,7},{7,6},{8,9},{9,8},{10,11... | collective-permute-start | bytes 294920 | tf_op jit(solution)/shard_map/ppermute | solution.py:199
  25.5 1.5 %collective-permute-start.14 = (bf16[192,128]{1,0:T(8,128)(2,1)S(1)}, bf16[192,128]{1,0:T(8,128)(2,1)S(1)}, u32[]{:S(2)}, u32[]{:S(2)}) collective-permute-start(bf16[192,128]{1,0:T(8,128)(2,1)S(1)} %get-tuple-element.33.factor_ref), channel_id=1, source_target_pairs={{0,16},{16,0},{1,17},{17,1},{2,18},{18,2},{3,19},{19,3},{4,20},{20... | collective-permute-start | bytes 147464 | tf_op jit(solution)/shard_map/ppermute | solution.py:199
  27.0 2.1 %collective-permute-done.8.refs_1_ = bf16[8,6144]{1,0:T(8,128)(2,1)S(1)} collective-permute-done((bf16[8,6144]{1,0:T(8,128)(2,1)S(1)}, bf16[8,6144]{1,0:T(8,128)(2,1)S(1)}, u32[]{:S(2)}, u32[]{:S(2)}) %collective-permute-start.8) | collective-permute-done | bytes 98336 | tf_op jit(solution)/shard_map/ppermute | solution.py:199
  29.1 2.7 %collective-permute-start.12 = (bf16[4,6144]{1,0:T(4,128)(2,1)S(1)}, bf16[4,6144]{1,0:T(4,128)(2,1)S(1)}, u32[]{:S(2)}, u32[]{:S(2)}) collective-permute-start(bf16[4,6144]{1,0:T(4,128)(2,1)S(1)} %get-tuple-element.32), channel_id=1, source_target_pairs={{0,12},{2,14},{4,8},{6,10},{8,4},{10,6},{12,0},{14,2},{1,13},{3,15... | collective-permute-start | bytes 147464 | tf_op jit(solution)/shard_map/ppermute | solution.py:199
  31.9 0.5 %collective-permute-start.10 = (bf16[4,6144]{1,0:T(4,128)(2,1)S(1)}, bf16[4,6144]{1,0:T(4,128)(2,1)S(1)}, u32[]{:S(2)}, u32[]{:S(2)}) collective-permute-start(bf16[4,6144]{1,0:T(4,128)(2,1)S(1)} %get-tuple-element.30), channel_id=1, source_target_pairs={{0,4},{2,6},{4,0},{6,2},{8,12},{10,14},{12,8},{14,10},{1,5},{3,7},... | collective-permute-start | bytes 147464 | tf_op jit(solution)/shard_map/ppermute | solution.py:199
  32.4 1.3 %collective-permute-start.11 = (bf16[4,6144]{1,0:T(4,128)(2,1)S(1)}, bf16[4,6144]{1,0:T(4,128)(2,1)S(1)}, u32[]{:S(2)}, u32[]{:S(2)}) collective-permute-start(bf16[4,6144]{1,0:T(4,128)(2,1)S(1)} %get-tuple-element.31), channel_id=1, source_target_pairs={{0,8},{2,10},{4,12},{6,14},{8,0},{10,2},{12,4},{14,6},{1,9},{3,11}... | collective-permute-start | bytes 147464 | tf_op jit(solution)/shard_map/ppermute | solution.py:199
  33.7 0.5 %collective-permute-done.14.refs_2_ = bf16[192,128]{1,0:T(8,128)(2,1)S(1)} collective-permute-done((bf16[192,128]{1,0:T(8,128)(2,1)S(1)}, bf16[192,128]{1,0:T(8,128)(2,1)S(1)}, u32[]{:S(2)}, u32[]{:S(2)}) %collective-permute-start.14) | collective-permute-done | bytes 49184 | tf_op jit(solution)/shard_map/ppermute | solution.py:199
  34.2 2.6 %shard_map.114 = (f32[3072,128]{1,0:T(8,128)}, f32[3072,128]{1,0:T(8,128)}, f32[128,3072]{1,0:T(8,128)}) custom-call(bf16[64,6144]{1,0:T(8,128)(2,1)S(1)} %bitcast.9, bf16[32,6272]{1,0:T(8,128)(2,1)S(1)} %shard_map.108.near_ref, bf16[32,6272]{1,0:T(8,128)(2,1)S(1)} %collective-permute-done.6.away_ref, bf16[192,128]{1,0:T(8,128)(2,1)S(1)} %get-tuple-element.33.factor_ref, ...), custom_call_target="tpu_custom_call" | custom-call | flops 301989888 | tf_op jit(solution)/shard_map/pallas_call | solution.py:27
  36.8 0.6 %collective-permute-done.11.refs_2_ = bf16[4,6144]{1,0:T(4,128)(2,1)S(1)} collective-permute-done((bf16[4,6144]{1,0:T(4,128)(2,1)S(1)}, bf16[4,6144]{1,0:T(4,128)(2,1)S(1)}, u32[]{:S(2)}, u32[]{:S(2)}) %collective-permute-start.11) | collective-permute-done | bytes 49184 | tf_op jit(solution)/shard_map/ppermute | solution.py:199
  37.4 0.7 %shard_map.113 = bf16[4,6144]{1,0:T(4,128)(2,1)} custom-call(f32[4,6144]{1,0:T(4,128)S(1)} %get-tuple-element.27.refs_0_, bf16[4,6144]{1,0:T(4,128)(2,1)S(1)} %collective-permute-done.10.refs_1_, bf16[4,6144]{1,0:T(4,128)(2,1)S(1)} %collective-permute-done.11.refs_2_, bf16[4,6144]{1,0:T(4,128)(2,1)S(1)} %collective-permute-done.12.refs_3_), custom_call_target="tpu_custom_call" | custom-call | tf_op jit(solution)/shard_map/pallas_call | solution.py:27
  (25 shorter events, 0.2 us)
Async XLA Ops:
  0.6 0.7 %copy-start.6 = (f32[4,4]{1,0:T(4,128)S(1)}, f32[4,4]{1,0:T(4,128)}, u32[]{:S(2)}) copy-start(f32[4,4]{1,0:T(4,128)} %gates_ref.1) | copy-start | bytes 196
  0.6 0.7 %copy-start.5 = (s32[4,4]{1,0:T(4,128)S(1)}, s32[4,4]{1,0:T(4,128)}, u32[]{:S(2)}) copy-start(s32[4,4]{1,0:T(4,128)} %experts_ref.1) | copy-start | bytes 196
  0.7 0.8 %copy-start.4 = (bf16[4,6144]{1,0:T(4,128)(2,1)S(1)}, bf16[4,6144]{1,0:T(4,128)(2,1)}, u32[]{:S(2)}) copy-start(bf16[4,6144]{1,0:T(4,128)(2,1)} %grad_ref.1) | copy-start | bytes 147460
  1.5 5.8 %copy-start = (bf16[1,1,64,6144]{3,2,1,0:T(8,128)(2,1)S(1)}, bf16[1,1,64,6144]{3,2,1,0:T(8,128)(2,1)}, u32[]{:S(2)}) copy-start(bf16[1,1,64,6144]{3,2,1,0:T(8,128)(2,1)} %param.10) | copy-start | bytes 2359300
  1.6 7.3 %collective-permute-start = (bf16[4,6272]{1,0:T(4,128)(2,1)S(1)}, bf16[4,6272]{1,0:T(4,128)(2,1)S(1)}, u32[]{:S(2)}, u32[]{:S(2)}) collective-permute-start(bf16[4,6272]{1,0:T(4,128)(2,1)S(1)} %shard_map.103.refs_0_.after_ref), channel_id=1, source_target_pairs={{0,4},{2,6},{4,0},{6,2},{8,12},{10,14},{12,8},{14,10},{1,5},{3,7},... | collective-permute-start | bytes 150536 | tf_op jit(solution)/shard_map/ppermute | solution.py:199
  4.6 6.5 %collective-permute-start.2 = (bf16[4,6272]{1,0:T(4,128)(2,1)S(1)}, bf16[4,6272]{1,0:T(4,128)(2,1)S(1)}, u32[]{:S(2)}, u32[]{:S(2)}) collective-permute-start(bf16[4,6272]{1,0:T(4,128)(2,1)S(1)} %shard_map.103.refs_0_.after_ref), channel_id=1, source_target_pairs={{0,12},{2,14},{4,8},{6,10},{8,4},{10,6},{12,0},{14,2},{1,13},{3,15... | collective-permute-start | bytes 150536 | tf_op jit(solution)/shard_map/ppermute | solution.py:199
  7.1 5.5 %collective-permute-start.1 = (bf16[4,6272]{1,0:T(4,128)(2,1)S(1)}, bf16[4,6272]{1,0:T(4,128)(2,1)S(1)}, u32[]{:S(2)}, u32[]{:S(2)}) collective-permute-start(bf16[4,6272]{1,0:T(4,128)(2,1)S(1)} %shard_map.103.refs_0_.after_ref), channel_id=1, source_target_pairs={{0,8},{2,10},{4,12},{6,14},{8,0},{10,2},{12,4},{14,6},{1,9},{3,11}... | collective-permute-start | bytes 150536 | tf_op jit(solution)/shard_map/ppermute | solution.py:199
  7.3 10.4 %collective-permute-start.5 = (bf16[64,3072]{1,0:T(8,128)(2,1)S(1)}, bf16[64,3072]{1,0:T(8,128)(2,1)S(1)}, u32[]{:S(2)}, u32[]{:S(2)}) collective-permute-start(bf16[64,3072]{1,0:T(8,128)(2,1)S(1)} %shard_map.106), channel_id=1, source_target_pairs={{0,16},{16,0},{1,17},{17,1},{2,18},{18,2},{3,19},{19,3},{4,20},{20... | collective-permute-start | bytes 1179656 | tf_op jit(solution)/shard_map/ppermute | solution.py:199
  8.9 5.4 %copy-start.1 = (bf16[1,6144,128]{2,1,0:T(8,128)(2,1)S(1)}, bf16[1,6144,128]{2,1,0:T(8,128)(2,1)}, u32[]{:S(2)}) copy-start(bf16[1,6144,128]{2,1,0:T(8,128)(2,1)} %param.11) | copy-start | bytes 4718596
  8.9 5.3 %copy-start.2 = (bf16[1,6144,128]{2,1,0:T(8,128)(2,1)S(1)}, bf16[1,6144,128]{2,1,0:T(8,128)(2,1)}, u32[]{:S(2)}) copy-start(bf16[1,6144,128]{2,1,0:T(8,128)(2,1)} %param.12) | copy-start | bytes 4718596
  8.9 6.3 %collective-permute-start.3 = (bf16[2,4,6272]{2,1,0:T(4,128)(2,1)S(1)}, bf16[2,4,6272]{2,1,0:T(4,128)(2,1)S(1)}, u32[]{:S(2)}, u32[]{:S(2)}) collective-permute-start(bf16[2,4,6272]{2,1,0:T(4,128)(2,1)S(1)} %shard_map.104.refs_0_), channel_id=1, source_target_pairs={{0,1},{1,0},{2,3},{3,2},{4,5},{5,4},{6,7},{7,6},{8,9},{9,8},{10,11... | collective-permute-start | bytes 301064 | tf_op jit(solution)/shard_map/ppermute | solution.py:199
  12.7 4.7 %collective-permute-start.4 = (bf16[2,4,6272]{2,1,0:T(4,128)(2,1)S(1)}, bf16[2,4,6272]{2,1,0:T(4,128)(2,1)S(1)}, u32[]{:S(2)}, u32[]{:S(2)}) collective-permute-start(bf16[2,4,6272]{2,1,0:T(4,128)(2,1)S(1)} %shard_map.105.refs_1_), channel_id=1, source_target_pairs={{0,1},{1,0},{2,3},{3,2},{4,5},{5,4},{6,7},{7,6},{8,9},{9,8},{10,11... | collective-permute-start | bytes 301064 | tf_op jit(solution)/shard_map/ppermute | solution.py:199
  14.2 5.3 %copy-start.3 = (bf16[1,128,6144]{2,1,0:T(8,128)(2,1)S(1)}, bf16[1,128,6144]{2,1,0:T(8,128)(2,1)}, u32[]{:S(2)}) copy-start(bf16[1,128,6144]{2,1,0:T(8,128)(2,1)} %param.13) | copy-start | bytes 4718596
  17.7 1.8 %collective-permute-start.6 = (bf16[32,6272]{1,0:T(8,128)(2,1)S(1)}, bf16[32,6272]{1,0:T(8,128)(2,1)S(1)}, u32[]{:S(2)}, u32[]{:S(2)}) collective-permute-start(bf16[32,6272]{1,0:T(8,128)(2,1)S(1)} %shard_map.108.near_ref), channel_id=1, source_target_pairs={{0,2},{2,0},{4,6},{6,4},{8,10},{10,8},{12,14},{14,12},{1,3},{3,1},... | collective-permute-start | bytes 1204232 | tf_op jit(solution)/shard_map/ppermute | solution.py:199
  21.5 1.8 %collective-permute-start.7 = (bf16[32,6144]{1,0:T(8,128)(2,1)S(1)}, bf16[32,6144]{1,0:T(8,128)(2,1)S(1)}, u32[]{:S(2)}, u32[]{:S(2)}) collective-permute-start(bf16[32,6144]{1,0:T(8,128)(2,1)S(1)} %get-tuple-element.24), channel_id=1, source_target_pairs={{0,2},{2,0},{4,6},{6,4},{8,10},{10,8},{12,14},{14,12},{1,3},{3,1},... | collective-permute-start | bytes 1179656 | tf_op jit(solution)/shard_map/ppermute | solution.py:199
  21.7 12.4 %collective-permute-start.13 = (bf16[64,3072]{1,0:T(8,128)(2,1)S(1)}, bf16[64,3072]{1,0:T(8,128)(2,1)S(1)}, u32[]{:S(2)}, u32[]{:S(2)}) collective-permute-start(bf16[64,3072]{1,0:T(8,128)(2,1)S(1)} %get-tuple-element.34), channel_id=1, source_target_pairs={{0,16},{16,0},{1,17},{17,1},{2,18},{18,2},{3,19},{19,3},{4,20},{20... | collective-permute-start | bytes 1179656 | tf_op jit(solution)/shard_map/ppermute | solution.py:199
  23.4 5.7 %collective-permute-start.8 = (bf16[8,6144]{1,0:T(8,128)(2,1)S(1)}, bf16[8,6144]{1,0:T(8,128)(2,1)S(1)}, u32[]{:S(2)}, u32[]{:S(2)}) collective-permute-start(bf16[8,6144]{1,0:T(8,128)(2,1)S(1)} %get-tuple-element.26), channel_id=1, source_target_pairs={{0,1},{1,0},{2,3},{3,2},{4,5},{5,4},{6,7},{7,6},{8,9},{9,8},{10,11... | collective-permute-start | bytes 294920 | tf_op jit(solution)/shard_map/ppermute | solution.py:199
  25.0 6.9 %collective-permute-start.9 = (bf16[8,6144]{1,0:T(8,128)(2,1)S(1)}, bf16[8,6144]{1,0:T(8,128)(2,1)S(1)}, u32[]{:S(2)}, u32[]{:S(2)}) collective-permute-start(bf16[8,6144]{1,0:T(8,128)(2,1)S(1)} %get-tuple-element.29), channel_id=1, source_target_pairs={{0,1},{1,0},{2,3},{3,2},{4,5},{5,4},{6,7},{7,6},{8,9},{9,8},{10,11... | collective-permute-start | bytes 294920 | tf_op jit(solution)/shard_map/ppermute | solution.py:199
  25.5 8.7 %collective-permute-start.14 = (bf16[192,128]{1,0:T(8,128)(2,1)S(1)}, bf16[192,128]{1,0:T(8,128)(2,1)S(1)}, u32[]{:S(2)}, u32[]{:S(2)}) collective-permute-start(bf16[192,128]{1,0:T(8,128)(2,1)S(1)} %get-tuple-element.33.factor_ref), channel_id=1, source_target_pairs={{0,16},{16,0},{1,17},{17,1},{2,18},{18,2},{3,19},{19,3},{4,20},{20... | collective-permute-start | bytes 147464 | tf_op jit(solution)/shard_map/ppermute | solution.py:199
  29.1 7.6 %collective-permute-start.12 = (bf16[4,6144]{1,0:T(4,128)(2,1)S(1)}, bf16[4,6144]{1,0:T(4,128)(2,1)S(1)}, u32[]{:S(2)}, u32[]{:S(2)}) collective-permute-start(bf16[4,6144]{1,0:T(4,128)(2,1)S(1)} %get-tuple-element.32), channel_id=1, source_target_pairs={{0,12},{2,14},{4,8},{6,10},{8,4},{10,6},{12,0},{14,2},{1,13},{3,15... | collective-permute-start | bytes 147464 | tf_op jit(solution)/shard_map/ppermute | solution.py:199
  31.9 4.9 %collective-permute-start.10 = (bf16[4,6144]{1,0:T(4,128)(2,1)S(1)}, bf16[4,6144]{1,0:T(4,128)(2,1)S(1)}, u32[]{:S(2)}, u32[]{:S(2)}) collective-permute-start(bf16[4,6144]{1,0:T(4,128)(2,1)S(1)} %get-tuple-element.30), channel_id=1, source_target_pairs={{0,4},{2,6},{4,0},{6,2},{8,12},{10,14},{12,8},{14,10},{1,5},{3,7},... | collective-permute-start | bytes 147464 | tf_op jit(solution)/shard_map/ppermute | solution.py:199
  32.4 5.0 %collective-permute-start.11 = (bf16[4,6144]{1,0:T(4,128)(2,1)S(1)}, bf16[4,6144]{1,0:T(4,128)(2,1)S(1)}, u32[]{:S(2)}, u32[]{:S(2)}) collective-permute-start(bf16[4,6144]{1,0:T(4,128)(2,1)S(1)} %get-tuple-element.31), channel_id=1, source_target_pairs={{0,8},{2,10},{4,12},{6,14},{8,0},{10,2},{12,4},{14,6},{1,9},{3,11}... | collective-permute-start | bytes 147464 | tf_op jit(solution)/shard_map/ppermute | solution.py:199

commit v5 on v4

--- a/solution.py
+++ b/solution.py
@@ -85,7 +85,8 @@
     share = send_refs[0].shape[1]
     me = lax.axis_index("rep")
     for i, send_ref in enumerate(send_refs):
-        send_ref[...] = x_ref[:, pl.ds(pl.multiple_of((me ^ (i + 1)) * share, LANES), share)]
+        columns = pl.ds(pl.multiple_of((me ^ (i + 1)) * share, LANES), share)
+        send_ref[...] = x_ref[: send_ref.shape[0], columns]
 
 
 def pre_kernel(x_ref, w_in_ref, w_lin_ref, *refs):
@@ -101,7 +102,7 @@
     both_ref[hidden_count:] = w_lin_ref[...].T
 
 
-def main_kernel(replicas, near_ref, away_ref, parts_ref, w_out_ref, both_ref, *refs):
+def main_kernel(replicas, near_ref, away_ref, parts_ref, w_out_ref, both_ref, x_ref, *refs):
     keep_ref, back_ref, factor_ref, *send_refs = refs
     half = near_ref.shape[0]
     tokens = 2 * half
@@ -141,7 +142,8 @@
     for j, send_ref in enumerate(send_refs):
         columns = pl.ds(pl.multiple_of((me ^ (j + 1)) * share, LANES), share)
         send_ref[:half] = near_ref[:, columns]
-        send_ref[half:] = away_ref[:, columns]
+        send_ref[half:tokens] = away_ref[:, columns]
+        send_ref[tokens:] = x_ref[slots - (send_ref.shape[0] - tokens) :, columns]
 
 
 def sum_kernel(arrived, cuts, *refs):
@@ -170,6 +172,7 @@
     x_others, t_others, f_others = (refs[i * others : (i + 1) * others] for i in range(3))
     outs, held, sem = refs[3 * others : 3 * others + 3], refs[-4:-1], refs[-1]
     share = outs[0].shape[0]
+    count = 2 * near_ref.shape[0]
     start = lax.axis_index("rep") * share
     factors = (factor_ref, *f_others)
     hidden = jnp.concatenate([f[2 * slots :] for f in factors], axis=0)
@@ -180,11 +183,11 @@
     for begin in range(0, share, step):
         cols = slice(begin, begin + step)
         columns = pl.ds(pl.multiple_of(start + begin, LANES), step)
-        inputs = jnp.concatenate([x_ref[:, columns], *(x[:, cols] for x in x_others)], axis=0)
+        inputs = jnp.concatenate([x_ref[:, columns], *(x[:, cols] for pair in zip(x_others, (t.at[count:] for t in t_others)) for x in pair)], axis=0)
         held[0][cols, :] = tn(inputs, d_gate)
         held[1][cols, :] = tn(inputs, d_linear)
         tokens = jnp.concatenate(
-            [near_ref[:, columns], away_ref[:, columns], *(t[:, cols] for t in t_others)], axis=0
+            [near_ref[:, columns], away_ref[:, columns], *(t[:count, cols] for t in t_others)], axis=0
         )
         held[2][:, cols] = tn(hidden, tokens)
         for i, at in enumerate(((cols, slice(None)), (cols, slice(None)), (slice(None), cols))):
@@ -219,8 +222,10 @@
         flops=100 * weight_flops,
     )
     across = range(1, column_groups)
+    early = slots // 64 * 56
     steps = range(0, groups, 2)
-    column = [own] + [swap(own, "exp", k) for k in steps[:0:-1]][::-1]
+    taken = [0, groups - 2, *range(2, groups - 2, 2)]
+    column = [own] + [swap(own, "exp", k) for k in taken[1:]]
     half = len(column) // 2
     stacks = [
         local_call(stack_kernel, shape((half, *own.shape), BF16), tuple(part), flops=50 * weight_flops)
@@ -230,9 +235,9 @@
     for j in across:
         pieces += [swap(stack, "ffn", j) for stack in stacks]
     steps = [0, groups - 2, *range(2, groups - 2, 2)]
-    order = [(2 * j + k // 2 // half, k // 2 % half) for j in range(column_groups) for k in steps]
+    order = [(2 * j + taken.index(k) // half, taken.index(k) % half) for j in range(column_groups) for k in steps]
     x_sends = local_call(
-        share_kernel, [shape((slots, share), BF16)] * (replicas - 1), (inputs, own)
+        share_kernel, [shape((early, share), BF16)] * (replicas - 1), (inputs, own)
     )
     x_others = [swap(x, "rep", i + 1) for i, x in enumerate(x_sends)]
     split, both = local_call(
@@ -252,8 +257,8 @@
         functools.partial(main_kernel, replicas),
         [shape((tokens // 2, width), F32), shape((tokens // 2, width), BF16)]
         + [shape((2 * slots + tokens, hidden_count), BF16)]
-        + [shape((tokens, share), BF16)] * (replicas - 1),
-        (*parts, split, down_w, both),
+        + [shape((tokens + slots - early, share), BF16)] * (replicas - 1),
+        (*parts, split, down_w, both, inputs),
         flops=3 * weight_flops,
     )
     back = swap(send, "exp", 1)

time: 38.2 us -> 37.7 us (0.987)
  waiting for transfers between devices: 9.52 us -> 7.82 us
  starting transfers between devices: 20.3 us -> 21.5 us
    ppermute x15, waiting for transfers between devices: 9.52 us -> 7.82 us  [swap(): return lax.ppermute(values, axis, [(i, i ^ distance) for i in range(size)])]
    ppermute x15, starting transfers between devices: 20.3 us -> 21.5 us  [swap(): return lax.ppermute(values, axis, [(i, i ^ distance) for i in range(size)])]
  transfers between devices with their start and end apart: 15 -> 15, of which waited for: 9 -> 8; matrix products, arithmetic and copies ran while one was open for 0% -> 0% of each run, Pallas kernels for 10% -> 10%
where the time goes in v5:
time: 37.7 us; the launch traced here: 37.5 us
  starting transfers between devices  21.5 us (57%)
  waiting for transfers between devices  7.82 us (21%)
  Pallas kernels  6.58 us (17%)
  local copies, waits for them, and re-layouts  0.82 us (2%)
  between operations  0.78 us (2%)
    ppermute x15, starting transfers between devices, swap(): return lax.ppermute(values, axis, [(i, i ^ distance) for i in range(size)])  21.5 us
    ppermute x15, waiting for transfers between devices, swap(): return lax.ppermute(values, axis, [(i, i ^ distance) for i in range(size)])  7.82 us
    pallas_call x13, Pallas kernels, local_call(): pl.pallas_call(kernel, out_shape=out_shape, in_specs=[whole] * len(args),...  6.58 us
    unnamed x14, local copies, waits for them, and re-layouts  0.82 us
  transfers between devices with their start and end apart: 15, of which 8 were waited for; matrix products, arithmetic and copies ran while one was open for 0% of the time, Pallas kernels for 10%

profile of v5, /device:TPU:0, one launch (start us, length us, event | category | flops | bytes accessed | tf_op | source)
XLA Modules:
  0.0 37.5 jit_solution(12121598636963494203)
XLA Ops:
  0.7 0.6 %copy-done.6 = f32[4,4]{1,0:T(4,128)S(1)} copy-done((f32[4,4]{1,0:T(4,128)S(1)}, f32[4,4]{1,0:T(4,128)}, u32[]{:S(2)}) %copy-start.6) | copy-done | bytes 88
  1.3 0.0 copy-done.5
  1.3 0.1 copy-done.4
  1.5 0.1 shard_map.103.refs_0_.after_ref
  1.6 5.1 %collective-permute-start = (bf16[4,6272]{1,0:T(4,128)(2,1)S(1)}, bf16[4,6272]{1,0:T(4,128)(2,1)S(1)}, u32[]{:S(2)}, u32[]{:S(2)}) collective-permute-start(bf16[4,6272]{1,0:T(4,128)(2,1)S(1)} %shard_map.103.refs_0_.after_ref), channel_id=1, source_target_pairs={{0,12},{2,14},{4,8},{6,10},{8,4},{10,6},{12,0},{14,2},{1,13},{3,15... | collective-permute-start | bytes 150536 | tf_op jit(solution)/shard_map/ppermute | solution.py:202
  6.7 0.6 %collective-permute-start.1 = (bf16[4,6272]{1,0:T(4,128)(2,1)S(1)}, bf16[4,6272]{1,0:T(4,128)(2,1)S(1)}, u32[]{:S(2)}, u32[]{:S(2)}) collective-permute-start(bf16[4,6272]{1,0:T(4,128)(2,1)S(1)} %shard_map.103.refs_0_.after_ref), channel_id=1, source_target_pairs={{0,4},{2,6},{4,0},{6,2},{8,12},{10,14},{12,8},{14,10},{1,5},{3,7},... | collective-permute-start | bytes 150536 | tf_op jit(solution)/shard_map/ppermute | solution.py:202
  7.3 1.7 %collective-permute-start.5 = (bf16[56,3072]{1,0:T(8,128)(2,1)S(1)}, bf16[56,3072]{1,0:T(8,128)(2,1)S(1)}, u32[]{:S(2)}, u32[]{:S(2)}) collective-permute-start(bf16[56,3072]{1,0:T(8,128)(2,1)S(1)} %shard_map.106), channel_id=1, source_target_pairs={{0,16},{16,0},{1,17},{17,1},{2,18},{18,2},{3,19},{19,3},{4,20},{20... | collective-permute-start | bytes 1032200 | tf_op jit(solution)/shard_map/ppermute | solution.py:202
  9.1 1.7 %collective-permute-start.3 = (bf16[2,4,6272]{2,1,0:T(4,128)(2,1)S(1)}, bf16[2,4,6272]{2,1,0:T(4,128)(2,1)S(1)}, u32[]{:S(2)}, u32[]{:S(2)}) collective-permute-start(bf16[2,4,6272]{2,1,0:T(4,128)(2,1)S(1)} %shard_map.104.refs_0_), channel_id=1, source_target_pairs={{0,1},{1,0},{2,3},{3,2},{4,5},{5,4},{6,7},{7,6},{8,9},{9,8},{10,11... | collective-permute-start | bytes 301064 | tf_op jit(solution)/shard_map/ppermute | solution.py:202
  10.8 0.8 %collective-permute-done.2.refs_1_ = bf16[4,6272]{1,0:T(4,128)(2,1)S(1)} collective-permute-done((bf16[4,6272]{1,0:T(4,128)(2,1)S(1)}, bf16[4,6272]{1,0:T(4,128)(2,1)S(1)}, u32[]{:S(2)}, u32[]{:S(2)}) %collective-permute-start.2) | collective-permute-done | bytes 50208 | tf_op jit(solution)/shard_map/ppermute | solution.py:202
  11.7 1.6 %collective-permute-start.4 = (bf16[2,4,6272]{2,1,0:T(4,128)(2,1)S(1)}, bf16[2,4,6272]{2,1,0:T(4,128)(2,1)S(1)}, u32[]{:S(2)}, u32[]{:S(2)}) collective-permute-start(bf16[2,4,6272]{2,1,0:T(4,128)(2,1)S(1)} %shard_map.105.refs_1_), channel_id=1, source_target_pairs={{0,1},{1,0},{2,3},{3,2},{4,5},{5,4},{6,7},{7,6},{8,9},{9,8},{10,11... | collective-permute-start | bytes 301064 | tf_op jit(solution)/shard_map/ppermute | solution.py:202
  13.3 1.0 %shard_map.107 = (bf16[64,768]{1,0:T(8,128)(2,1)S(1)}, bf16[256,6144]{1,0:T(8,128)(2,1)S(1)}) custom-call(bf16[64,6144]{1,0:T(8,128)(2,1)S(1)} %bitcast.8, bf16[6144,128]{1,0:T(8,128)(2,1)S(1)} %bitcast.11, bf16[6144,128]{1,0:T(8,128)(2,1)S(1)} %bitcast.12, bf16[2,4,6272]{2,1,0:T(4,128)(2,1)S(1)} %shard_map.104.refs_0_), custom_call_target="tpu_custom_call" | custom-call | flops 201326592 | tf_op jit(solution)/shard_map/pallas_call | solution.py:27
  14.3 0.1 collective-permute-done.3.refs_2_
  14.4 2.0 %collective-permute-done.4.refs_3_ = bf16[2,4,6272]{2,1,0:T(4,128)(2,1)S(1)} collective-permute-done((bf16[2,4,6272]{2,1,0:T(4,128)(2,1)S(1)}, bf16[2,4,6272]{2,1,0:T(4,128)(2,1)S(1)}, u32[]{:S(2)}, u32[]{:S(2)}) %collective-permute-start.4) | collective-permute-done | bytes 100384 | tf_op jit(solution)/shard_map/ppermute | solution.py:202
  16.4 0.3 collective-permute-done.5.refs_4_.refs_0_
  16.7 0.1 shard_map.108.near_ref
  16.8 0.1 collective-permute-start.6
  16.8 1.7 %collective-permute-done.6.away_ref = bf16[32,6272]{1,0:T(8,128)(2,1)S(1)} collective-permute-done((bf16[32,6272]{1,0:T(8,128)(2,1)S(1)}, bf16[32,6272]{1,0:T(8,128)(2,1)S(1)}, u32[]{:S(2)}, u32[]{:S(2)}) %collective-permute-start.6) | collective-permute-done | bytes 401440 | tf_op jit(solution)/shard_map/ppermute | solution.py:202
  18.6 2.0 %shard_map.109 = (f32[32,6144]{1,0:T(8,128)S(1)}, bf16[32,6144]{1,0:T(8,128)(2,1)S(1)}, bf16[192,128]{1,0:T(8,128)(2,1)S(1)}, bf16[72,3072]{1,0:T(8,128)(2,1)S(1)}) custom-call(bf16[32,6272]{1,0:T(8,128)(2,1)S(1)} %shard_map.108.near_ref, bf16[32,6272]{1,0:T(8,128)(2,1)S(1)} %collective-permute-done.6.away_ref, ...), custom_call_target="tpu_custom_call" | custom-call | flops 301989888 | tf_op jit(solution)/shard_map/pallas_call | solution.py:27
  20.5 0.2 collective-permute-start.7
  20.7 1.5 %collective-permute-start.13 = (bf16[72,3072]{1,0:T(8,128)(2,1)S(1)}, bf16[72,3072]{1,0:T(8,128)(2,1)S(1)}, u32[]{:S(2)}, u32[]{:S(2)}) collective-permute-start(bf16[72,3072]{1,0:T(8,128)(2,1)S(1)} %get-tuple-element.34), channel_id=1, source_target_pairs={{0,16},{16,0},{1,17},{17,1},{2,18},{18,2},{3,19},{19,3},{4,20},{20... | collective-permute-start | bytes 1327112 | tf_op jit(solution)/shard_map/ppermute | solution.py:202
  22.3 0.1 collective-permute-done.7.refs_1_
  22.3 0.1 shard_map.110
  22.4 1.6 %collective-permute-start.8 = (bf16[8,6144]{1,0:T(8,128)(2,1)S(1)}, bf16[8,6144]{1,0:T(8,128)(2,1)S(1)}, u32[]{:S(2)}, u32[]{:S(2)}) collective-permute-start(bf16[8,6144]{1,0:T(8,128)(2,1)S(1)} %get-tuple-element.26), channel_id=1, source_target_pairs={{0,1},{1,0},{2,3},{3,2},{4,5},{5,4},{6,7},{7,6},{8,9},{9,8},{10,11... | collective-permute-start | bytes 294920 | tf_op jit(solution)/shard_map/ppermute | solution.py:202
  24.0 0.5 %collective-permute-start.9 = (bf16[8,6144]{1,0:T(8,128)(2,1)S(1)}, bf16[8,6144]{1,0:T(8,128)(2,1)S(1)}, u32[]{:S(2)}, u32[]{:S(2)}) collective-permute-start(bf16[8,6144]{1,0:T(8,128)(2,1)S(1)} %get-tuple-element.29), channel_id=1, source_target_pairs={{0,1},{1,0},{2,3},{3,2},{4,5},{5,4},{6,7},{7,6},{8,9},{9,8},{10,11... | collective-permute-start | bytes 294920 | tf_op jit(solution)/shard_map/ppermute | solution.py:202
  24.5 1.5 %collective-permute-start.14 = (bf16[192,128]{1,0:T(8,128)(2,1)S(1)}, bf16[192,128]{1,0:T(8,128)(2,1)S(1)}, u32[]{:S(2)}, u32[]{:S(2)}) collective-permute-start(bf16[192,128]{1,0:T(8,128)(2,1)S(1)} %get-tuple-element.33.factor_ref), channel_id=1, source_target_pairs={{0,16},{16,0},{1,17},{17,1},{2,18},{18,2},{3,19},{19,3},{4,20},{20... | collective-permute-start | bytes 147464 | tf_op jit(solution)/shard_map/ppermute | solution.py:202
  26.0 2.1 %collective-permute-done.8.refs_1_ = bf16[8,6144]{1,0:T(8,128)(2,1)S(1)} collective-permute-done((bf16[8,6144]{1,0:T(8,128)(2,1)S(1)}, bf16[8,6144]{1,0:T(8,128)(2,1)S(1)}, u32[]{:S(2)}, u32[]{:S(2)}) %collective-permute-start.8) | collective-permute-done | bytes 98336 | tf_op jit(solution)/shard_map/ppermute | solution.py:202
  28.1 3.5 %collective-permute-start.12 = (bf16[4,6144]{1,0:T(4,128)(2,1)S(1)}, bf16[4,6144]{1,0:T(4,128)(2,1)S(1)}, u32[]{:S(2)}, u32[]{:S(2)}) collective-permute-start(bf16[4,6144]{1,0:T(4,128)(2,1)S(1)} %get-tuple-element.32), channel_id=1, source_target_pairs={{0,12},{2,14},{4,8},{6,10},{8,4},{10,6},{12,0},{14,2},{1,13},{3,15... | collective-permute-start | bytes 147464 | tf_op jit(solution)/shard_map/ppermute | solution.py:202
  31.7 0.1 collective-permute-start.10
  31.8 1.8 %collective-permute-start.11 = (bf16[4,6144]{1,0:T(4,128)(2,1)S(1)}, bf16[4,6144]{1,0:T(4,128)(2,1)S(1)}, u32[]{:S(2)}, u32[]{:S(2)}) collective-permute-start(bf16[4,6144]{1,0:T(4,128)(2,1)S(1)} %get-tuple-element.31), channel_id=1, source_target_pairs={{0,8},{2,10},{4,12},{6,14},{8,0},{10,2},{12,4},{14,6},{1,9},{3,11}... | collective-permute-start | bytes 147464 | tf_op jit(solution)/shard_map/ppermute | solution.py:202
  33.5 0.7 %collective-permute-done.14.refs_2_ = bf16[192,128]{1,0:T(8,128)(2,1)S(1)} collective-permute-done((bf16[192,128]{1,0:T(8,128)(2,1)S(1)}, bf16[192,128]{1,0:T(8,128)(2,1)S(1)}, u32[]{:S(2)}, u32[]{:S(2)}) %collective-permute-start.14) | collective-permute-done | bytes 49184 | tf_op jit(solution)/shard_map/ppermute | solution.py:202
  34.2 2.6 %shard_map.114 = (f32[3072,128]{1,0:T(8,128)}, f32[3072,128]{1,0:T(8,128)}, f32[128,3072]{1,0:T(8,128)}) custom-call(bf16[64,6144]{1,0:T(8,128)(2,1)S(1)} %bitcast.10, bf16[32,6272]{1,0:T(8,128)(2,1)S(1)} %shard_map.108.near_ref, bf16[32,6272]{1,0:T(8,128)(2,1)S(1)} %collective-permute-done.6.away_ref, bf16[192,128]{1,0:T(8,128)(2,1)S(1)} %get-tuple-element.33.factor_ref, ...), custom_call_target="tpu_custom_call" | custom-call | flops 301989888 | tf_op jit(solution)/shard_map/pallas_call | solution.py:27
  36.9 0.7 %shard_map.113 = bf16[4,6144]{1,0:T(4,128)(2,1)} custom-call(f32[4,6144]{1,0:T(4,128)S(1)} %get-tuple-element.27.refs_0_, bf16[4,6144]{1,0:T(4,128)(2,1)S(1)} %collective-permute-done.10.refs_1_, bf16[4,6144]{1,0:T(4,128)(2,1)S(1)} %collective-permute-done.11.refs_2_, bf16[4,6144]{1,0:T(4,128)(2,1)S(1)} %collective-permute-done.12.refs_3_), custom_call_target="tpu_custom_call" | custom-call | tf_op jit(solution)/shard_map/pallas_call | solution.py:27
  (25 shorter events, 0.1 us)
Async XLA Ops:
  0.6 0.7 %copy-start.6 = (f32[4,4]{1,0:T(4,128)S(1)}, f32[4,4]{1,0:T(4,128)}, u32[]{:S(2)}) copy-start(f32[4,4]{1,0:T(4,128)} %gates_ref.1) | copy-start | bytes 196
  0.6 0.7 %copy-start.5 = (s32[4,4]{1,0:T(4,128)S(1)}, s32[4,4]{1,0:T(4,128)}, u32[]{:S(2)}) copy-start(s32[4,4]{1,0:T(4,128)} %experts_ref.1) | copy-start | bytes 196
  0.7 0.8 %copy-start.4 = (bf16[4,6144]{1,0:T(4,128)(2,1)S(1)}, bf16[4,6144]{1,0:T(4,128)(2,1)}, u32[]{:S(2)}) copy-start(bf16[4,6144]{1,0:T(4,128)(2,1)} %grad_ref.1) | copy-start | bytes 147460
  1.5 5.9 %copy-start = (bf16[1,1,64,6144]{3,2,1,0:T(8,128)(2,1)S(1)}, bf16[1,1,64,6144]{3,2,1,0:T(8,128)(2,1)}, u32[]{:S(2)}) copy-start(bf16[1,1,64,6144]{3,2,1,0:T(8,128)(2,1)} %param.10) | copy-start | bytes 2359300
  1.6 7.5 %collective-permute-start = (bf16[4,6272]{1,0:T(4,128)(2,1)S(1)}, bf16[4,6272]{1,0:T(4,128)(2,1)S(1)}, u32[]{:S(2)}, u32[]{:S(2)}) collective-permute-start(bf16[4,6272]{1,0:T(4,128)(2,1)S(1)} %shard_map.103.refs_0_.after_ref), channel_id=1, source_target_pairs={{0,12},{2,14},{4,8},{6,10},{8,4},{10,6},{12,0},{14,2},{1,13},{3,15... | collective-permute-start | bytes 150536 | tf_op jit(solution)/shard_map/ppermute | solution.py:202
  6.7 5.0 %collective-permute-start.2 = (bf16[4,6272]{1,0:T(4,128)(2,1)S(1)}, bf16[4,6272]{1,0:T(4,128)(2,1)S(1)}, u32[]{:S(2)}, u32[]{:S(2)}) collective-permute-start(bf16[4,6272]{1,0:T(4,128)(2,1)S(1)} %shard_map.103.refs_0_.after_ref), channel_id=1, source_target_pairs={{0,8},{2,10},{4,12},{6,14},{8,0},{10,2},{12,4},{14,6},{1,9},{3,11}... | collective-permute-start | bytes 150536 | tf_op jit(solution)/shard_map/ppermute | solution.py:202
  6.7 5.0 %collective-permute-start.1 = (bf16[4,6272]{1,0:T(4,128)(2,1)S(1)}, bf16[4,6272]{1,0:T(4,128)(2,1)S(1)}, u32[]{:S(2)}, u32[]{:S(2)}) collective-permute-start(bf16[4,6272]{1,0:T(4,128)(2,1)S(1)} %shard_map.103.refs_0_.after_ref), channel_id=1, source_target_pairs={{0,4},{2,6},{4,0},{6,2},{8,12},{10,14},{12,8},{14,10},{1,5},{3,7},... | collective-permute-start | bytes 150536 | tf_op jit(solution)/shard_map/ppermute | solution.py:202
  7.3 9.3 %collective-permute-start.5 = (bf16[56,3072]{1,0:T(8,128)(2,1)S(1)}, bf16[56,3072]{1,0:T(8,128)(2,1)S(1)}, u32[]{:S(2)}, u32[]{:S(2)}) collective-permute-start(bf16[56,3072]{1,0:T(8,128)(2,1)S(1)} %shard_map.106), channel_id=1, source_target_pairs={{0,16},{16,0},{1,17},{17,1},{2,18},{18,2},{3,19},{19,3},{4,20},{20... | collective-permute-start | bytes 1032200 | tf_op jit(solution)/shard_map/ppermute | solution.py:202
  9.1 4.2 %copy-start.1 = (bf16[1,6144,128]{2,1,0:T(8,128)(2,1)S(1)}, bf16[1,6144,128]{2,1,0:T(8,128)(2,1)}, u32[]{:S(2)}) copy-start(bf16[1,6144,128]{2,1,0:T(8,128)(2,1)} %param.11) | copy-start | bytes 4718596
  9.1 4.1 %copy-start.2 = (bf16[1,6144,128]{2,1,0:T(8,128)(2,1)S(1)}, bf16[1,6144,128]{2,1,0:T(8,128)(2,1)}, u32[]{:S(2)}) copy-start(bf16[1,6144,128]{2,1,0:T(8,128)(2,1)} %param.12) | copy-start | bytes 4718596
  9.1 5.3 %collective-permute-start.3 = (bf16[2,4,6272]{2,1,0:T(4,128)(2,1)S(1)}, bf16[2,4,6272]{2,1,0:T(4,128)(2,1)S(1)}, u32[]{:S(2)}, u32[]{:S(2)}) collective-permute-start(bf16[2,4,6272]{2,1,0:T(4,128)(2,1)S(1)} %shard_map.104.refs_0_), channel_id=1, source_target_pairs={{0,1},{1,0},{2,3},{3,2},{4,5},{5,4},{6,7},{7,6},{8,9},{9,8},{10,11... | collective-permute-start | bytes 301064 | tf_op jit(solution)/shard_map/ppermute | solution.py:202
  11.7 4.7 %collective-permute-start.4 = (bf16[2,4,6272]{2,1,0:T(4,128)(2,1)S(1)}, bf16[2,4,6272]{2,1,0:T(4,128)(2,1)S(1)}, u32[]{:S(2)}, u32[]{:S(2)}) collective-permute-start(bf16[2,4,6272]{2,1,0:T(4,128)(2,1)S(1)} %shard_map.105.refs_1_), channel_id=1, source_target_pairs={{0,1},{1,0},{2,3},{3,2},{4,5},{5,4},{6,7},{7,6},{8,9},{9,8},{10,11... | collective-permute-start | bytes 301064 | tf_op jit(solution)/shard_map/ppermute | solution.py:202
  13.2 5.3 %copy-start.3 = (bf16[1,128,6144]{2,1,0:T(8,128)(2,1)S(1)}, bf16[1,128,6144]{2,1,0:T(8,128)(2,1)}, u32[]{:S(2)}) copy-start(bf16[1,128,6144]{2,1,0:T(8,128)(2,1)} %param.13) | copy-start | bytes 4718596
  16.8 1.8 %collective-permute-start.6 = (bf16[32,6272]{1,0:T(8,128)(2,1)S(1)}, bf16[32,6272]{1,0:T(8,128)(2,1)S(1)}, u32[]{:S(2)}, u32[]{:S(2)}) collective-permute-start(bf16[32,6272]{1,0:T(8,128)(2,1)S(1)} %shard_map.108.near_ref), channel_id=1, source_target_pairs={{0,2},{2,0},{4,6},{6,4},{8,10},{10,8},{12,14},{14,12},{1,3},{3,1},... | collective-permute-start | bytes 1204232 | tf_op jit(solution)/shard_map/ppermute | solution.py:202
  20.5 1.8 %collective-permute-start.7 = (bf16[32,6144]{1,0:T(8,128)(2,1)S(1)}, bf16[32,6144]{1,0:T(8,128)(2,1)S(1)}, u32[]{:S(2)}, u32[]{:S(2)}) collective-permute-start(bf16[32,6144]{1,0:T(8,128)(2,1)S(1)} %get-tuple-element.24), channel_id=1, source_target_pairs={{0,2},{2,0},{4,6},{6,4},{8,10},{10,8},{12,14},{14,12},{1,3},{3,1},... | collective-permute-start | bytes 1179656 | tf_op jit(solution)/shard_map/ppermute | solution.py:202
  20.7 13.5 %collective-permute-start.13 = (bf16[72,3072]{1,0:T(8,128)(2,1)S(1)}, bf16[72,3072]{1,0:T(8,128)(2,1)S(1)}, u32[]{:S(2)}, u32[]{:S(2)}) collective-permute-start(bf16[72,3072]{1,0:T(8,128)(2,1)S(1)} %get-tuple-element.34), channel_id=1, source_target_pairs={{0,16},{16,0},{1,17},{17,1},{2,18},{18,2},{3,19},{19,3},{4,20},{20... | collective-permute-start | bytes 1327112 | tf_op jit(solution)/shard_map/ppermute | solution.py:202
  22.4 5.7 %collective-permute-start.8 = (bf16[8,6144]{1,0:T(8,128)(2,1)S(1)}, bf16[8,6144]{1,0:T(8,128)(2,1)S(1)}, u32[]{:S(2)}, u32[]{:S(2)}) collective-permute-start(bf16[8,6144]{1,0:T(8,128)(2,1)S(1)} %get-tuple-element.26), channel_id=1, source_target_pairs={{0,1},{1,0},{2,3},{3,2},{4,5},{5,4},{6,7},{7,6},{8,9},{9,8},{10,11... | collective-permute-start | bytes 294920 | tf_op jit(solution)/shard_map/ppermute | solution.py:202
  24.0 7.7 %collective-permute-start.9 = (bf16[8,6144]{1,0:T(8,128)(2,1)S(1)}, bf16[8,6144]{1,0:T(8,128)(2,1)S(1)}, u32[]{:S(2)}, u32[]{:S(2)}) collective-permute-start(bf16[8,6144]{1,0:T(8,128)(2,1)S(1)} %get-tuple-element.29), channel_id=1, source_target_pairs={{0,1},{1,0},{2,3},{3,2},{4,5},{5,4},{6,7},{7,6},{8,9},{9,8},{10,11... | collective-permute-start | bytes 294920 | tf_op jit(solution)/shard_map/ppermute | solution.py:202
  24.5 9.8 %collective-permute-start.14 = (bf16[192,128]{1,0:T(8,128)(2,1)S(1)}, bf16[192,128]{1,0:T(8,128)(2,1)S(1)}, u32[]{:S(2)}, u32[]{:S(2)}) collective-permute-start(bf16[192,128]{1,0:T(8,128)(2,1)S(1)} %get-tuple-element.33.factor_ref), channel_id=1, source_target_pairs={{0,16},{16,0},{1,17},{17,1},{2,18},{18,2},{3,19},{19,3},{4,20},{20... | collective-permute-start | bytes 147464 | tf_op jit(solution)/shard_map/ppermute | solution.py:202
  28.1 8.7 %collective-permute-start.12 = (bf16[4,6144]{1,0:T(4,128)(2,1)S(1)}, bf16[4,6144]{1,0:T(4,128)(2,1)S(1)}, u32[]{:S(2)}, u32[]{:S(2)}) collective-permute-start(bf16[4,6144]{1,0:T(4,128)(2,1)S(1)} %get-tuple-element.32), channel_id=1, source_target_pairs={{0,12},{2,14},{4,8},{6,10},{8,4},{10,6},{12,0},{14,2},{1,13},{3,15... | collective-permute-start | bytes 147464 | tf_op jit(solution)/shard_map/ppermute | solution.py:202
  31.7 5.2 %collective-permute-start.10 = (bf16[4,6144]{1,0:T(4,128)(2,1)S(1)}, bf16[4,6144]{1,0:T(4,128)(2,1)S(1)}, u32[]{:S(2)}, u32[]{:S(2)}) collective-permute-start(bf16[4,6144]{1,0:T(4,128)(2,1)S(1)} %get-tuple-element.30), channel_id=1, source_target_pairs={{0,4},{2,6},{4,0},{6,2},{8,12},{10,14},{12,8},{14,10},{1,5},{3,7},... | collective-permute-start | bytes 147464 | tf_op jit(solution)/shard_map/ppermute | solution.py:202
  31.8 5.1 %collective-permute-start.11 = (bf16[4,6144]{1,0:T(4,128)(2,1)S(1)}, bf16[4,6144]{1,0:T(4,128)(2,1)S(1)}, u32[]{:S(2)}, u32[]{:S(2)}) collective-permute-start(bf16[4,6144]{1,0:T(4,128)(2,1)S(1)} %get-tuple-element.31), channel_id=1, source_target_pairs={{0,8},{2,10},{4,12},{6,14},{8,0},{10,2},{12,4},{14,6},{1,9},{3,11}... | collective-permute-start | bytes 147464 | tf_op jit(solution)/shard_map/ppermute | solution.py:202
